TPU v7x, 32 devices: a whole 2x2x4 slice. The times are simulated.
32 devices in a mesh: det: 4 (over y, core), patch: 8 (over z, x).
Axes of the slice: x: 2, y: 2, z: 4, core: 2. Of those that a mesh axis runs over, the one named last changes fastest.
Arguments:
- exposure: bfloat16 [8192, 4096], P(('det', 'patch')), may hold values from -8 to 8
- block_dest: int32 [1024], P(('det', 'patch')), may hold values from 0 to 1023, as said below
- band_offset: int32 [1024], P(('det', 'patch')), may hold values from -8 to 8
- col_shift: float32 [1024], P(('det', 'patch')), may hold values from 0.05 to 0.95
- block_weight: float32 [1024], P(('det', 'patch')), may hold values from 0.5 to 4
- basis_width: float32 [3], replicated, may hold values from 1 to 5
- kernel_fit: float32 [32, 3, 6], P(('det', 'patch')), may hold values from -3 to 3
- fit_owner: int32 [1], replicated, may hold values from 0 to 31
Outputs:
- matched: bfloat16 [8192, 4096], P(('det', 'patch'))
- coverage: float32 [1024], P(('det', 'patch'))
Inputs may be any that keep to these rules, and one draw needn't show every extreme that they name: `block_dest`: block b of device d (b in d * 32 .. d * 32 + 31) lands in a slot of a device of d's det group (slots d' 32 .. d' 32 + 31 belong to device d'); no device sends more than 5 of its blocks to one device, and every device sends exactly 5 to some device.
All inputs are finite; a program needn't handle non-finite values.
Results may differ from a plain program's by a relative error of at most 0.013.
Values may be sent and summed in bfloat16 or wider, within the bound.
No kernel may reach another device: no remote copies, remote signals or barrier semaphores. Data moves between devices by JAX's collectives and lax.ppermute only.
A program may use at most 448 MiB of HBM per device.

v0:
```python
import jax
import jax.numpy as jnp
from jax import lax
from jax.sharding import PartitionSpec as P

TAPS = 31
BASES = 3
TILE = 512


def spread(value, axis, root):
    mine = lax.axis_index(axis) == root
    return lax.psum(jnp.where(mine, value, jnp.zeros_like(value)), axis)


def with_halo(block, sides, width):
    for axis, dim in sides:
        count = lax.axis_size(axis)
        forward = [(i, i + 1) for i in range(count - 1)]
        backward = [(target, source) for source, target in forward]
        low = lax.ppermute(
            lax.slice_in_dim(block, block.shape[dim] - width, None, axis=dim), axis, forward
        )
        high = lax.ppermute(lax.slice_in_dim(block, 0, width, axis=dim), axis, backward)
        block = jnp.concatenate([low, block, high], axis=dim)
    return block


def lanczos(position):
    return jnp.sinc(position) * jnp.sinc(position / 3.0)


def resample_blocks(source_rows, offsets, shifts, weights):
    col_count = source_rows.shape[2]
    column_margin = 128
    padded = jnp.pad(source_rows, ((0, 0), (0, 0), (column_margin, column_margin)))
    summed = jnp.zeros(source_rows.shape, jnp.float32)
    for shift_value in range(-10, 12):
        coeffs = jnp.zeros(shifts.shape, jnp.float32)
        for offset_tap in range(-2, 4):
            coeffs = coeffs + jnp.where(
                offsets + offset_tap == shift_value, lanczos(offset_tap - shifts), 0.0
            )
        start_col = column_margin + shift_value
        picked = padded[:, :, start_col : start_col + col_count]
        summed = summed + coeffs[:, None, None] * picked.astype(jnp.float32)
    return summed * weights[:, None, None]


def gaussian_taps(basis_width):
    half_span = (TAPS - 1) // 2
    positions = jnp.arange(TAPS).astype(jnp.float32) - half_span
    profile = jnp.exp(-positions[None, :] ** 2 / (2.0 * basis_width[:, None] ** 2))
    return profile / jnp.sum(profile, axis=1, keepdims=True)


def poly_field(coeff_row, row_pos, col_pos):
    yy_pos = row_pos[:, None]
    xx_pos = col_pos[None, :]
    return (
        coeff_row[0]
        + coeff_row[1] * xx_pos
        + coeff_row[2] * yy_pos
        + coeff_row[3] * xx_pos * xx_pos
        + coeff_row[4] * xx_pos * yy_pos
        + coeff_row[5] * yy_pos * yy_pos
    )


def band_table(taps_row, tile_step):
    half_span = (TAPS - 1) // 2
    differ = jnp.arange(TILE)[:, None] - jnp.arange(TILE)[None, :] + tile_step * TILE + half_span
    table = jnp.zeros((TILE, TILE), jnp.float32)
    for tap_index in range(TAPS):
        table = table + jnp.where(differ == tap_index, taps_row[tap_index].astype(jnp.float32), 0.0)
    return table.astype(jnp.bfloat16)


def column_convolve(image_rows, taps_row):
    row_count, col_count = image_rows.shape
    tile_count = col_count // TILE
    tiles = image_rows.reshape(row_count, tile_count, TILE)
    zero_tile = jnp.zeros((row_count, 1, TILE), image_rows.dtype)
    before = jnp.concatenate([zero_tile, tiles[:, :-1]], axis=1)
    after = jnp.concatenate([tiles[:, 1:], zero_tile], axis=1)
    smoothed = jnp.einsum(
        "rna,ab->rnb", tiles, band_table(taps_row, 0), preferred_element_type=jnp.float32
    )
    smoothed = smoothed + jnp.einsum(
        "rna,ab->rnb", before, band_table(taps_row, -1), preferred_element_type=jnp.float32
    )
    smoothed = smoothed + jnp.einsum(
        "rna,ab->rnb", after, band_table(taps_row, 1), preferred_element_type=jnp.float32
    )
    return smoothed.reshape(row_count, col_count)


def row_convolve(rimmed, taps_row, row_count):
    result = jnp.zeros((row_count, rimmed.shape[1]), jnp.float32)
    for tap_index in range(TAPS):
        result = result + taps_row[tap_index] * rimmed[tap_index : tap_index + row_count]
    return result


def shards(
    exposure, block_dest, band_offset, col_shift, block_weight, basis_width, kernel_fit, fit_owner
):
    rows_dev, col_count = exposure.shape
    num_blocks = block_dest.shape[0]
    block_rows = rows_dev // num_blocks
    peers = lax.axis_size("patch")
    capacity = num_blocks // peers + 1
    source_blocks = exposure.reshape(num_blocks, block_rows, col_count)
    dest_local = block_dest % num_blocks
    dest_peer = block_dest // num_blocks % peers
    peer_onehot = (dest_peer[:, None] == jnp.arange(peers)[None, :]).astype(jnp.int32)
    rank_in_peer = jnp.sum((jnp.cumsum(peer_onehot, axis=0) - peer_onehot) * peer_onehot, axis=1)
    position = dest_peer * capacity + rank_in_peer
    select = jnp.arange(peers * capacity)[:, None] == position[None, :]
    select_bf = select.astype(jnp.bfloat16)
    slot_sent = jnp.sum(jnp.where(select, dest_local[None, :] + 1, 0), axis=1) - 1
    weight_sent = jnp.sum(jnp.where(select, block_weight[None, :], 0.0), axis=1)
    weighted = resample_blocks(source_blocks, band_offset, col_shift, block_weight).astype(
        jnp.bfloat16
    )
    packed = jnp.einsum(
        "ib,brw->irw", select_bf, weighted, preferred_element_type=jnp.float32
    ).astype(jnp.bfloat16)
    arrived, slot_got, weight_got = (
        lax.all_to_all(packed, "patch", split_axis=0, concat_axis=0, tiled=True),
        lax.all_to_all(slot_sent, "patch", split_axis=0, concat_axis=0, tiled=True),
        lax.all_to_all(
            weight_sent.astype(jnp.bfloat16), "patch", split_axis=0, concat_axis=0, tiled=True
        ).astype(weight_sent.dtype),
    )
    slot_match = jnp.arange(num_blocks)[:, None] == slot_got[None, :]
    coadd_sum = jnp.einsum(
        "si,irw->srw", slot_match.astype(jnp.bfloat16), arrived, preferred_element_type=jnp.float32
    )
    coverage = jnp.sum(jnp.where(slot_match, weight_got[None, :], 0.0), axis=1)
    image = (
        (coadd_sum / jnp.maximum(coverage, 1.0)[:, None, None])
        .astype(jnp.bfloat16)
        .reshape(rows_dev, col_count)
    )
    half_span = (TAPS - 1) // 2
    profile = gaussian_taps(basis_width)
    col_taps = profile.astype(jnp.bfloat16)
    chosen = spread(kernel_fit, ("det", "patch"), fit_owner[0])
    coeff = chosen[0]
    global_start = lax.axis_index(("det", "patch")) * rows_dev
    all_rows = rows_dev * lax.axis_size(("det", "patch"))
    row_pos = 2.0 * (global_start + jnp.arange(rows_dev)).astype(jnp.float32) / (all_rows - 1) - 1.0
    col_pos = 2.0 * jnp.arange(col_count).astype(jnp.float32) / (col_count - 1) - 1.0
    rimmed = with_halo(image, ((("det", "patch"), 0),), half_span)
    smoothed_list = [column_convolve(rimmed, col_taps[basis_index]) for basis_index in range(BASES)]
    matched = jnp.zeros((rows_dev, col_count), jnp.float32)
    for basis_index in range(BASES):
        rowconv = row_convolve(smoothed_list[basis_index], profile[basis_index], rows_dev)
        matched = matched + poly_field(coeff[basis_index], row_pos, col_pos) * rowconv
    return (matched.astype(jnp.bfloat16), coverage)


def solution(mesh):
    in_specs = (
        P(("det", "patch"), None),
        P(("det", "patch")),
        P(("det", "patch")),
        P(("det", "patch")),
        P(("det", "patch")),
        P(),
        P(("det", "patch"), None, None),
        P(),
    )
    out_specs = (P(("det", "patch"), None), P(("det", "patch")))
    return jax.shard_map(shards, mesh=mesh, in_specs=in_specs, out_specs=out_specs, check_vma=False)
```

profile of v0, /device:TPU:1, one launch (start us, length us, event | category | flops | bytes accessed | tf_op | source)
XLA Modules:
  0.0 838.8 jit_solution(17805499576924528894)
XLA Ops:
  3.1 6.4 all-to-all-start.2
  21.2 29.8 %convolution_convert_fusion = bf16[40,8,4096]{2,0,1:T(8,128)(2,1)S(1)} fusion(bf16[32,8,4096]{2,0,1:T(8,128)(2,1)} %copy.21, f32[32]{0:T(128)S(1)} %copy-done.59, f32[32]{0:T(128)S(1)} %get-tuple-element.81, f32[32]{0:T(128)S(1)} %get-tuple-element.62, f32[32]{0:T(128)S(1)} %get-tuple-element.63, f32[32]{0:T(128)S(1)} %get-tuple-element.64, ...), kind=kOutput, calls=%fused_computation | convolution fusion | flops 155452672 | bytes 4721664 | tf_op jit(solution)/shard_map/ib,brw->irw/dot_general | solution.py:126
  60.0 78.6 %psum.7 = f32[1,3,6]{2,0,1:T(1,128)S(1)} all-reduce(f32[1,3,6]{2,0,1:T(1,128)S(1)} %broadcast_select_fusion), channel_id=1, replica_groups=mesh['det'=4,'patch'=8] {'det','patch'}, use_global_device_ids=true, to_apply=%region_0.1 | all-reduce | flops 18 | bytes 144 | tf_op jit(solution)/shard_map/psum | solution.py:13
  247.6 7.8 fusion.54
  255.4 6.4 fusion.153
  261.8 7.9 fusion.50
  269.7 6.4 fusion.167
  277.5 19.4 %slice_multiply_fusion.45 = (f32[256,8,512]{2,1,0:T(8,128)}, f32[256,8,512]{2,1,0:T(8,128)}, f32[256,8,512]{2,1,0:T(8,128)}, f32[256,8,512]{2,1,0:T(8,128)}, f32...) fusion(f32[286,8,512]{2,1,0:T(8,128)S(1)} %add_add_fusion.1, ...), kind=kLoop, calls=%fused_computation.66 | loop fusion | flops 9437184 | bytes 75497504 | tf_op jit(solution)/shard_map/mul | solution.py:101
  296.9 8.1 copy.48
  311.0 6.3 copy.56
  352.9 6.6 add_add_fusion.2
  359.4 34.1 %slice_multiply_fusion.76 = (f32[256,8,512]{2,1,0:T(8,128)}, f32[256,8,512]{2,1,0:T(8,128)}, f32[256,8,512]{2,1,0:T(8,128)}, f32[256,8,512]{2,1,0:T(8,128)}, f32...) fusion(f32[286,8,512]{2,1,0:T(8,128)} %add_add_fusion.2, ...), kind=kLoop, calls=%fused_computation.112 | loop fusion | flops 9437184 | bytes 75497504 | tf_op jit(solution)/shard_map/mul | solution.py:101
  393.5 8.1 copy.32
  425.2 6.2 copy.43
  449.2 12.5 %slice_multiply_fusion.44 = (f32[256,8,512]{2,1,0:T(8,128)}, f32[256,8,512]{2,1,0:T(8,128)}, f32[256,8,512]{2,1,0:T(8,128)}, f32[256,8,512]{2,1,0:T(8,128)}, f32[256,8,512]{2,1,0:T(8,128)}, /*index=5*/f32[256,8,512]{2,1,0:T(8,128)}) fusion(f32[286,8,512]{2,1,0:T(8,128)S(1)} %add_add_fusion.1, f32[]{:T(128)} %bitcast.134, f32[]{:T(128)} %bitcast.139, ...), kind=kLoop, calls=%fused_computation.65 | loop fusion | flops 6291456 | bytes 50331672 | tf_op jit(solution)/shard_map/mul | solution.py:101
  461.7 8.1 copy.49
  475.8 6.2 copy.51
  499.6 21.1 %slice_multiply_fusion.75 = (f32[256,8,512]{2,1,0:T(8,128)}, f32[256,8,512]{2,1,0:T(8,128)}, f32[256,8,512]{2,1,0:T(8,128)}, f32[256,8,512]{2,1,0:T(8,128)}, f32[256,8,512]{2,1,0:T(8,128)}, /*index=5*/f32[256,8,512]{2,1,0:T(8,128)}) fusion(f32[286,8,512]{2,1,0:T(8,128)} %add_add_fusion.2, f32[]{:T(128)} %bitcast.63, f32[]{:T(128)} %bitcast.68, f32[]{:T(128)} %bitcast.67, ...), kind=kLoop, calls=%fused_computation.111 | loop fusion | flops 6291456 | bytes 50331672 | tf_op jit(solution)/shard_map/mul | solution.py:101
  520.7 8.1 copy.33
  558.5 19.5 %fusion.16 = f32[256,8,512]{2,1,0:T(8,128)} fusion(f32[286,8,512]{2,1,0:T(8,128)S(1)} %add_add_fusion.1, f32[]{:T(128)} %bitcast.132, f32[]{:T(128)} %bitcast.131, f32[]{:T(128)} %bitcast.130, f32[]{:T(128)} %bitcast.129, f32[]{:T(128)} %bitcast.128, f32[]{:T(128)} %bitcast.127, f32[]{:T(128)} %bitcast.126, f32[]{:T(128)} %bitcast.125, f32[]{:T(128)} %bitcast.124, ...), kind=kLoop, calls=%fused_computation.68 | loop fusion | flops 32505856 | bytes 71303232 | tf_op jit(solution)/shard_map/add | solution.py:101
  578.0 8.2 copy.47
  586.3 19.6 %fusion.31 = f32[256,8,512]{2,1,0:T(8,128)} fusion(f32[286,8,512]{2,1,0:T(8,128)S(1)} %bitcast.446, f32[]{:T(128)} %bitcast.61, f32[]{:T(128)} %bitcast.60, f32[]{:T(128)} %bitcast.59, f32[]{:T(128)} %bitcast.58, f32[]{:T(128)} %bitcast.57, f32[]{:T(128)} %bitcast.56, f32[]{:T(128)} %bitcast.55, f32[]{:T(128)} %bitcast.54, f32[]{:T(128)} %bitcast.53, ...), kind=kLoop, calls=%fused_computation.114 | loop fusion | flops 32505856 | bytes 71303232 | tf_op jit(solution)/shard_map/add | solution.py:101
  605.8 8.2 copy.31
  614.0 7.5 add_add_fusion
  621.6 19.5 %slice_multiply_fusion.14 = (f32[256,8,512]{2,1,0:T(8,128)}, f32[256,8,512]{2,1,0:T(8,128)}, f32[256,8,512]{2,1,0:T(8,128)}, f32[256,8,512]{2,1,0:T(8,128)}, f32...) fusion(f32[286,8,512]{2,1,0:T(8,128)S(1)} %add_add_fusion, ...), kind=kLoop, calls=%fused_computation.20 | loop fusion | flops 9437184 | bytes 75497504 | tf_op jit(solution)/shard_map/mul | solution.py:101
  641.0 8.2 copy.64
  655.1 6.3 copy.72
  697.0 12.3 %slice_multiply_fusion.13 = (f32[256,8,512]{2,1,0:T(8,128)}, f32[256,8,512]{2,1,0:T(8,128)}, f32[256,8,512]{2,1,0:T(8,128)}, f32[256,8,512]{2,1,0:T(8,128)}, f32[256,8,512]{2,1,0:T(8,128)}, /*index=5*/f32[256,8,512]{2,1,0:T(8,128)}) fusion(f32[286,8,512]{2,1,0:T(8,128)S(1)} %add_add_fusion, f32[]{:T(128)} %bitcast.205, f32[]{:T(128)} %bitcast.210, ...), kind=kLoop, calls=%fused_computation.19 | loop fusion | flops 6291456 | bytes 50331672 | tf_op jit(solution)/shard_map/mul | solution.py:101
  709.3 8.1 copy.65
  746.8 19.5 %fusion.1 = f32[256,8,512]{2,1,0:T(8,128)} fusion(f32[286,8,512]{2,1,0:T(8,128)S(1)} %add_add_fusion, f32[]{:T(128)} %bitcast.203, f32[]{:T(128)} %bitcast.202, f32[]{:T(128)} %bitcast.201, f32[]{:T(128)} %bitcast.200, f32[]{:T(128)} %bitcast.199, f32[]{:T(128)} %bitcast.198, f32[]{:T(128)} %bitcast.197, f32[]{:T(128)} %bitcast.196, f32[]{:T(128)} %bitcast.195, ...), kind=kLoop, calls=%fused_computation.22 | loop fusion | flops 32505856 | bytes 71303232 | tf_op jit(solution)/shard_map/add | solution.py:101
  766.5 8.0 copy.63
  774.7 63.9 %add_convert_fusion = bf16[256,4096]{1,0:T(8,128)(2,1)} fusion(f32[256,4096]{1,0:T(8,128)} %bitcast.487, f32[256,4096]{1,0:T(8,128)} %bitcast.486, f32[256,4096]{1,0:T(8,128)} %bitcast.485, f32[256,4096]{1,0:T(8,128)} %bitcast.484, f32[256,4096]{1,0:T(8,128)} %bitcast.483, f32[256,4096]{1,0:T(8,128)} %bitcast.482, f32[256,4096]{1,0:T(8,128)} %bitcast.481, ...), kind=kLoop, calls=%fused_computation.144 | loop fusion | flops 69206016 | bytes 203578368 | tf_op jit(solution)/shard_map/convert_element_type | solution.py:161
  (242 shorter events, 281.3 us)
Async XLA Ops:
  0.6 20.6 %copy-start.59 = (f32[32]{0:T(128)S(1)}, f32[32]{0:T(128)}, u32[]{:S(2)}) copy-start(f32[32]{0:T(128)} %param.13) | copy-start | bytes 388
  3.1 12.7 %all-to-all-start.2 = ((bf16[8,5,1]{1,2,0:T(2,128)(2,1)}), bf16[8,5,1]{1,2,0:T(2,128)(2,1)S(1)}, u32[]{:S(2)}, u32[]{:S(2)}) async-start(bf16[8,5,1]{1,2,0:T(2,128)(2,1)} %convert_element_type.1294), calls=%async_computation.2 | async-start | bytes 8192 | tf_op jit(solution)/shard_map/all_to_all | solution.py:132
  15.7 38.1 %all-to-all-start = ((s32[8,5,1]{1,2,0:T(1,128)}), s32[8,5,1]{1,2,0:T(1,128)S(1)}, u32[]{:S(2)}, u32[]{:S(2)}) async-start(s32[8,5,1]{1,2,0:T(1,128)} %bitcast.8), calls=%async_computation | async-start | bytes 8192 | tf_op jit(solution)/shard_map/all_to_all | solution.py:131
  51.0 9.0 %copy-start.57 = (f32[1,3,6]{2,0,1:T(1,128)S(1)}, f32[1,3,6]{2,0,1:T(1,128)}, u32[]{:S(2)}) copy-start(f32[1,3,6]{2,0,1:T(1,128)} %param.15) | copy-start | bytes 220
  51.0 87.6 %copy-start.60 = (f32[3]{0:T(128)S(1)}, f32[3]{0:T(128)}, u32[]{:S(2)}) copy-start(f32[3]{0:T(128)} %param.14) | copy-start | bytes 40
  53.9 127.8 %all-to-all-start.1 = ((bf16[40,8,4096]{2,1,0:T(8,128)(2,1)}), bf16[40,8,4096]{2,1,0:T(8,128)(2,1)S(1)}, u32[]{:S(2)}, u32[]{:S(2)}) async-start(bf16[40,8,4096]{2,1,0:T(8,128)(2,1)} %copy.23), calls=%async_computation.1 | async-start | bytes 5242880 | tf_op jit(solution)/shard_map/all_to_all | solution.py:130
  186.6 52.1 %collective-permute-start = (bf16[15,4096]{1,0:T(8,128)(2,1)S(1)}, bf16[15,4096]{1,0:T(8,128)(2,1)S(1)}, u32[]{:S(2)}, u32[]{:S(2)}) collective-permute-start(bf16[15,4096]{1,0:T(8,128)(2,1)S(1)} %get-tuple-element.58), channel_id=1, source_target_pairs={{0,1},{1,2},{2,3},{3,4},{4,5},{5,6},{6,7},{7,8},{8,9},{9,10},{10,1... | collective-permute-start | bytes 368648 | tf_op jit(solution)/shard_map/ppermute | solution.py:21
  233.0 7.2 collective-permute-start.1
  241.2 34.9 %copy-start.39 = (bf16[286,7,512]{2,1,0:T(8,128)(2,1)}, bf16[286,7,512]{2,1,0:T(8,128)(2,1)S(1)}, u32[]{:S(2)}) copy-start(bf16[286,7,512]{2,1,0:T(8,128)(2,1)S(1)} %get-tuple-element.55) | copy-start | bytes 6150148
  296.9 8.2 copy-start.21
  311.0 41.8 %slice-start.4 = ((s8[4685824]{0:T(1024)(128)(4,1)}), s8[4194304]{0:T(1024)(128)(4,1)S(1)}, s32[]{:S(2)}) async-start(s8[4685824]{0:T(1024)(128)(4,1)} %bitcast.553), calls=%async_computation.7 | async-start | bytes 8388608
  329.0 23.9 %slice-start.5 = ((s8[4685824]{0:T(1024)(128)(4,1)}), s8[491520]{0:T(1024)(128)(4,1)S(1)}, s32[]{:S(2)}) async-start(s8[4685824]{0:T(1024)(128)(4,1)} %bitcast.553), calls=%async_computation.8 | async-start | bytes 983040
  335.0 17.8 %slice-start.2 = ((s8[4685824]{0:T(1024)(128)(4,1)}), s8[4194304]{0:T(1024)(128)(4,1)S(1)}, s32[]{:S(2)}) async-start(s8[4685824]{0:T(1024)(128)(4,1)} %bitcast.551), calls=%async_computation.5 | async-start | bytes 8388608
  340.8 12.0 %slice-start.3 = ((s8[4685824]{0:T(1024)(128)(4,1)}), s8[491520]{0:T(1024)(128)(4,1)S(1)}, s32[]{:S(2)}) async-start(s8[4685824]{0:T(1024)(128)(4,1)} %bitcast.551), calls=%async_computation.6 | async-start | bytes 983040
  461.7 8.1 copy-start.36
  578.0 8.2 slice-start
  578.0 8.2 slice-start.1
  605.8 8.2 copy-start.41
  641.0 8.2 copy-start.23
  766.4 8.1 copy-start.45
  766.4 8.1 copy-start.46
  766.4 8.1 copy-start.47
  766.4 8.1 copy-start.48
  766.4 8.1 copy-start.49
  766.4 8.1 copy-start.50
  766.4 8.1 copy-start.51
  766.5 8.1 copy-start.52
  766.5 8.1 copy-start.53
  766.5 8.1 copy-start.54
  766.5 8.1 copy-start.55
  766.5 8.1 copy-start.56
  766.5 8.1 copy-start.58
  (41 other events, 254.2 us)
where the time goes:
time: 851 us; the launch traced here: 839 us
  local copies, waits for them, and re-layouts  325 us (38%)
  other arithmetic  263 us (31%)
  matrix products  83.8 us (10%)
  blocking collectives  78.6 us (9%)
  between operations  60.6 us (7%)
  starting transfers between devices  26.6 us (3%)
    unnamed x189, local copies, waits for them, and re-layouts  306 us
    mul x6, other arithmetic, row_convolve(): taps_row[tap_index] * rimmed[tap_index:tap_index + row_count]  119 us
    psum x1, blocking collectives, spread(): return lax.psum(jnp.where(mine, value, jnp.zeros_like(value)), axis)  78.6 us
    convert_element_type x1, other arithmetic, shards(): return (matched.astype(jnp.bfloat16), coverage)  63.9 us
    add x3, other arithmetic, row_convolve(): result + taps_row[tap_index] * rimmed[tap_index:tap_index + row_count]  58.6 us
    dot_general x1, matrix products, shards(): jnp.einsum('ib,brw->irw', select_bf, weighted, preferred_element_type=jnp...  29.8 us
    dot_general x3, matrix products, column_convolve(): jnp.einsum('rna,ab->rnb', tiles, band_table(taps_row, 0), preferred_eleme...  17.8 us
    dot_general x3, matrix products, column_convolve(): jnp.einsum('rna,ab->rnb', before, band_table(taps_row, -1), preferred_ele...  17.1 us
  transfers between devices with their start and end apart: 5, of which 1 were waited for; matrix products, arithmetic and copies ran while one was open for 8% of the time, Pallas kernels for 0%

commit v1 on v0

v1 whole, which is shorter than its diff:
```python
import functools
import math

import jax
import jax.numpy as jnp
from jax import lax
from jax.experimental import pallas as pl
from jax.experimental.pallas import tpu as pltpu
from jax.sharding import PartitionSpec as P

TAPS = 31
HALF = 15
BASES = 3
NPOLY = 6
LANE = 128
SHIFT = 16
EDGE = 16
BOTH = ("det", "patch")
BF = jnp.bfloat16
F32 = jnp.float32
MIB = 1 << 20


def dot(a, b):
    return jnp.dot(a, b, preferred_element_type=F32)


def lanczos(position):
    def sinc(v):
        at = jnp.where(v == 0.0, 1.0, math.pi * v)
        return jnp.where(v == 0.0, 1.0, jnp.sin(at) / at)

    return sinc(position) * sinc(position / 3.0)


def resample_kernel(
    peers, cap, pairs, dest_ref, off_ref, wgt_s_ref, shift_ref, wgt_v_ref, x_ref, out_ref,
    src_ref, count_ref, xf_ref, coef_ref, diff_ref,
):
    blocks, rows, width = xf_ref.shape
    tiles = width // LANE + 1
    step = pl.program_id(0)

    @pl.when(step == 0)
    def _():
        for p in range(peers):
            count_ref[p] = 0
        for q in range(peers * cap):
            src_ref[q] = -1
        for b in range(blocks):
            peer = dest_ref[b] // blocks % peers
            rank = count_ref[peer]
            src_ref[peer * cap + rank] = b
            count_ref[peer] = rank + 1
        xf_ref[...] = x_ref[...].astype(F32).reshape(blocks, rows, width)
        tap = lax.broadcasted_iota(jnp.int32, (8, blocks), 0).astype(F32) - 2.0
        coef_ref[...] = lanczos(tap - shift_ref[...]) * wgt_v_ref[...]
        diff_ref[...] = (
            lax.broadcasted_iota(jnp.int32, diff_ref.shape, 0)
            - lax.broadcasted_iota(jnp.int32, diff_ref.shape, 1)
            - (LANE - SHIFT - 2)
        )

    lane = lax.broadcasted_iota(jnp.int32, (8, LANE), 1)
    block_lane = lax.broadcasted_iota(jnp.int32, (8, blocks), 1)
    zero = jnp.zeros((2 * rows, LANE), BF)

    def one_pair(pair, carry):
        xs, bands, metas = [], [], []
        for side in range(2):
            got = src_ref[(step * pairs + pair) * 2 + side]
            valid = got >= 0
            b = jnp.maximum(got, 0)
            xs.append(xf_ref[b])
            column = jnp.sum(
                jnp.where((block_lane == b) & valid, coef_ref[...], 0.0), axis=1, keepdims=True
            )
            off = off_ref[b]
            diff = diff_ref[...] - off
            band = jnp.zeros(diff.shape, F32)
            for t in range(6):
                band = jnp.where(diff == t, column[t : t + 1, :], band)
            bands.append(band)
            slot = jnp.where(valid, dest_ref[b] % blocks, -1).astype(F32)
            weight = jnp.full((8, LANE), jnp.where(valid, wgt_s_ref[b], 0.0), F32)
            high = weight.astype(BF).astype(F32)
            mid = (weight - high).astype(BF).astype(F32)
            low = weight - high - mid
            metas.append(
                jnp.where(
                    lane == SHIFT,
                    slot,
                    jnp.where(
                        lane == SHIFT + 1,
                        high,
                        jnp.where(lane == SHIFT + 2, mid, jnp.where(lane == SHIFT + 3, low, 0.0)),
                    ),
                )
            )
        x16 = jnp.concatenate(xs, axis=0).astype(BF)
        padded = jnp.concatenate([zero, x16, zero], axis=1)
        windows = jnp.concatenate(
            [padded[:, LANE * t : LANE * (t + 2)] for t in range(tiles)], axis=0
        )
        band = jnp.concatenate(bands, axis=1).astype(BF)
        made = dot(windows, band)
        first = pl.multiple_of(pair * 2 * rows, 2 * rows)
        for t in range(tiles):
            top = made[2 * rows * t : 2 * rows * t + rows, :LANE]
            bottom = made[2 * rows * t + rows : 2 * rows * (t + 1), LANE:]
            if t == 0:
                top = jnp.where(lane < SHIFT, 0.0, top)
                bottom = jnp.where(lane < SHIFT, 0.0, bottom)
            if t == tiles - 1:
                top = jnp.where(lane < SHIFT, top, metas[0])
                bottom = jnp.where(lane < SHIFT, bottom, metas[1])
            out_ref[pl.ds(first, 2 * rows), LANE * t : LANE * (t + 1)] = jnp.concatenate(
                [top, bottom], axis=0
            ).astype(BF)
        return carry

    lax.fori_loop(0, pairs, one_pair, 0)


def resample(exposure, dest, offset, shift, weight, peers, cap):
    rows_dev, width = exposure.shape
    blocks = dest.shape[0]
    rows = rows_dev // blocks
    all_pairs = peers * cap // 2
    steps = 4
    while all_pairs % steps:
        steps -= 1
    pairs = all_pairs // steps
    smem = pl.BlockSpec(memory_space=pltpu.SMEM)
    whole = lambda shape: pl.BlockSpec(shape, lambda i: (0, 0))
    return pl.pallas_call(
        functools.partial(resample_kernel, peers, cap, pairs),
        grid=(steps,),
        in_specs=[smem, smem, smem, whole((1, blocks)), whole((1, blocks)), whole((rows_dev, width))],
        out_specs=pl.BlockSpec((pairs * 2 * rows, width + LANE), lambda i: (i, 0)),
        out_shape=jax.ShapeDtypeStruct((peers * cap * rows, width + LANE), BF),
        scratch_shapes=[
            pltpu.SMEM((peers * cap,), jnp.int32),
            pltpu.SMEM((peers,), jnp.int32),
            pltpu.VMEM((blocks, rows, width), F32),
            pltpu.VMEM((8, blocks), F32),
            pltpu.VMEM((2 * LANE, LANE), jnp.int32),
        ],
        compiler_params=pltpu.CompilerParams(vmem_limit_bytes=40 * MIB),
        name="resample",
    )(dest, offset, weight, shift.reshape(1, blocks), weight.reshape(1, blocks), exposure)


def tables_kernel(inner, width_ref, band_ref, high_ref, low_ref, edge_high_ref, edge_low_ref):
    def weights(k, shape, delta):
        u = lax.broadcasted_iota(jnp.int32, shape, 1) - lax.broadcasted_iota(jnp.int32, shape, 0)
        u = u - delta
        at = (u - HALF).astype(F32)
        value = jnp.exp(-(at * at) / (2.0 * width * width))
        return jnp.where((u >= 0) & (u < TAPS), value, 0.0)

    def put(k, value, high, low):
        top = value.astype(BF)
        high[k] = top
        low[k] = (value - top.astype(F32)).astype(BF)

    for k in range(BASES):
        width = jnp.full((8, LANE), width_ref[k], F32)[:1, :1]
        total = jnp.sum(
            jnp.where(
                lax.broadcasted_iota(jnp.int32, (1, LANE), 1) < TAPS,
                jnp.exp(
                    -((lax.broadcasted_iota(jnp.int32, (1, LANE), 1) - HALF).astype(F32) ** 2)
                    / (2.0 * width * width)
                ),
                0.0,
            ),
            axis=1,
            keepdims=True,
        )
        u = (
            lax.broadcasted_iota(jnp.int32, (2 * LANE, LANE), 0)
            - lax.broadcasted_iota(jnp.int32, (2 * LANE, LANE), 1)
            - 1
        )
        at = (u - HALF).astype(F32)
        value = jnp.exp(-(at * at) / (2.0 * width * width)) / total
        band_ref[:, LANE * k : LANE * (k + 1)] = jnp.where(
            (u >= 0) & (u < TAPS), value, 0.0
        ).astype(BF)
        put(k, weights(k, (inner, inner + 2 * EDGE), 1) / total, high_ref, low_ref)
        put(k, weights(k, (EDGE, 3 * EDGE), 1) / total, edge_high_ref, edge_low_ref)


def tables(basis_width, rows_dev):
    inner = rows_dev - 2 * EDGE
    sd = lambda *shape: jax.ShapeDtypeStruct(shape, BF)
    return pl.pallas_call(
        functools.partial(tables_kernel, inner),
        in_specs=[pl.BlockSpec(memory_space=pltpu.SMEM)],
        out_shape=[
            sd(2 * LANE, BASES * LANE),
            sd(BASES, inner, rows_dev),
            sd(BASES, inner, rows_dev),
            sd(BASES, EDGE, 3 * EDGE),
            sd(BASES, EDGE, 3 * EDGE),
        ],
        compiler_params=pltpu.CompilerParams(vmem_limit_bytes=40 * MIB),
        name="tables",
    )(basis_width)


def coadd_kernel(steps, meta_ref, x_ref, image_ref, top_ref, bottom_ref, cover_ref):
    rows_dev, chunk = image_ref.shape
    arrived = x_ref.shape[0]
    step = pl.program_id(0)
    row = lax.broadcasted_iota(jnp.int32, (arrived, rows_dev), 0)
    col = lax.broadcasted_iota(jnp.int32, (arrived, rows_dev), 1)
    meta = meta_ref[...]
    slot = meta[:, SHIFT : SHIFT + 1].astype(F32).astype(jnp.int32)
    place = jnp.where((slot == col // 8) & (row % 8 == col % 8), 1.0, 0.0).astype(BF)
    pick = lambda v: lax.dot_general(
        place, v, (((0,), (0,)), ((), ())), preferred_element_type=F32
    )
    sums = pick(meta)
    cover = (
        sums[:, SHIFT + 1 : SHIFT + 2] + sums[:, SHIFT + 2 : SHIFT + 3] + sums[:, SHIFT + 3 : SHIFT + 4]
    )
    scale = 1.0 / jnp.maximum(cover, 1.0)
    value = pick(x_ref[...]) * scale
    column = lax.broadcasted_iota(jnp.int32, (1, chunk), 1) + step * chunk
    value = jnp.where(column < steps * chunk - LANE + SHIFT, value, 0.0).astype(BF)
    image_ref[...] = value
    top_ref[...] = value[:EDGE]
    bottom_ref[...] = value[rows_dev - EDGE :]

    @pl.when(step == 0)
    def _():
        cover_ref[...] = jnp.broadcast_to(cover, (rows_dev, LANE))


def coadd(arrived, rows_dev):
    count, width = arrived.shape
    steps = 3
    chunk = width // steps
    last = width // LANE - 1
    return pl.pallas_call(
        functools.partial(coadd_kernel, steps),
        grid=(steps,),
        in_specs=[
            pl.BlockSpec((count, LANE), lambda i: (0, last)),
            pl.BlockSpec((count, chunk), lambda i: (0, i)),
        ],
        out_specs=[
            pl.BlockSpec((rows_dev, chunk), lambda i: (0, i)),
            pl.BlockSpec((EDGE, chunk), lambda i: (0, i)),
            pl.BlockSpec((EDGE, chunk), lambda i: (0, i)),
            pl.BlockSpec((rows_dev, LANE), lambda i: (0, 0)),
        ],
        out_shape=[
            jax.ShapeDtypeStruct((rows_dev, width), BF),
            jax.ShapeDtypeStruct((EDGE, width), BF),
            jax.ShapeDtypeStruct((EDGE, width), BF),
            jax.ShapeDtypeStruct((rows_dev, LANE), F32),
        ],
        compiler_params=pltpu.CompilerParams(vmem_limit_bytes=40 * MIB),
        name="coadd",
    )(arrived, arrived)


def match_columns(x, high, low, band, fit_ref, y, first_col, col_count):
    parts = [dot(x[:, LANE * i : LANE * (i + 2)], band) for i in range(2)]
    xx = (first_col + lax.broadcasted_iota(jnp.int32, (1, 2 * LANE), 1)).astype(F32)
    xx = 2.0 * xx / (col_count - 1) - 1.0
    total = None
    for k in range(BASES):
        smooth = jnp.concatenate([p[:, LANE * k : LANE * (k + 1)] for p in parts], axis=1).astype(BF)
        both = dot(high[k], smooth) + dot(low[k], smooth)
        c = lambda i: fit_ref[k, i]
        field = (c(0) + c(2) * y + c(5) * y * y) + (c(1) + c(4) * y) * xx + c(3) * (xx * xx)
        total = field * both if total is None else total + field * both
    return total.astype(BF)


def row_position(base, count, all_rows):
    at = (base + lax.broadcasted_iota(jnp.int32, (count, 1), 0)).astype(F32)
    return 2.0 * at / (all_rows - 1) - 1.0


def inner_kernel(
    all_rows, col_count, start_ref, fit_ref, x_ref, next_ref, band_ref, high_ref, low_ref, out_ref
):
    rows_dev, chunk = out_ref.shape
    inner = rows_dev - 2 * EDGE
    step = pl.program_id(0)
    y = row_position(start_ref[0] + EDGE, inner, all_rows)
    x = jnp.concatenate([x_ref[...], next_ref[...]], axis=1)
    for g in range(chunk // (2 * LANE)):
        out_ref[EDGE : EDGE + inner, 2 * LANE * g : 2 * LANE * (g + 1)] = match_columns(
            x[:, 2 * LANE * g : 2 * LANE * g + 3 * LANE], high_ref, low_ref, band_ref[...], fit_ref, y,
            step * chunk + 2 * LANE * g, col_count,
        )


def edge_kernel(
    all_rows, col_count, rows_dev, start_ref, fit_ref, above_ref, top_ref, bottom_ref, below_ref,
    band_ref, high_ref, low_ref, old_ref, out_ref,
):
    side = pl.program_id(0)
    first = start_ref[0] + side * (rows_dev - EDGE)
    y = row_position(first, EDGE, all_rows)
    lower = side == 1
    for g in range(col_count // (2 * LANE)):
        cols = slice(2 * LANE * g, 2 * LANE * g + 3 * LANE)
        upper_rows = jnp.concatenate([above_ref[:, cols], top_ref[:, cols]], axis=0)
        lower_rows = jnp.concatenate([bottom_ref[:, cols], below_ref[:, cols]], axis=0)
        x = jnp.where(lower, lower_rows, upper_rows)
        out_ref[:, 2 * LANE * g : 2 * LANE * (g + 1)] = match_columns(
            x, high_ref, low_ref, band_ref[...], fit_ref, y, 2 * LANE * g, col_count
        )


def match_inner(image, start, fit, band, high, low, all_rows):
    rows_dev, width = image.shape
    col_count = width - LANE
    chunk = 512
    inner = rows_dev - 2 * EDGE
    smem = pl.BlockSpec(memory_space=pltpu.SMEM)
    return pl.pallas_call(
        functools.partial(inner_kernel, all_rows, col_count),
        grid=(col_count // chunk,),
        in_specs=[
            smem,
            smem,
            pl.BlockSpec((rows_dev, chunk), lambda i: (0, i)),
            pl.BlockSpec((rows_dev, LANE), lambda i: (0, (i + 1) * (chunk // LANE))),
            pl.BlockSpec(band.shape, lambda i: (0, 0)),
            pl.BlockSpec(high.shape, lambda i: (0, 0, 0)),
            pl.BlockSpec(low.shape, lambda i: (0, 0, 0)),
        ],
        out_specs=pl.BlockSpec((rows_dev, chunk), lambda i: (0, i)),
        out_shape=jax.ShapeDtypeStruct((rows_dev, col_count), BF),
        compiler_params=pltpu.CompilerParams(vmem_limit_bytes=40 * MIB),
        name="match_inner",
    )(start, fit, image, image, band, high, low)


def match_edges(matched, image, above, below, start, fit, band, high, low, all_rows):
    rows_dev, width = image.shape
    col_count = width - LANE
    smem = pl.BlockSpec(memory_space=pltpu.SMEM)
    strip = lambda rows, at: pl.BlockSpec((rows, width), lambda i: (at, 0))
    return pl.pallas_call(
        functools.partial(edge_kernel, all_rows, col_count, rows_dev),
        grid=(2,),
        in_specs=[
            smem,
            smem,
            strip(EDGE, 0),
            strip(2 * EDGE, 0),
            strip(2 * EDGE, rows_dev // (2 * EDGE) - 1),
            strip(EDGE, 0),
            pl.BlockSpec(band.shape, lambda i: (0, 0)),
            pl.BlockSpec(high.shape, lambda i: (0, 0, 0)),
            pl.BlockSpec(low.shape, lambda i: (0, 0, 0)),
            pl.BlockSpec(memory_space=pl.ANY),
        ],
        out_specs=pl.BlockSpec((EDGE, col_count), lambda i: (i * (rows_dev // EDGE - 1), 0)),
        out_shape=jax.ShapeDtypeStruct(matched.shape, BF),
        input_output_aliases={9: 0},
        compiler_params=pltpu.CompilerParams(vmem_limit_bytes=40 * MIB),
        name="match_edges",
    )(start, fit, above, image, image, below, band, high, low, matched)


def cube_sum(value):
    for axis in BOTH[::-1]:
        count = lax.axis_size(axis)
        span = 1
        while span < count:
            value = value + lax.ppermute(value, axis, [(i, i ^ span) for i in range(count)])
            span *= 2
    return value


def shards(
    exposure, block_dest, band_offset, col_shift, block_weight, basis_width, kernel_fit, fit_owner
):
    rows_dev, _ = exposure.shape
    blocks = block_dest.shape[0]
    peers = lax.axis_size("patch")
    devices = lax.axis_size(BOTH)
    cap = blocks // peers + 1
    me = lax.axis_index(BOTH)
    payload = resample(exposure, block_dest, band_offset, col_shift, block_weight, peers, cap)
    arrived = lax.all_to_all(payload, "patch", split_axis=0, concat_axis=0, tiled=True)
    fit = cube_sum(jnp.where(me == fit_owner[0], kernel_fit[0], 0.0))
    band, high, low, edge_high, edge_low = tables(basis_width, rows_dev)
    image, top, bottom, cover = coadd(arrived, rows_dev)
    down = [(i, i + 1) for i in range(devices - 1)]
    up = [(i + 1, i) for i in range(devices - 1)]
    above = lax.ppermute(bottom, BOTH, down)
    below = lax.ppermute(top, BOTH, up)
    start = jnp.full((1,), me * rows_dev, jnp.int32)
    all_rows = rows_dev * devices
    matched = match_inner(image, start, fit, band, high, low, all_rows)
    matched = match_edges(
        matched, image, above, below, start, fit, band, edge_high, edge_low, all_rows
    )
    coverage = cover.reshape(blocks, rows_dev // blocks, LANE)[:, 0, 0]
    return matched, coverage


def solution(mesh):
    in_specs = (
        P(BOTH, None),
        P(BOTH),
        P(BOTH),
        P(BOTH),
        P(BOTH),
        P(),
        P(BOTH, None, None),
        P(),
    )
    out_specs = (P(BOTH, None), P(BOTH))
    return jax.shard_map(shards, mesh=mesh, in_specs=in_specs, out_specs=out_specs, check_vma=False)
```

time: 851 us -> 132 us (0.16); the launches traced: 839 us -> 130 us
  local copies, waits for them, and re-layouts: 325 us -> 9.62 us
  other arithmetic: 263 us -> 0.02 us
  matrix products: 83.8 us -> 0 us
  blocking collectives: 78.6 us -> 0 us
  waiting for transfers between devices: 1.45 us -> 62.8 us
  between operations: 60.6 us -> 1.4 us
  Pallas kernels: 0 us -> 32 us
    unnamed x189 -> x22, local copies, waits for them, and re-layouts: 306 us -> 9.61 us
    mul x14 -> x0, other arithmetic: 132 us -> none  [the longest x6 119 us: row_convolve(): taps_row[tap_index] * rimmed[tap_index:tap_index + row_count]]
    dot_general x11 -> x0, matrix products: 83.8 us -> none  [the longest x1 29.8 us: shards(): jnp.einsum('ib,brw->irw', select_bf, weighted, preferred_element_type=jnp...]
    psum x1 -> x0, blocking collectives: 78.6 us -> none  [spread(): return lax.psum(jnp.where(mine, value, jnp.zeros_like(value)), axis)]
    convert_element_type x3 -> x0, other arithmetic: 64 us -> none  [the longest x1 63.9 us: shards(): return (matched.astype(jnp.bfloat16), coverage)]
    add x8 -> x5, other arithmetic: 64 us -> 0.02 us  [cube_sum(): value + lax.ppermute(value, axis, [(i, i ^ span) for i in range(count)])]
    all_to_all x3 -> x1, waiting for transfers between devices: 0.01 us -> 58.1 us  [shards(): lax.all_to_all(payload, 'patch', split_axis=0, concat_axis=0, tiled=True)]
    pallas_call x0 -> x5, Pallas kernels: none -> 32 us  [the longest x1 10.5 us: match_inner(): pl.pallas_call(functools.partial(inner_kernel, all_rows, col_count), grid...]
  transfers between devices with their start and end apart: 5 -> 8, of which waited for: 1 -> 5; matrix products, arithmetic and copies ran while one was open for 8% -> 0% of each run, Pallas kernels for 0% -> 11%
where the time goes in v1:
time: 132 us; the launch traced here: 130 us
  waiting for transfers between devices  62.8 us (48%)
  Pallas kernels  32 us (24%)
  starting transfers between devices  24.6 us (19%)
  local copies, waits for them, and re-layouts  9.62 us (7%)
  between operations  1.4 us (1%)
    all_to_all x1, waiting for transfers between devices, shards(): lax.all_to_all(payload, 'patch', split_axis=0, concat_axis=0, tiled=True)  58.1 us
    pallas_call x1, Pallas kernels, match_inner(): pl.pallas_call(functools.partial(inner_kernel, all_rows, col_count), grid...  10.5 us
    ppermute x5, starting transfers between devices, cube_sum(): lax.ppermute(value, axis, [(i, i ^ span) for i in range(count)])  9.91 us
    unnamed x22, local copies, waits for them, and re-layouts  9.61 us
    pallas_call x1, Pallas kernels, resample(): pl.pallas_call(functools.partial(resample_kernel, peers, cap, pairs), gri...  8.85 us
    pallas_call x1, Pallas kernels, match_edges(): pl.pallas_call(functools.partial(edge_kernel, all_rows, col_count, rows_d...  8.44 us
    all_to_all x1, starting transfers between devices, shards(): lax.all_to_all(payload, 'patch', split_axis=0, concat_axis=0, tiled=True)  6.46 us
    ppermute x1, starting transfers between devices, shards(): below = lax.ppermute(top, BOTH, up)  4.8 us
  transfers between devices with their start and end apart: 8, of which 5 were waited for; matrix products, arithmetic and copies ran while one was open for 0% of the time, Pallas kernels for 11%

profile of v1, /device:TPU:1, one launch (start us, length us, event | category | flops | bytes accessed | tf_op | source)
XLA Modules:
  0.0 130.4 jit_solution(3144304135113493240)
XLA Ops:
  0.6 0.0 copy-start.3
  0.6 1.6 %copy-done.3 = bf16[256,4096]{1,0:T(8,128)(2,1)S(1)} copy-done((bf16[256,4096]{1,0:T(8,128)(2,1)S(1)}, bf16[256,4096]{1,0:T(8,128)(2,1)}, u32[]{:S(2)}) %copy-start.3) | copy-done | bytes 2097176
  2.2 0.7 copy-done.4
  2.9 0.7 copy-done.5
  3.5 0.7 copy-done.6
  4.2 0.7 copy-done.7
  4.8 8.9 %resample.1 = bf16[320,4224]{1,0:T(8,128)(2,1)S(1)} custom-call(s32[32]{0:T(128)S(1)} %copy-done.5, s32[32]{0:T(128)S(1)} %copy-done.6, f32[32]{0:T(128)S(1)} %copy-done.4, f32[1,32]{1,0:T(1,128)S(1)} %bitcast.19, f32[1,32]{1,0:T(1,128)S(1)} %bitcast.17, bf16[256,4096]{1,0:T(8,128)(2,1)S(1)} %copy-done.3), custom_call_target="tpu_custom_call" | custom-call | tf_op jit(solution)/shard_map/resample/pallas_call | solution.py:136
  13.7 1.5 %copy-done.2 = bf16[320,4224]{1,0:T(8,128)(2,1)} copy-done((bf16[320,4224]{1,0:T(8,128)(2,1)}, bf16[320,4224]{1,0:T(8,128)(2,1)S(1)}, u32[]{:S(2)}) %copy-start.2) | copy-done | bytes 2703384
  15.2 6.5 %all-to-all-start = ((bf16[8,40,4224]{2,1,0:T(8,128)(2,1)}), bf16[8,40,4224]{2,1,0:T(8,128)(2,1)S(1)}, u32[]{:S(2)}, u32[]{:S(2)}) async-start(bf16[8,40,4224]{2,1,0:T(8,128)(2,1)} %bitcast.16), calls=%async_computation | async-start | bytes 5406720 | tf_op jit(solution)/shard_map/all_to_all | solution.py:396
  22.4 0.0 copy-done.9
  22.4 1.5 %collective-permute-start = (f32[3,6]{1,0:T(4,128)S(1)}, f32[3,6]{1,0:T(4,128)S(1)}, u32[]{:S(2)}, u32[]{:S(2)}) collective-permute-start(f32[3,6]{1,0:T(4,128)S(1)} %bitcast.20), channel_id=1, source_target_pairs={{0,1},{1,0},{2,3},{3,2},{4,5},{5,4},{6,7},{7,6},{8,9},{9,8},{10,11... | collective-permute-start | bytes 224 | tf_op jit(solution)/shard_map/ppermute | solution.py:381
  23.9 58.1 %all-to-all-done = bf16[8,40,4224]{2,1,0:T(8,128)(2,1)S(1)} async-done(((bf16[8,40,4224]{2,1,0:T(8,128)(2,1)}), bf16[8,40,4224]{2,1,0:T(8,128)(2,1)S(1)}, u32[]{:S(2)}, u32[]{:S(2)}) %all-to-all-start) | async-done | bytes 2703392 | tf_op jit(solution)/shard_map/all_to_all | solution.py:396
  82.1 1.5 %copy-done = bf16[8,40,4224]{2,1,0:T(8,128)(2,1)} copy-done((bf16[8,40,4224]{2,1,0:T(8,128)(2,1)}, bf16[8,40,4224]{2,1,0:T(8,128)(2,1)S(1)}, u32[]{:S(2)}) %copy-start) | copy-done | bytes 2703384
  83.6 1.8 %copy-done.1 = bf16[8,40,4224]{2,1,0:T(8,128)(2,1)S(1)} copy-done((bf16[8,40,4224]{2,1,0:T(8,128)(2,1)S(1)}, bf16[8,40,4224]{2,1,0:T(8,128)(2,1)}, u32[]{:S(2)}) %copy-start.1) | copy-done | bytes 2703384
  85.3 3.4 %coadd.1 = (bf16[256,4224]{1,0:T(8,128)(2,1)S(1)}, bf16[16,4224]{1,0:T(8,128)(2,1)}, bf16[16,4224]{1,0:T(8,128)(2,1)}, f32[256,128]{1,0:T(8,128)S(1)}) custom-call(bf16[320,4224]{1,0:T(8,128)(2,1)S(1)} %bitcast.14, bf16[320,4224]{1,0:T(8,128)(2,1)S(1)} %bitcast.15), custom_call_target="tpu_custom_call" | custom-call | tf_op jit(solution)/shard_map/coadd/pallas_call | solution.py:247
  88.7 3.5 %collective-permute-start.5 = (bf16[16,4224]{1,0:T(8,128)(2,1)}, bf16[16,4224]{1,0:T(8,128)(2,1)S(1)}, u32[]{:S(2)}, u32[]{:S(2)}) collective-permute-start(bf16[16,4224]{1,0:T(8,128)(2,1)} %get-tuple-element.11), channel_id=1, source_target_pairs={{0,1},{1,2},{2,3},{3,4},{4,5},{5,6},{6,7},{7,8},{8,9},{9,10},{10,1... | collective-permute-start | bytes 405512 | tf_op jit(solution)/shard_map/ppermute | solution.py:402
  92.2 4.8 %collective-permute-start.6 = (bf16[16,4224]{1,0:T(8,128)(2,1)}, bf16[16,4224]{1,0:T(8,128)(2,1)S(1)}, u32[]{:S(2)}, u32[]{:S(2)}) collective-permute-start(bf16[16,4224]{1,0:T(8,128)(2,1)} %get-tuple-element.13), channel_id=1, source_target_pairs={{1,0},{2,1},{3,2},{4,3},{5,4},{6,5},{7,6},{8,7},{9,8},{10,9},{11,1... | collective-permute-start | bytes 405512 | tf_op jit(solution)/shard_map/ppermute | solution.py:403
  97.0 0.0 collective-permute-done
  97.0 0.1 collective-permute-start.1
  97.1 2.5 %collective-permute-done.1 = f32[3,6]{1,0:T(4,128)S(1)} collective-permute-done((f32[3,6]{1,0:T(4,128)S(1)}, f32[3,6]{1,0:T(4,128)S(1)}, u32[]{:S(2)}, u32[]{:S(2)}) %collective-permute-start.1) | collective-permute-done | bytes 104 | tf_op jit(solution)/shard_map/ppermute | solution.py:381
  99.6 2.1 %collective-permute-start.2 = (f32[3,6]{1,0:T(4,128)S(1)}, f32[3,6]{1,0:T(4,128)S(1)}, u32[]{:S(2)}, u32[]{:S(2)}) collective-permute-start(f32[3,6]{1,0:T(4,128)S(1)} %add.20), channel_id=1, source_target_pairs={{0,4},{1,5},{2,6},{3,7},{4,0},{5,1},{6,2},{7,3},{8,12},{9,13},{10,... | collective-permute-start | bytes 224 | tf_op jit(solution)/shard_map/ppermute | solution.py:381
  101.6 1.3 collective-permute-done.2
  102.9 2.2 %collective-permute-start.3 = (f32[3,6]{1,0:T(4,128)S(1)}, f32[3,6]{1,0:T(4,128)S(1)}, u32[]{:S(2)}, u32[]{:S(2)}) collective-permute-start(f32[3,6]{1,0:T(4,128)S(1)} %add.21), channel_id=1, source_target_pairs={{0,8},{8,0},{16,24},{24,16},{1,9},{9,1},{17,25},{25,17},{2,10},{10... | collective-permute-start | bytes 224 | tf_op jit(solution)/shard_map/ppermute | solution.py:381
  105.1 0.8 collective-permute-done.3
  106.0 4.0 %collective-permute-start.4 = (f32[3,6]{1,0:T(4,128)S(1)}, f32[3,6]{1,0:T(4,128)S(1)}, u32[]{:S(2)}, u32[]{:S(2)}) collective-permute-start(f32[3,6]{1,0:T(4,128)S(1)} %add.22), channel_id=1, source_target_pairs={{0,16},{8,24},{16,0},{24,8},{1,17},{9,25},{17,1},{25,9},{2,18},{10... | collective-permute-start | bytes 224 | tf_op jit(solution)/shard_map/ppermute | solution.py:381
  110.0 0.9 tables.1
  110.8 0.1 collective-permute-done.4
  110.9 0.6 copy.13
  111.5 10.5 %match_inner.1.old_ref = bf16[256,4096]{1,0:T(8,128)(2,1)} custom-call(s32[1]{0:T(128)} %bitcast.start_ref, f32[3,6]{1,0:T(4,128)S(1)} %add.23.fit_ref, bf16[256,4224]{1,0:T(8,128)(2,1)S(1)} %get-tuple-element.12.x_ref.next_ref.top_ref.bottom_ref, bf16[256,4224]{1,0:T(8,128)(2,1)S(1)} %get-tuple-element.12.x_ref.next_ref.top_ref.bottom_ref, ...), custom_call_target="tpu_custom_call" | custom-call | tf_op jit(solution)/shard_map/match_inner/pallas_call | solution.py:329
  122.0 0.0 collective-permute-done.5.above_ref
  122.0 0.0 collective-permute-done.6.below_ref
  122.0 8.4 %match_edges.1 = bf16[256,4096]{1,0:T(8,128)(2,1)} custom-call(s32[1]{0:T(128)} %bitcast.start_ref, f32[3,6]{1,0:T(4,128)S(1)} %add.23.fit_ref, bf16[16,4224]{1,0:T(8,128)(2,1)S(1)} %collective-permute-done.5.above_ref, bf16[256,4224]{1,0:T(8,128)(2,1)S(1)} %get-tuple-element.12.x_ref.next_ref.top_ref.bottom_ref, ...), custom_call_target="tpu_custom_call", output_to_operand_aliasing={{}: (9, {})} | custom-call | tf_op jit(solution)/shard_map/match_edges/pallas_call | solution.py:353
  (18 shorter events, 0.1 us)
Async XLA Ops:
  0.6 1.6 %copy-start.3 = (bf16[256,4096]{1,0:T(8,128)(2,1)S(1)}, bf16[256,4096]{1,0:T(8,128)(2,1)}, u32[]{:S(2)}) copy-start(bf16[256,4096]{1,0:T(8,128)(2,1)} %x_ref.1) | copy-start | bytes 6291460
  2.2 0.7 copy-start.4
  2.9 0.7 copy-start.5
  3.5 0.7 copy-start.6
  4.2 0.7 copy-start.7
  13.7 1.5 %copy-start.2 = (bf16[320,4224]{1,0:T(8,128)(2,1)}, bf16[320,4224]{1,0:T(8,128)(2,1)S(1)}, u32[]{:S(2)}) copy-start(bf16[320,4224]{1,0:T(8,128)(2,1)S(1)} %resample.1) | copy-start | bytes 8110084
  15.2 7.1 %copy-start.9 = (f32[1,3,6]{2,0,1:T(1,128)S(1)}, f32[1,3,6]{2,0,1:T(1,128)}, u32[]{:S(2)}) copy-start(f32[1,3,6]{2,0,1:T(1,128)} %param.14) | copy-start | bytes 220
  15.2 66.8 %all-to-all-start = ((bf16[8,40,4224]{2,1,0:T(8,128)(2,1)}), bf16[8,40,4224]{2,1,0:T(8,128)(2,1)S(1)}, u32[]{:S(2)}, u32[]{:S(2)}) async-start(bf16[8,40,4224]{2,1,0:T(8,128)(2,1)} %bitcast.16), calls=%async_computation | async-start | bytes 5406720 | tf_op jit(solution)/shard_map/all_to_all | solution.py:396
  22.4 74.6 %collective-permute-start = (f32[3,6]{1,0:T(4,128)S(1)}, f32[3,6]{1,0:T(4,128)S(1)}, u32[]{:S(2)}, u32[]{:S(2)}) collective-permute-start(f32[3,6]{1,0:T(4,128)S(1)} %bitcast.20), channel_id=1, source_target_pairs={{0,1},{1,0},{2,3},{3,2},{4,5},{5,4},{6,7},{7,6},{8,9},{9,8},{10,11... | collective-permute-start | bytes 224 | tf_op jit(solution)/shard_map/ppermute | solution.py:381
  82.1 1.5 %copy-start = (bf16[8,40,4224]{2,1,0:T(8,128)(2,1)}, bf16[8,40,4224]{2,1,0:T(8,128)(2,1)S(1)}, u32[]{:S(2)}) copy-start(bf16[8,40,4224]{2,1,0:T(8,128)(2,1)S(1)} %all-to-all-done) | copy-start | bytes 8110084
  83.6 1.8 %copy-start.1 = (bf16[8,40,4224]{2,1,0:T(8,128)(2,1)S(1)}, bf16[8,40,4224]{2,1,0:T(8,128)(2,1)}, u32[]{:S(2)}) copy-start(bf16[8,40,4224]{2,1,0:T(8,128)(2,1)} %copy-done) | copy-start | bytes 8110084
  85.3 24.6 %copy-start.8 = (f32[3]{0:T(128)S(1)}, f32[3]{0:T(128)}, u32[]{:S(2)}) copy-start(f32[3]{0:T(128)} %width_ref.1) | copy-start | bytes 40
  88.7 33.3 %collective-permute-start.5 = (bf16[16,4224]{1,0:T(8,128)(2,1)}, bf16[16,4224]{1,0:T(8,128)(2,1)S(1)}, u32[]{:S(2)}, u32[]{:S(2)}) collective-permute-start(bf16[16,4224]{1,0:T(8,128)(2,1)} %get-tuple-element.11), channel_id=1, source_target_pairs={{0,1},{1,2},{2,3},{3,4},{4,5},{5,6},{6,7},{7,8},{8,9},{9,10},{10,1... | collective-permute-start | bytes 405512 | tf_op jit(solution)/shard_map/ppermute | solution.py:402
  92.2 29.8 %collective-permute-start.6 = (bf16[16,4224]{1,0:T(8,128)(2,1)}, bf16[16,4224]{1,0:T(8,128)(2,1)S(1)}, u32[]{:S(2)}, u32[]{:S(2)}) collective-permute-start(bf16[16,4224]{1,0:T(8,128)(2,1)} %get-tuple-element.13), channel_id=1, source_target_pairs={{1,0},{2,1},{3,2},{4,3},{5,4},{6,5},{7,6},{8,7},{9,8},{10,9},{11,1... | collective-permute-start | bytes 405512 | tf_op jit(solution)/shard_map/ppermute | solution.py:403
  97.0 2.5 %collective-permute-start.1 = (f32[3,6]{1,0:T(4,128)S(1)}, f32[3,6]{1,0:T(4,128)S(1)}, u32[]{:S(2)}, u32[]{:S(2)}) collective-permute-start(f32[3,6]{1,0:T(4,128)S(1)} %fusion), channel_id=1, source_target_pairs={{0,2},{1,3},{2,0},{3,1},{4,6},{5,7},{6,4},{7,5},{8,10},{9,11},{10,... | collective-permute-start | bytes 224 | tf_op jit(solution)/shard_map/ppermute | solution.py:381
  99.6 3.3 %collective-permute-start.2 = (f32[3,6]{1,0:T(4,128)S(1)}, f32[3,6]{1,0:T(4,128)S(1)}, u32[]{:S(2)}, u32[]{:S(2)}) collective-permute-start(f32[3,6]{1,0:T(4,128)S(1)} %add.20), channel_id=1, source_target_pairs={{0,4},{1,5},{2,6},{3,7},{4,0},{5,1},{6,2},{7,3},{8,12},{9,13},{10,... | collective-permute-start | bytes 224 | tf_op jit(solution)/shard_map/ppermute | solution.py:381
  102.9 3.1 %collective-permute-start.3 = (f32[3,6]{1,0:T(4,128)S(1)}, f32[3,6]{1,0:T(4,128)S(1)}, u32[]{:S(2)}, u32[]{:S(2)}) collective-permute-start(f32[3,6]{1,0:T(4,128)S(1)} %add.21), channel_id=1, source_target_pairs={{0,8},{8,0},{16,24},{24,16},{1,9},{9,1},{17,25},{25,17},{2,10},{10... | collective-permute-start | bytes 224 | tf_op jit(solution)/shard_map/ppermute | solution.py:381
  106.0 5.0 %collective-permute-start.4 = (f32[3,6]{1,0:T(4,128)S(1)}, f32[3,6]{1,0:T(4,128)S(1)}, u32[]{:S(2)}, u32[]{:S(2)}) collective-permute-start(f32[3,6]{1,0:T(4,128)S(1)} %add.22), channel_id=1, source_target_pairs={{0,16},{8,24},{16,0},{24,8},{1,17},{9,25},{17,1},{25,9},{2,18},{10... | collective-permute-start | bytes 224 | tf_op jit(solution)/shard_map/ppermute | solution.py:381

commit v2 on v1

v2 whole, which is shorter than its diff:
```python
import functools
import math

import jax
import jax.numpy as jnp
from jax import lax
from jax.experimental import pallas as pl
from jax.experimental.pallas import tpu as pltpu
from jax.sharding import PartitionSpec as P

TAPS = 31
HALF = 15
BASES = 3
NPOLY = 6
LANE = 128
SHIFT = 16
EDGE = 16
BOTH = ("det", "patch")
BF = jnp.bfloat16
F32 = jnp.float32
VMEM = 62 << 20
ROW0 = 96
STEPS1 = 4
STEPS2 = 3
CHUNK3 = 1024


def dot(a, b):
    return jnp.dot(a, b, preferred_element_type=F32)


def lanczos(position):
    def sinc(v):
        at = jnp.where(v == 0.0, 1.0, math.pi * v)
        return jnp.where(v == 0.0, 1.0, jnp.sin(at) / at)

    return sinc(position) * sinc(position / 3.0)


def resample_kernel(
    peers, cap, pairs, dest_hbm, off_hbm, wgt_hbm, shift_hbm, wgt_row_hbm, x_hbm, out_ref,
    dest_ref, off_ref, wgt_s_ref, src_ref, count_ref, shift_ref, wgt_v_ref, x_ref, xf_ref, coef_ref,
    diff_ref, sems,
):
    blocks, rows, width = xf_ref.shape
    tiles = width // LANE + 1
    step = pl.program_id(0)

    @pl.when(step == 0)
    def _():
        copies = [
            pltpu.make_async_copy(source, target, sems.at[i])
            for i, (source, target) in enumerate(
                [
                    (dest_hbm, dest_ref),
                    (off_hbm, off_ref),
                    (wgt_hbm, wgt_s_ref),
                    (shift_hbm, shift_ref),
                    (wgt_row_hbm, wgt_v_ref),
                    (x_hbm, x_ref),
                ]
            )
        ]
        for copy in copies:
            copy.start()
        diff_ref[...] = (
            lax.broadcasted_iota(jnp.int32, diff_ref.shape, 0)
            - lax.broadcasted_iota(jnp.int32, diff_ref.shape, 1)
            + (ROW0 - (LANE - SHIFT - 2))
        )
        for p in range(peers):
            count_ref[p] = 0
        for q in range(peers * cap):
            src_ref[q] = -1
        for copy in copies[:5]:
            copy.wait()
        for b in range(blocks):
            peer = dest_ref[b] // blocks % peers
            rank = count_ref[peer]
            src_ref[peer * cap + rank] = b
            count_ref[peer] = rank + 1
        tap = lax.broadcasted_iota(jnp.int32, (8, blocks), 0).astype(F32) - 2.0
        coef_ref[...] = lanczos(tap - shift_ref[...]) * wgt_v_ref[...]
        copies[5].wait()
        xf_ref[...] = x_ref[...].astype(F32).reshape(blocks, rows, width)

    lane = lax.broadcasted_iota(jnp.int32, (8, LANE), 1)
    block_lane = lax.broadcasted_iota(jnp.int32, (8, blocks), 1)
    zero = jnp.zeros((2 * rows, LANE), BF)

    for pair in range(pairs):
        xs, bands, metas = [], [], []
        for side in range(2):
            got = src_ref[(step * pairs + pair) * 2 + side]
            valid = got >= 0
            b = jnp.maximum(got, 0)
            xs.append(xf_ref[b])
            column = jnp.sum(
                jnp.where((block_lane == b) & valid, coef_ref[...], 0.0), axis=1, keepdims=True
            )
            diff = diff_ref[...] - off_ref[b]
            band = jnp.zeros(diff.shape, F32)
            for t in range(6):
                band = jnp.where(diff == t, column[t : t + 1, :], band)
            bands.append(band)
            slot = jnp.where(valid, dest_ref[b] % blocks, -1).astype(F32)
            weight = jnp.full((8, LANE), jnp.where(valid, wgt_s_ref[b], 0.0), F32)
            high = weight.astype(BF).astype(F32)
            mid = (weight - high).astype(BF).astype(F32)
            low = weight - high - mid
            metas.append(
                jnp.where(
                    lane == SHIFT,
                    slot,
                    jnp.where(
                        lane == SHIFT + 1,
                        high,
                        jnp.where(lane == SHIFT + 2, mid, jnp.where(lane == SHIFT + 3, low, 0.0)),
                    ),
                )
            )
        x16 = jnp.concatenate(xs, axis=0).astype(BF)
        padded = jnp.concatenate([zero, x16, zero], axis=1)
        windows = jnp.concatenate(
            [padded[:, LANE * t : LANE * (t + 2)] for t in range(tiles)], axis=0
        )
        band = jnp.concatenate(bands, axis=1).astype(BF)
        band = jnp.concatenate([jnp.zeros((ROW0, 2 * LANE), BF), band], axis=0)
        made = dot(windows, band)
        for t in range(tiles):
            top = made[2 * rows * t : 2 * rows * t + rows, :LANE]
            bottom = made[2 * rows * t + rows : 2 * rows * (t + 1), LANE:]
            if t == 0:
                top = jnp.where(lane < SHIFT, 0.0, top)
                bottom = jnp.where(lane < SHIFT, 0.0, bottom)
            if t == tiles - 1:
                top = jnp.where(lane < SHIFT, top, metas[0])
                bottom = jnp.where(lane < SHIFT, bottom, metas[1])
            out_ref[2 * rows * pair : 2 * rows * (pair + 1), LANE * t : LANE * (t + 1)] = (
                jnp.concatenate([top, bottom], axis=0).astype(BF)
            )


def resample(exposure, dest, offset, shift, weight, peers, cap):
    rows_dev, width = exposure.shape
    blocks = dest.shape[0]
    rows = rows_dev // blocks
    all_pairs = peers * cap // 2
    steps = STEPS1
    while all_pairs % steps:
        steps -= 1
    pairs = all_pairs // steps
    hbm = pl.BlockSpec(memory_space=pl.ANY)
    return pl.pallas_call(
        functools.partial(resample_kernel, peers, cap, pairs),
        grid=(steps,),
        in_specs=[hbm] * 6,
        out_specs=pl.BlockSpec((pairs * 2 * rows, width + LANE), lambda i: (i, 0)),
        out_shape=jax.ShapeDtypeStruct((peers * cap * rows, width + LANE), BF),
        scratch_shapes=[
            pltpu.SMEM((blocks,), jnp.int32),
            pltpu.SMEM((blocks,), jnp.int32),
            pltpu.SMEM((blocks,), F32),
            pltpu.SMEM((peers * cap,), jnp.int32),
            pltpu.SMEM((peers,), jnp.int32),
            pltpu.VMEM((1, blocks), F32),
            pltpu.VMEM((1, blocks), F32),
            pltpu.VMEM((rows_dev, width), BF),
            pltpu.VMEM((blocks, rows, width), F32),
            pltpu.VMEM((8, blocks), F32),
            pltpu.VMEM((2 * LANE - ROW0, LANE), jnp.int32),
            pltpu.SemaphoreType.DMA((6,)),
        ],
        compiler_params=pltpu.CompilerParams(vmem_limit_bytes=VMEM),
        name="resample",
    )(dest, offset, weight, shift.reshape(1, blocks), weight.reshape(1, blocks), exposure)


def gauss_band(shape, rows_axis, width, total):
    u = lax.broadcasted_iota(jnp.int32, shape, 1 - rows_axis)
    u = u - lax.broadcasted_iota(jnp.int32, shape, rows_axis) - 1
    at = (u - HALF).astype(F32)
    value = jnp.exp(-(at * at) / (2.0 * width * width)) / total
    return jnp.where((u >= 0) & (u < TAPS), value, 0.0).astype(BF)


def tables_kernel(width_ref, band_ref, inner_ref, edge_ref):
    inner, rows_dev = inner_ref.shape[1:]
    edge_ref[...] = jnp.zeros(edge_ref.shape, BF)
    for k in range(BASES):
        width = jnp.full((8, LANE), width_ref[k], F32)[:1, :1]
        tap = lax.broadcasted_iota(jnp.int32, (1, LANE), 1)
        at = (tap - HALF).astype(F32)
        each = jnp.where(tap < TAPS, jnp.exp(-(at * at) / (2.0 * width * width)), 0.0)
        total = jnp.sum(each, axis=1, keepdims=True)
        band_ref[:, LANE * k : LANE * (k + 1)] = gauss_band((2 * LANE, LANE), 1, width, total)
        inner_ref[k] = gauss_band((inner, rows_dev), 0, width, total)
        strip = gauss_band((EDGE, 3 * EDGE), 0, width, total)
        none = jnp.zeros(strip.shape, BF)
        edge_ref[2 * EDGE * k : 2 * EDGE * k + EDGE, :] = jnp.concatenate([strip, none], axis=1)
        edge_ref[2 * EDGE * k + EDGE : 2 * EDGE * (k + 1), :] = jnp.concatenate([none, strip], axis=1)


def tables(basis_width, rows_dev):
    sd = lambda *shape: jax.ShapeDtypeStruct(shape, BF)
    return pl.pallas_call(
        tables_kernel,
        in_specs=[pl.BlockSpec(memory_space=pltpu.SMEM)],
        out_shape=[
            sd(2 * LANE, BASES * LANE),
            sd(BASES, rows_dev - 2 * EDGE, rows_dev),
            sd(2 * EDGE * BASES, 6 * EDGE),
        ],
        compiler_params=pltpu.CompilerParams(vmem_limit_bytes=VMEM),
        name="tables",
    )(basis_width)


def coadd_kernel(
    rows, meta_ref, x_ref, image_ref, top_ref, bottom_ref, cover_ref, place_ref, scale_ref
):
    rows_dev, chunk = image_ref.shape
    arrived = x_ref.shape[0]
    slots = rows_dev // rows
    step = pl.program_id(0)

    @pl.when(step == 0)
    def _():
        meta = meta_ref[...]
        slot = meta[:, SHIFT : SHIFT + 1].astype(F32)
        across = jnp.broadcast_to(slot, (arrived, LANE)).T[:1].astype(jnp.int32)
        row = lax.broadcasted_iota(jnp.int32, (rows_dev, 1), 0)
        lane = lax.broadcasted_iota(jnp.int32, (1, arrived), 1)
        match = (across == row // rows) & (lane % rows == row % rows)
        place = jnp.where(match, 1.0, 0.0).astype(BF)
        place_ref[...] = place
        sums = dot(place, meta)
        cover = sums[:, SHIFT + 1 : SHIFT + 2] + sums[:, SHIFT + 2 : SHIFT + 3]
        cover = cover + sums[:, SHIFT + 3 : SHIFT + 4]
        scale_ref[...] = jnp.broadcast_to(1.0 / jnp.maximum(cover, 1.0), (rows_dev, LANE))
        source = lax.broadcasted_iota(jnp.int32, (arrived, 1), 0)
        index = lax.broadcasted_iota(jnp.int32, (1, slots), 1)
        match = (slot.astype(jnp.int32) == index) & (source % rows == 0)
        sums = lax.dot_general(
            meta, jnp.where(match, 1.0, 0.0).astype(BF), (((0,), (0,)), ((), ())),
            preferred_element_type=F32,
        )
        cover = sums[SHIFT + 1 : SHIFT + 2] + sums[SHIFT + 2 : SHIFT + 3]
        cover_ref[...] = cover + sums[SHIFT + 3 : SHIFT + 4]

    value = dot(place_ref[...], x_ref[...]) * scale_ref[:, :1]
    column = lax.broadcasted_iota(jnp.int32, (1, chunk), 1) + step * chunk
    tail = pl.num_programs(0) * chunk - LANE + SHIFT
    value = jnp.where(column < tail, value, 0.0).astype(BF)
    image_ref[...] = value
    top_ref[...] = value[:EDGE]
    bottom_ref[...] = value[rows_dev - EDGE :]


def coadd(arrived, rows_dev, rows):
    count, width = arrived.shape
    steps = STEPS2
    chunk = width // steps
    last = width // LANE - 1
    strip = pl.BlockSpec((EDGE, chunk), lambda i: (0, i))
    sd = jax.ShapeDtypeStruct
    return pl.pallas_call(
        functools.partial(coadd_kernel, rows),
        grid=(steps,),
        in_specs=[
            pl.BlockSpec((count, LANE), lambda i: (0, last)),
            pl.BlockSpec((count, chunk), lambda i: (0, i)),
        ],
        out_specs=[
            pl.BlockSpec((rows_dev, chunk), lambda i: (0, i)),
            strip,
            strip,
            pl.BlockSpec((1, rows_dev // rows), lambda i: (0, 0)),
        ],
        out_shape=[
            sd((rows_dev, width), BF),
            sd((EDGE, width), BF),
            sd((EDGE, width), BF),
            sd((1, rows_dev // rows), F32),
        ],
        scratch_shapes=[pltpu.VMEM((rows_dev, count), BF), pltpu.VMEM((rows_dev, LANE), F32)],
        compiler_params=pltpu.CompilerParams(vmem_limit_bytes=VMEM),
        name="coadd",
    )(arrived, arrived)


def row_position(base, count, all_rows):
    at = (base + lax.broadcasted_iota(jnp.int32, (count, 1), 0)).astype(F32)
    return 2.0 * at / (all_rows - 1) - 1.0


def col_position(first, count, col_count):
    at = (first + lax.broadcasted_iota(jnp.int32, (1, count), 1)).astype(F32)
    return 2.0 * at / (col_count - 1) - 1.0


def field(fit_ref, k, y, xx):
    c = lambda i: fit_ref[NPOLY * k + i]
    return (c(0) + c(2) * y + c(5) * y * y) + (c(1) + c(4) * y) * xx + c(3) * (xx * xx)


def tile_windows(value, tiles):
    return jnp.concatenate([value[:, LANE * t : LANE * (t + 2)] for t in range(tiles)], axis=0)


def inner_kernel(
    all_rows, col_count, start_ref, fit_ref, x_ref, next_ref, band_ref, inner_ref, out_ref
):
    rows_dev, chunk = out_ref.shape
    inner = rows_dev - 2 * EDGE
    tiles = chunk // LANE
    first = pl.program_id(0) * chunk
    image = jnp.concatenate([x_ref[...], next_ref[...]], axis=1)
    smooth = dot(tile_windows(image, tiles), band_ref[...]).astype(BF)
    y = row_position(start_ref[0] + EDGE, inner, all_rows)
    xx = col_position(first, chunk, col_count)
    total = None
    for k in range(BASES):
        part = jnp.concatenate(
            [smooth[rows_dev * t : rows_dev * (t + 1), LANE * k : LANE * (k + 1)] for t in range(tiles)],
            axis=1,
        )
        term = field(fit_ref, k, y, xx) * dot(inner_ref[k], part)
        total = term if total is None else total + term
    out_ref[EDGE : EDGE + inner, :] = total.astype(BF)


def match_inner(image, start, fit, band, inner, all_rows):
    rows_dev, width = image.shape
    col_count = width - LANE
    chunk = CHUNK3
    smem = pl.BlockSpec(memory_space=pltpu.SMEM)
    whole = lambda v: pl.BlockSpec(v.shape, lambda i: (0,) * v.ndim)
    return pl.pallas_call(
        functools.partial(inner_kernel, all_rows, col_count),
        grid=(col_count // chunk,),
        in_specs=[
            smem,
            smem,
            pl.BlockSpec((rows_dev, chunk), lambda i: (0, i)),
            pl.BlockSpec((rows_dev, LANE), lambda i: (0, (i + 1) * (chunk // LANE))),
            whole(band),
            whole(inner),
        ],
        out_specs=pl.BlockSpec((rows_dev, chunk), lambda i: (0, i)),
        out_shape=jax.ShapeDtypeStruct((rows_dev, col_count), BF),
        compiler_params=pltpu.CompilerParams(vmem_limit_bytes=VMEM),
        name="match_inner",
    )(start, fit, image, image, band, inner)


def edge_kernel(
    all_rows, rows_dev, start_ref, fit_ref, above_ref, top_ref, bottom_ref, below_ref, band_ref, edge_ref, old_ref, out_ref, made_ref, sems,
):
    col_count = made_ref.shape[1]
    tiles = col_count // LANE
    strips_in = (above_ref, top_ref, bottom_ref, below_ref)
    x = jnp.concatenate([ref[...] for ref in strips_in], axis=0)
    rowconv = dot(edge_ref[...], x).astype(BF)
    y = jnp.concatenate(
        [row_position(start_ref[0] + at, EDGE, all_rows) for at in (0, rows_dev - EDGE)], axis=0
    )
    both = 2 * EDGE
    parts = [
        dot(tile_windows(rowconv[both * k : both * (k + 1)], tiles), band_ref[:, LANE * k : LANE * (k + 1)])
        for k in range(BASES)
    ]
    for t in range(tiles):
        xx = col_position(LANE * t, LANE, col_count)
        total = None
        for k in range(BASES):
            term = field(fit_ref, k, y, xx) * parts[k][both * t : both * (t + 1)]
            total = term if total is None else total + term
        made_ref[:, LANE * t : LANE * (t + 1)] = total.astype(BF)
    copies = [
        pltpu.make_async_copy(
            made_ref.at[pl.ds(EDGE * i, EDGE)], out_ref.at[pl.ds(at, EDGE)], sems.at[i]
        )
        for i, at in enumerate((0, rows_dev - EDGE))
    ]
    for copy in copies:
        copy.start()
    for copy in copies:
        copy.wait()


def match_edges(matched, image, above, below, start, fit, band, edge, all_rows):
    rows_dev, col_count = matched.shape
    width = image.shape[1]
    smem = pl.BlockSpec(memory_space=pltpu.SMEM)
    hbm = pl.BlockSpec(memory_space=pl.ANY)
    block = lambda rows, cols, at: pl.BlockSpec((rows, cols), lambda i: (at, 0))
    return pl.pallas_call(
        functools.partial(edge_kernel, all_rows, rows_dev),
        grid=(1,),
        in_specs=[
            smem,
            smem,
            block(EDGE, width, 0),
            block(2 * EDGE, width, 0),
            block(2 * EDGE, width, rows_dev // (2 * EDGE) - 1),
            block(EDGE, width, 0),
            block(*band.shape, 0),
            block(*edge.shape, 0),
            hbm,
        ],
        out_specs=hbm,
        out_shape=jax.ShapeDtypeStruct(matched.shape, BF),
        scratch_shapes=[pltpu.VMEM((2 * EDGE, col_count), BF), pltpu.SemaphoreType.DMA((2,))],
        input_output_aliases={8: 0},
        compiler_params=pltpu.CompilerParams(vmem_limit_bytes=VMEM),
        name="match_edges",
    )(start, fit, above, image, image, below, band, edge, matched)


def axis_sum(value, axis):
    count = lax.axis_size(axis)
    span = 1
    while span < count:
        value = value + lax.ppermute(value, axis, [(i, i ^ span) for i in range(count)])
        span *= 2
    return value


def shards(
    exposure, block_dest, band_offset, col_shift, block_weight, basis_width, kernel_fit, fit_owner
):
    rows_dev, _ = exposure.shape
    blocks = block_dest.shape[0]
    peers = lax.axis_size("patch")
    devices = lax.axis_size(BOTH)
    cap = blocks // peers + 1
    me = lax.axis_index(BOTH)
    payload = resample(exposure, block_dest, band_offset, col_shift, block_weight, peers, cap)
    arrived = lax.all_to_all(payload, "patch", split_axis=0, concat_axis=0, tiled=True)
    fit = jnp.where(me == fit_owner[0], kernel_fit[0], 0.0).reshape(1, BASES * NPOLY)
    band, inner, edge = tables(basis_width, rows_dev)
    payload, fit = lax.optimization_barrier((payload, fit))
    fit = axis_sum(fit, "det")
    fit, band, inner, edge = lax.optimization_barrier((fit, band, inner, edge))
    fit = axis_sum(fit, "patch")
    arrived, fit = lax.optimization_barrier((arrived, fit))
    fit = fit.reshape(BASES * NPOLY)
    image, top, bottom, cover = coadd(arrived, rows_dev, rows_dev // blocks)
    down = [(i, i + 1) for i in range(devices - 1)]
    up = [(i + 1, i) for i in range(devices - 1)]
    above = lax.ppermute(bottom, BOTH, down)
    below = lax.ppermute(top, BOTH, up)
    start = jnp.full((1,), me * rows_dev, jnp.int32)
    all_rows = rows_dev * devices
    matched = match_inner(image, start, fit, band, inner, all_rows)
    matched = match_edges(matched, image, above, below, start, fit, band, edge, all_rows)
    return matched, cover.reshape(blocks)


def solution(mesh):
    in_specs = (
        P(BOTH, None),
        P(BOTH),
        P(BOTH),
        P(BOTH),
        P(BOTH),
        P(),
        P(BOTH, None, None),
        P(),
    )
    out_specs = (P(BOTH, None), P(BOTH))
    return jax.shard_map(shards, mesh=mesh, in_specs=in_specs, out_specs=out_specs, check_vma=False)
```

time: 132 us -> 101 us (0.77)
  waiting for transfers between devices: 62.8 us -> 49.4 us
  Pallas kernels: 32 us -> 23.6 us
  local copies, waits for them, and re-layouts: 9.62 us -> 1.41 us
  starting transfers between devices: 24.6 us -> 23.2 us
    all_to_all x1, waiting for transfers between devices: 58.1 us -> 0.01 us  [shards(): lax.all_to_all(payload, 'patch', split_axis=0, concat_axis=0, tiled=True)]
    ppermute x5, waiting for transfers between devices: 4.64 us -> 49.4 us  [axis_sum(): lax.ppermute(value, axis, [(i, i ^ span) for i in range(count)])]
    unnamed x22 -> x6, local copies, waits for them, and re-layouts: 9.61 us -> 1.33 us
    pallas_call x1, Pallas kernels: 10.5 us -> 7.48 us  [match_inner(): pl.pallas_call(functools.partial(inner_kernel, all_rows, col_count), grid...]
    pallas_call x3, Pallas kernels: 12.7 us -> 9.86 us  [the longest x1 5.26 us: coadd(): pl.pallas_call(functools.partial(coadd_kernel, rows), grid=(steps,), in_s...]
    pallas_call x1, Pallas kernels: 8.85 us -> 6.27 us  [resample(): pl.pallas_call(functools.partial(resample_kernel, peers, cap, pairs), gri...]
  transfers between devices with their start and end apart: 8 -> 8, of which waited for: 5 -> 4; matrix products, arithmetic and copies ran while one was open for 0% -> 1% of each run, Pallas kernels for 11% -> 9%
where the time goes in v2:
time: 101 us; the launch traced here: 99.6 us
  waiting for transfers between devices  49.4 us (49%)
  Pallas kernels  23.6 us (23%)
  starting transfers between devices  23.2 us (23%)
  local copies, waits for them, and re-layouts  1.41 us (1%)
  between operations  1.35 us (1%)
    ppermute x5, waiting for transfers between devices, axis_sum(): lax.ppermute(value, axis, [(i, i ^ span) for i in range(count)])  49.4 us
    ppermute x5, starting transfers between devices, axis_sum(): lax.ppermute(value, axis, [(i, i ^ span) for i in range(count)])  8.62 us
    pallas_call x1, Pallas kernels, match_inner(): pl.pallas_call(functools.partial(inner_kernel, all_rows, col_count), grid...  7.48 us
    all_to_all x1, starting transfers between devices, shards(): lax.all_to_all(payload, 'patch', split_axis=0, concat_axis=0, tiled=True)  6.37 us
    pallas_call x1, Pallas kernels, resample(): pl.pallas_call(functools.partial(resample_kernel, peers, cap, pairs), gri...  6.27 us
    pallas_call x1, Pallas kernels, coadd(): pl.pallas_call(functools.partial(coadd_kernel, rows), grid=(steps,), in_s...  5.26 us
    ppermute x1, starting transfers between devices, shards(): below = lax.ppermute(top, BOTH, up)  4.79 us
    ppermute x1, starting transfers between devices, shards(): above = lax.ppermute(bottom, BOTH, down)  3.45 us
  transfers between devices with their start and end apart: 8, of which 4 were waited for; matrix products, arithmetic and copies ran while one was open for 1% of the time, Pallas kernels for 9%

profile of v2, /device:TPU:1, one launch (start us, length us, event | category | flops | bytes accessed | tf_op | source)
XLA Modules:
  0.0 99.6 jit_solution(11277599889971705388)
XLA Ops:
  0.6 6.3 %resample.1 = bf16[320,4224]{1,0:T(8,128)(2,1)} custom-call(s32[32]{0:T(128)} %dest_hbm.1, s32[32]{0:T(128)} %off_hbm.1, f32[32]{0:T(128)} %wgt_hbm.1, f32[1,32]{1,0:T(1,128)} %bitcast.13, f32[1,32]{1,0:T(1,128)} %bitcast.10, bf16[256,4096]{1,0:T(8,128)(2,1)} %x_hbm.1), custom_call_target="tpu_custom_call" | custom-call | tf_op jit(solution)/shard_map/resample/pallas_call | solution.py:154
  6.9 0.0 copy-start.2
  6.9 6.4 %all-to-all-start = ((bf16[8,40,4224]{2,1,0:T(8,128)(2,1)}), bf16[8,40,4224]{2,1,0:T(8,128)(2,1)}, u32[]{:S(2)}, u32[]{:S(2)}) async-start(bf16[8,40,4224]{2,1,0:T(8,128)(2,1)} %bitcast.9), calls=%async_computation | async-start | bytes 5406720 | tf_op jit(solution)/shard_map/all_to_all | solution.py:440
  13.9 0.0 copy-done.2
  14.0 0.1 select_n.20
  14.1 1.0 collective-permute-start
  15.0 0.8 collective-permute-done
  15.8 1.2 %collective-permute-start.1 = (f32[1,18]{1,0:T(1,128)S(1)}, f32[1,18]{1,0:T(1,128)S(1)}, u32[]{:S(2)}, u32[]{:S(2)}) collective-permute-start(f32[1,18]{1,0:T(1,128)S(1)} %add.19), channel_id=1, source_target_pairs={{0,16},{8,24},{16,0},{24,8},{1,17},{9,25},{17,1},{25,9},{2,18},{10... | collective-permute-start | bytes 224 | tf_op jit(solution)/shard_map/ppermute | solution.py:425
  17.1 1.7 %tables.1 = (bf16[256,384]{1,0:T(8,128)(2,1)}, bf16[3,224,256]{2,1,0:T(8,128)(2,1)}, bf16[96,96]{1,0:T(8,128)(2,1)}) custom-call(f32[3]{0:T(128)} %width_ref.1), custom_call_target="tpu_custom_call" | custom-call | tf_op jit(solution)/shard_map/tables/pallas_call | solution.py:206
  18.7 0.0 collective-permute-done.1
  18.8 1.8 %collective-permute-start.2 = (f32[1,18]{1,0:T(1,128)S(1)}, f32[1,18]{1,0:T(1,128)S(1)}, u32[]{:S(2)}, u32[]{:S(2)}) collective-permute-start(f32[1,18]{1,0:T(1,128)S(1)} %add.20), channel_id=1, source_target_pairs={{0,1},{1,0},{2,3},{3,2},{4,5},{5,4},{6,7},{7,6},{8,9},{9,8},{10,11... | collective-permute-start | bytes 224 | tf_op jit(solution)/shard_map/ppermute | solution.py:425
  20.6 14.1 %collective-permute-done.2 = f32[1,18]{1,0:T(1,128)S(1)} collective-permute-done((f32[1,18]{1,0:T(1,128)S(1)}, f32[1,18]{1,0:T(1,128)S(1)}, u32[]{:S(2)}, u32[]{:S(2)}) %collective-permute-start.2) | collective-permute-done | bytes 104 | tf_op jit(solution)/shard_map/ppermute | solution.py:425
  34.7 1.6 %collective-permute-start.3 = (f32[1,18]{1,0:T(1,128)S(1)}, f32[1,18]{1,0:T(1,128)S(1)}, u32[]{:S(2)}, u32[]{:S(2)}) collective-permute-start(f32[1,18]{1,0:T(1,128)S(1)} %add.21), channel_id=1, source_target_pairs={{0,2},{1,3},{2,0},{3,1},{4,6},{5,7},{6,4},{7,5},{8,10},{9,11},{10,... | collective-permute-start | bytes 224 | tf_op jit(solution)/shard_map/ppermute | solution.py:425
  36.2 21.3 %collective-permute-done.3 = f32[1,18]{1,0:T(1,128)S(1)} collective-permute-done((f32[1,18]{1,0:T(1,128)S(1)}, f32[1,18]{1,0:T(1,128)S(1)}, u32[]{:S(2)}, u32[]{:S(2)}) %collective-permute-start.3) | collective-permute-done | bytes 104 | tf_op jit(solution)/shard_map/ppermute | solution.py:425
  57.5 3.0 %collective-permute-start.4 = (f32[1,18]{1,0:T(1,128)S(1)}, f32[1,18]{1,0:T(1,128)S(1)}, u32[]{:S(2)}, u32[]{:S(2)}) collective-permute-start(f32[1,18]{1,0:T(1,128)S(1)} %add.22), channel_id=1, source_target_pairs={{0,4},{1,5},{2,6},{3,7},{4,0},{5,1},{6,2},{7,3},{8,12},{9,13},{10,... | collective-permute-start | bytes 224 | tf_op jit(solution)/shard_map/ppermute | solution.py:425
  60.5 13.2 %collective-permute-done.4 = f32[1,18]{1,0:T(1,128)S(1)} collective-permute-done((f32[1,18]{1,0:T(1,128)S(1)}, f32[1,18]{1,0:T(1,128)S(1)}, u32[]{:S(2)}, u32[]{:S(2)}) %collective-permute-start.4) | collective-permute-done | bytes 104 | tf_op jit(solution)/shard_map/ppermute | solution.py:425
  73.8 0.5 add.23
  74.3 0.0 all-to-all-done
  74.3 5.3 %coadd.1 = (bf16[256,4224]{1,0:T(8,128)(2,1)}, bf16[16,4224]{1,0:T(8,128)(2,1)}, bf16[16,4224]{1,0:T(8,128)(2,1)}, f32[1,32]{1,0:T(1,128)}) custom-call(bf16[320,4224]{1,0:T(8,128)(2,1)} %bitcast.4.meta_ref.x_ref, bf16[320,4224]{1,0:T(8,128)(2,1)} %bitcast.4.meta_ref.x_ref), custom_call_target="tpu_custom_call" | custom-call | tf_op jit(solution)/shard_map/coadd/pallas_call | solution.py:267
  79.6 3.5 %collective-permute-start.5 = (bf16[16,4224]{1,0:T(8,128)(2,1)}, bf16[16,4224]{1,0:T(8,128)(2,1)S(1)}, u32[]{:S(2)}, u32[]{:S(2)}) collective-permute-start(bf16[16,4224]{1,0:T(8,128)(2,1)} %get-tuple-element.23), channel_id=1, source_target_pairs={{0,1},{1,2},{2,3},{3,4},{4,5},{5,6},{6,7},{7,8},{8,9},{9,10},{10,1... | collective-permute-start | bytes 405512 | tf_op jit(solution)/shard_map/ppermute | solution.py:452
  83.0 4.8 %collective-permute-start.6 = (bf16[16,4224]{1,0:T(8,128)(2,1)}, bf16[16,4224]{1,0:T(8,128)(2,1)S(1)}, u32[]{:S(2)}, u32[]{:S(2)}) collective-permute-start(bf16[16,4224]{1,0:T(8,128)(2,1)} %get-tuple-element.25), channel_id=1, source_target_pairs={{1,0},{2,1},{3,2},{4,3},{5,4},{6,5},{7,6},{8,7},{9,8},{10,9},{11,1... | collective-permute-start | bytes 405512 | tf_op jit(solution)/shard_map/ppermute | solution.py:453
  87.8 7.5 %match_inner.1.old_ref = bf16[256,4096]{1,0:T(8,128)(2,1)} custom-call(s32[1]{0:T(128)} %bitcast.start_ref, f32[18]{0:T(128)} %bitcast.11, bf16[256,4224]{1,0:T(8,128)(2,1)} %get-tuple-element.24.x_ref.next_ref.top_ref.bottom_ref, bf16[256,4224]{1,0:T(8,128)(2,1)} %get-tuple-element.24.x_ref.next_ref.top_ref.bottom_ref, ...), custom_call_target="tpu_custom_call" | custom-call | tf_op jit(solution)/shard_map/match_inner/pallas_call | solution.py:339
  95.3 0.0 collective-permute-done.5.above_ref
  95.3 0.0 copy-start
  95.3 0.0 collective-permute-done.6.below_ref
  95.3 0.7 copy-done
  96.0 0.0 copy-start.1
  96.0 0.7 copy-done.1
  96.6 2.9 %match_edges.1 = bf16[256,4096]{1,0:T(8,128)(2,1)} custom-call(s32[1]{0:T(128)} %bitcast.start_ref, f32[18]{0:T(128)} %bitcast.12, bf16[16,4224]{1,0:T(8,128)(2,1)} %copy-done, bf16[256,4224]{1,0:T(8,128)(2,1)} %get-tuple-element.24.x_ref.next_ref.top_ref.bottom_ref, ...), custom_call_target="tpu_custom_call", output_to_operand_aliasing={{}: (8, {})} | custom-call | tf_op jit(solution)/shard_map/match_edges/pallas_call | solution.py:398
  (5 shorter events, 0.0 us)
Async XLA Ops:
  6.9 7.0 %copy-start.2 = (f32[1,3,6]{2,0,1:T(1,128)S(1)}, f32[1,3,6]{2,0,1:T(1,128)}, u32[]{:S(2)}) copy-start(f32[1,3,6]{2,0,1:T(1,128)} %param.14) | copy-start | bytes 220
  6.9 67.4 %all-to-all-start = ((bf16[8,40,4224]{2,1,0:T(8,128)(2,1)}), bf16[8,40,4224]{2,1,0:T(8,128)(2,1)}, u32[]{:S(2)}, u32[]{:S(2)}) async-start(bf16[8,40,4224]{2,1,0:T(8,128)(2,1)} %bitcast.9), calls=%async_computation | async-start | bytes 5406720 | tf_op jit(solution)/shard_map/all_to_all | solution.py:440
  14.1 1.8 %collective-permute-start = (f32[1,18]{1,0:T(1,128)S(1)}, f32[1,18]{1,0:T(1,128)S(1)}, u32[]{:S(2)}, u32[]{:S(2)}) collective-permute-start(f32[1,18]{1,0:T(1,128)S(1)} %select_n.20), channel_id=1, source_target_pairs={{0,8},{8,0},{16,24},{24,16},{1,9},{9,1},{17,25},{25,17},{2,10},{10... | collective-permute-start | bytes 224 | tf_op jit(solution)/shard_map/ppermute | solution.py:425
  15.8 2.9 %collective-permute-start.1 = (f32[1,18]{1,0:T(1,128)S(1)}, f32[1,18]{1,0:T(1,128)S(1)}, u32[]{:S(2)}, u32[]{:S(2)}) collective-permute-start(f32[1,18]{1,0:T(1,128)S(1)} %add.19), channel_id=1, source_target_pairs={{0,16},{8,24},{16,0},{24,8},{1,17},{9,25},{17,1},{25,9},{2,18},{10... | collective-permute-start | bytes 224 | tf_op jit(solution)/shard_map/ppermute | solution.py:425
  18.8 15.9 %collective-permute-start.2 = (f32[1,18]{1,0:T(1,128)S(1)}, f32[1,18]{1,0:T(1,128)S(1)}, u32[]{:S(2)}, u32[]{:S(2)}) collective-permute-start(f32[1,18]{1,0:T(1,128)S(1)} %add.20), channel_id=1, source_target_pairs={{0,1},{1,0},{2,3},{3,2},{4,5},{5,4},{6,7},{7,6},{8,9},{9,8},{10,11... | collective-permute-start | bytes 224 | tf_op jit(solution)/shard_map/ppermute | solution.py:425
  34.7 22.8 %collective-permute-start.3 = (f32[1,18]{1,0:T(1,128)S(1)}, f32[1,18]{1,0:T(1,128)S(1)}, u32[]{:S(2)}, u32[]{:S(2)}) collective-permute-start(f32[1,18]{1,0:T(1,128)S(1)} %add.21), channel_id=1, source_target_pairs={{0,2},{1,3},{2,0},{3,1},{4,6},{5,7},{6,4},{7,5},{8,10},{9,11},{10,... | collective-permute-start | bytes 224 | tf_op jit(solution)/shard_map/ppermute | solution.py:425
  57.5 16.3 %collective-permute-start.4 = (f32[1,18]{1,0:T(1,128)S(1)}, f32[1,18]{1,0:T(1,128)S(1)}, u32[]{:S(2)}, u32[]{:S(2)}) collective-permute-start(f32[1,18]{1,0:T(1,128)S(1)} %add.22), channel_id=1, source_target_pairs={{0,4},{1,5},{2,6},{3,7},{4,0},{5,1},{6,2},{7,3},{8,12},{9,13},{10,... | collective-permute-start | bytes 224 | tf_op jit(solution)/shard_map/ppermute | solution.py:425
  79.6 15.7 %collective-permute-start.5 = (bf16[16,4224]{1,0:T(8,128)(2,1)}, bf16[16,4224]{1,0:T(8,128)(2,1)S(1)}, u32[]{:S(2)}, u32[]{:S(2)}) collective-permute-start(bf16[16,4224]{1,0:T(8,128)(2,1)} %get-tuple-element.23), channel_id=1, source_target_pairs={{0,1},{1,2},{2,3},{3,4},{4,5},{5,6},{6,7},{7,8},{8,9},{9,10},{10,1... | collective-permute-start | bytes 405512 | tf_op jit(solution)/shard_map/ppermute | solution.py:452
  83.0 12.3 %collective-permute-start.6 = (bf16[16,4224]{1,0:T(8,128)(2,1)}, bf16[16,4224]{1,0:T(8,128)(2,1)S(1)}, u32[]{:S(2)}, u32[]{:S(2)}) collective-permute-start(bf16[16,4224]{1,0:T(8,128)(2,1)} %get-tuple-element.25), channel_id=1, source_target_pairs={{1,0},{2,1},{3,2},{4,3},{5,4},{6,5},{7,6},{8,7},{9,8},{10,9},{11,1... | collective-permute-start | bytes 405512 | tf_op jit(solution)/shard_map/ppermute | solution.py:453
  95.3 0.7 copy-start
  96.0 0.7 copy-start.1

commit v3 on v2

v3 whole, which is shorter than its diff:
```python
import functools
import math

import jax
import jax.numpy as jnp
from jax import lax
from jax.experimental import pallas as pl
from jax.experimental.pallas import tpu as pltpu
from jax.sharding import PartitionSpec as P

TAPS = 31
HALF = 15
BASES = 3
NPOLY = 6
LANE = 128
SHIFT = 16
EDGE = 16
BOTH = ("det", "patch")
BF = jnp.bfloat16
F32 = jnp.float32
MIB = 1 << 20
EARLY_VMEM, LATE_VMEM = 62 * MIB, 32 * MIB
SMALL_VMEM, MATCH_VMEM = 24 * MIB, 32 * MIB
ROW0 = 96
FIT0 = 32
CHUNK2 = 1024
CHUNK3 = 1024


def dot(a, b):
    return jnp.dot(a, b, preferred_element_type=F32)


def lanczos(position):
    def sinc(v):
        at = jnp.where(v == 0.0, 1.0, math.pi * v)
        return jnp.where(v == 0.0, 1.0, jnp.sin(at) / at)

    return sinc(position) * sinc(position / 3.0)


def resample_kernel(cap, peers, order, with_fit, *refs):
    dest_hbm, off_hbm, shift_hbm, wgt_hbm, x_hbm = refs[:5]
    outs = refs[5 + with_fit : -12]
    (
        dest_ref, off_ref, src_ref, count_ref, shift_ref, wgt_ref, x_ref, xf_ref, made_ref, diff_ref,
        fit_ref, sems,
    ) = refs[-12:]
    blocks, rows, width = xf_ref.shape
    tiles = width // LANE
    me = lax.axis_index("patch")
    smalls = [(dest_hbm, dest_ref), (off_hbm, off_ref), (shift_hbm, shift_ref), (wgt_hbm, wgt_ref)]
    if with_fit:
        smalls.append((refs[5], fit_ref))
    copies = [
        pltpu.make_async_copy(source, target, sems.at[i])
        for i, (source, target) in enumerate([(x_hbm, x_ref)] + smalls)
    ]
    for copy in copies:
        copy.start()
    diff_ref[...] = (
        lax.broadcasted_iota(jnp.int32, diff_ref.shape, 0)
        - lax.broadcasted_iota(jnp.int32, diff_ref.shape, 1)
        + (ROW0 - (LANE - SHIFT - 2))
    )
    for p in range(peers):
        count_ref[p] = 0
    for q in range(peers * cap):
        src_ref[q] = -1
    for copy in copies[1:]:
        copy.wait()
    for b in range(blocks):
        group = (dest_ref[b] // blocks % peers - me + peers) % peers
        rank = count_ref[group]
        src_ref[group * cap + rank] = b
        count_ref[group] = rank + 1
    tap = lax.broadcasted_iota(jnp.int32, (8, blocks), 0).astype(F32) - 2.0
    coefs = lanczos(tap - shift_ref[...]) * wgt_ref[...]
    lane = lax.broadcasted_iota(jnp.int32, (rows, LANE), 1)
    block_lane = lax.broadcasted_iota(jnp.int32, (8, blocks), 1)
    zero = jnp.zeros((2 * rows, LANE), BF)

    def three(value):
        high = value.astype(BF).astype(F32)
        mid = (value - high).astype(BF).astype(F32)
        return high, mid, value - high - mid

    fit_note = jnp.zeros((rows, LANE), F32)
    line = lax.broadcasted_iota(jnp.int32, (rows, LANE), 0)
    if with_fit:
        for i, part in enumerate(three(jnp.broadcast_to(fit_ref[...], (rows, LANE)))):
            fit_note = jnp.where(line == i, part, fit_note)
    copies[0].wait()
    xf_ref[...] = x_ref[...].astype(F32).reshape(blocks, rows, width)

    def one_pair(slots):
        xs, bands, notes = [], [], []
        for group, rank in slots:
            got = src_ref[group * cap + rank]
            valid = got >= 0
            b = jnp.maximum(got, 0)
            xs.append(xf_ref[b])
            own = (block_lane == b) & valid
            column = jnp.sum(jnp.where(own, coefs, 0.0), axis=1, keepdims=True)
            diff = diff_ref[...] - off_ref[b]
            band = jnp.zeros(diff.shape, F32)
            for t in range(6):
                band = jnp.where(diff == t, column[t : t + 1, :], band)
            bands.append(band)
            slot = jnp.where(valid, dest_ref[b] % blocks, -1).astype(F32)
            weight = jnp.sum(jnp.where(own, wgt_ref[...], 0.0), axis=1, keepdims=True)
            note = jnp.where(lane == 0, slot, 0.0)
            for i, part in enumerate(three(jnp.broadcast_to(weight, (rows, LANE)))):
                note = jnp.where(lane == i + 1, part, note)
            notes.append(note + fit_note if rank == 0 else note)
        x16 = jnp.concatenate(xs, axis=0).astype(BF)
        padded = jnp.concatenate([zero, x16, zero], axis=1)
        windows = jnp.concatenate(
            [padded[:, LANE * t : LANE * (t + 2)] for t in range(tiles + 1)], axis=0
        )
        band = jnp.concatenate(bands, axis=1).astype(BF)
        band = jnp.concatenate([jnp.zeros((ROW0, 2 * LANE), BF), band], axis=0)
        made = dot(windows, band)

        def piece(i):
            at = made[2 * rows * i : 2 * rows * (i + 1)]
            return at[:rows, :LANE], at[rows:, LANE:]

        for t in range(tiles):
            top, bottom = piece(t)
            if t == 0:
                last = piece(tiles)
                top = jnp.where(lane < SHIFT, last[0], top)
                bottom = jnp.where(lane < SHIFT, last[1], bottom)
            put(slots, t, top, bottom)
        put(slots, tiles, notes[0], notes[1])

    def put(slots, t, top, bottom):
        cols = slice(LANE * t, LANE * (t + 1))
        (group0, rank0), (group1, rank1) = slots
        group0, group1 = order.index(group0), order.index(group1)
        if group0 == group1:
            made_ref[group0, rows * rank0 : rows * (rank0 + 2), cols] = jnp.concatenate(
                [top, bottom], axis=0
            ).astype(BF)
        else:
            made_ref[group0, rows * rank0 : rows * (rank0 + 1), cols] = top.astype(BF)
            made_ref[group1, rows * rank1 : rows * (rank1 + 1), cols] = bottom.astype(BF)

    sends = [pltpu.make_async_copy(made_ref.at[i], outs[i], sems.at[6 + i]) for i in range(len(order))]
    for at in range(0, len(order), 2):
        two = order[at : at + 2]
        for group in two:
            for rank in range(0, cap - 1, 2):
                one_pair([(group, rank), (group, rank + 1)])
        if cap % 2:
            one_pair([(two[0], cap - 1), (two[1], cap - 1)])
        for i in range(2):
            sends[at + i].start()
    for send in sends:
        send.wait()


def resample(exposure, dest, offset, shift, weight, fit, peers, cap, order):
    rows_dev, width = exposure.shape
    blocks = dest.shape[0]
    rows = rows_dev // blocks
    hbm = pl.BlockSpec(memory_space=pl.ANY)
    return pl.pallas_call(
        functools.partial(resample_kernel, cap, peers, order, len(fit)),
        in_specs=[hbm] * (5 + len(fit)),
        out_specs=[hbm] * len(order),
        out_shape=[jax.ShapeDtypeStruct((cap * rows, width + LANE), BF)] * len(order),
        scratch_shapes=[
            pltpu.SMEM((blocks,), jnp.int32),
            pltpu.SMEM((blocks,), jnp.int32),
            pltpu.SMEM((peers * cap,), jnp.int32),
            pltpu.SMEM((peers,), jnp.int32),
            pltpu.VMEM((1, blocks), F32),
            pltpu.VMEM((1, blocks), F32),
            pltpu.VMEM((rows_dev, width), BF),
            pltpu.VMEM((blocks, rows, width), F32),
            pltpu.VMEM((len(order), cap * rows, width + LANE), BF),
            pltpu.VMEM((2 * LANE - ROW0, LANE), jnp.int32),
            pltpu.VMEM((1, LANE), F32),
            pltpu.SemaphoreType.DMA((6 + len(order),)),
        ],
        compiler_params=pltpu.CompilerParams(vmem_limit_bytes=LATE_VMEM if fit else EARLY_VMEM),
        name="resample",
    )(dest, offset, shift.reshape(1, blocks), weight.reshape(1, blocks), exposure, *fit)


def gauss_band(shape, rows_axis, width, total):
    u = lax.broadcasted_iota(jnp.int32, shape, 1 - rows_axis)
    u = u - lax.broadcasted_iota(jnp.int32, shape, rows_axis) - 1
    at = (u - HALF).astype(F32)
    value = jnp.exp(-(at * at) / (2.0 * width * width)) / total
    return jnp.where((u >= 0) & (u < TAPS), value, 0.0).astype(BF)


def tables_kernel(width_ref, band_ref, inner_ref, edge_ref):
    inner, rows_dev = inner_ref.shape[1:]
    edge_ref[...] = jnp.zeros(edge_ref.shape, BF)
    for k in range(BASES):
        width = jnp.full((8, LANE), width_ref[k], F32)[:1, :1]
        tap = lax.broadcasted_iota(jnp.int32, (1, LANE), 1)
        at = (tap - HALF).astype(F32)
        each = jnp.where(tap < TAPS, jnp.exp(-(at * at) / (2.0 * width * width)), 0.0)
        total = jnp.sum(each, axis=1, keepdims=True)
        band_ref[:, LANE * k : LANE * (k + 1)] = gauss_band((2 * LANE, LANE), 1, width, total)
        inner_ref[k] = gauss_band((inner, rows_dev), 0, width, total)
        strip = gauss_band((EDGE, 3 * EDGE), 0, width, total)
        none = jnp.zeros(strip.shape, BF)
        edge_ref[2 * EDGE * k : 2 * EDGE * k + EDGE, :] = jnp.concatenate([strip, none], axis=1)
        edge_ref[2 * EDGE * k + EDGE : 2 * EDGE * (k + 1), :] = jnp.concatenate([none, strip], axis=1)


def tables(basis_width, rows_dev):
    sd = lambda *shape: jax.ShapeDtypeStruct(shape, BF)
    return pl.pallas_call(
        tables_kernel,
        in_specs=[pl.BlockSpec(memory_space=pltpu.SMEM)],
        out_shape=[
            sd(2 * LANE, BASES * LANE),
            sd(BASES, rows_dev - 2 * EDGE, rows_dev),
            sd(2 * EDGE * BASES, 6 * EDGE),
        ],
        compiler_params=pltpu.CompilerParams(vmem_limit_bytes=SMALL_VMEM),
        name="tables",
    )(basis_width)


def split_rows(groups, rows):
    even = groups[0].shape[0] // (2 * rows) * (2 * rows)
    parts = [jnp.concatenate([g[:even] for g in groups], axis=0)]
    if even < groups[0].shape[0]:
        parts.append(jnp.concatenate([g[even:].astype(F32) for g in groups], axis=0).astype(BF))
    return parts


def plan_slots(notes, rows, rows_dev):
    slots = rows_dev // rows
    fit = sum(sum(g[i : i + 1].astype(F32) for i in range(3)) for g in notes[::2])
    places, column, lined = [], None, None
    for part in split_rows(notes, rows):
        count = part.shape[0]
        slot = part[:, :1].astype(F32)
        across = jnp.broadcast_to(slot, (count, LANE)).T[:1].astype(jnp.int32)
        row = lax.broadcasted_iota(jnp.int32, (rows_dev, 1), 0)
        lane = lax.broadcasted_iota(jnp.int32, (1, count), 1)
        match = (across == row // rows) & (lane % rows == row % rows)
        place = jnp.where(match, 1.0, 0.0).astype(BF)
        sums = dot(place, part)
        column = sums if column is None else column + sums
        places.append(place)
        source = lax.broadcasted_iota(jnp.int32, (count, 1), 0)
        index = lax.broadcasted_iota(jnp.int32, (1, slots), 1)
        match = (slot.astype(jnp.int32) == index) & (source % rows == 0)
        sums = lax.dot_general(
            part, jnp.where(match, 1.0, 0.0).astype(BF), (((0,), (0,)), ((), ())),
            preferred_element_type=F32,
        )
        lined = sums if lined is None else lined + sums
    cover = column[:, 1:2] + column[:, 2:3] + column[:, 3:4]
    scale = jnp.broadcast_to(1.0 / jnp.maximum(cover, 1.0), (rows_dev, LANE))
    return places, scale, lined[1:2] + lined[2:3] + lined[3:4], fit


def coadd_kernel(peers, rows, chunk, *refs):
    groups, (image_hbm, top_ref, bottom_ref, cover_ref, fit_ref) = refs[:peers], refs[peers : peers + 5]
    x_ref, image_ref, sems = refs[peers + 5 :]
    rows_dev, width = image_ref.shape
    parts = [slice(width, width + LANE)] + [slice(i, i + chunk) for i in range(0, width, chunk)]
    copies = [
        [
            pltpu.make_async_copy(groups[g].at[:, cols], x_ref.at[g, :, cols], sems.at[i, g])
            for g in range(peers)
        ]
        for i, cols in enumerate(parts)
    ]
    for part in copies:
        for copy in part:
            copy.start()

    def arrived(i):
        for copy in copies[i]:
            copy.wait()
        return [x_ref[g, :, parts[i]] for g in range(peers)]

    places, scale, cover, fit = plan_slots(arrived(0), rows, rows_dev)
    cover_ref[...] = cover
    fit_ref[...] = fit
    sends = []
    for i, cols in enumerate(parts[1:]):
        value = None
        for part, place in zip(split_rows(arrived(i + 1), rows), places):
            sums = dot(place, part)
            value = sums if value is None else value + sums
        value = (value * scale[:, :1]).astype(BF)
        image_ref[:, cols] = value
        top_ref[:, cols] = value[:EDGE]
        bottom_ref[:, cols] = value[rows_dev - EDGE :]
        send = pltpu.make_async_copy(image_ref.at[:, cols], image_hbm.at[:, cols], sems.at[i + 1, peers])
        send.start()
        sends.append(send)
    for send in sends:
        send.wait()


def coadd(groups, rows_dev, rows):
    peers = len(groups)
    count, cols = groups[0].shape
    width = cols - LANE
    chunk = CHUNK2
    sd = jax.ShapeDtypeStruct
    hbm = pl.BlockSpec(memory_space=pl.ANY)
    vmem = pl.BlockSpec(memory_space=pltpu.VMEM)
    return pl.pallas_call(
        functools.partial(coadd_kernel, peers, rows, chunk),
        in_specs=[hbm] * peers,
        out_specs=[hbm] + [vmem] * 4,
        out_shape=[
            sd((rows_dev, width), BF),
            sd((EDGE, width), BF),
            sd((EDGE, width), BF),
            sd((1, rows_dev // rows), F32),
            sd((1, LANE), F32),
        ],
        scratch_shapes=[
            pltpu.VMEM((peers, count, cols), BF),
            pltpu.VMEM((rows_dev, width), BF),
            pltpu.SemaphoreType.DMA((1 + width // chunk, peers + 1)),
        ],
        compiler_params=pltpu.CompilerParams(vmem_limit_bytes=SMALL_VMEM),
        name="coadd",
    )(*groups)


def row_position(base, count, all_rows):
    at = (base + lax.broadcasted_iota(jnp.int32, (count, 1), 0)).astype(F32)
    return 2.0 * at / (all_rows - 1) - 1.0


def col_position(first, count, col_count):
    at = (first + lax.broadcasted_iota(jnp.int32, (1, count), 1)).astype(F32)
    return 2.0 * at / (col_count - 1) - 1.0


def field(fit_ref, k, y, xx):
    c = lambda i: fit_ref[0, FIT0 + NPOLY * k + i]
    return (c(0) + c(2) * y + c(5) * y * y) + (c(1) + c(4) * y) * xx + c(3) * (xx * xx)


def lane_of(value):
    return lax.broadcasted_iota(jnp.int32, (1, value.shape[1]), 1)


def blank(value, keep):
    return jnp.where(keep, value, jnp.zeros_like(value))


def tile_windows(value, tiles):
    return jnp.concatenate([value[:, LANE * t : LANE * (t + 2)] for t in range(tiles)], axis=0)


def inner_rows(image, first, start, fit_ref, band_ref, inner_ref, all_rows, col_count):
    rows_dev, width = image.shape
    inner = rows_dev - 2 * EDGE
    tiles = width // LANE - 1
    smooth = dot(tile_windows(image, tiles), band_ref[...]).astype(BF)
    y = row_position(start + EDGE, inner, all_rows)
    xx = col_position(first, LANE * tiles, col_count)
    total = None
    for k in range(BASES):
        part = jnp.concatenate(
            [smooth[rows_dev * t : rows_dev * (t + 1), LANE * k : LANE * (k + 1)] for t in range(tiles)],
            axis=1,
        )
        term = field(fit_ref, k, y, xx) * dot(inner_ref[k], part)
        total = term if total is None else total + term
    return total.astype(BF)


def inner_kernel(
    all_rows, col_count, start_ref, fit_ref, x_ref, next_ref, band_ref, inner_ref, out_ref
):
    rows_dev, chunk = out_ref.shape
    first = pl.program_id(0) * chunk
    x = x_ref[...]
    head = blank(x[:, :LANE], (lane_of(x[:, :LANE]) >= SHIFT) | (first > 0))
    tail = next_ref[...]
    tail = blank(tail, (lane_of(tail) < SHIFT) | (first + chunk < col_count))
    image = jnp.concatenate([head, x[:, LANE:], tail], axis=1)
    out_ref[EDGE : rows_dev - EDGE, :] = inner_rows(
        image, first, start_ref[0], fit_ref, band_ref, inner_ref, all_rows, col_count
    )


def whole_of(v):
    return pl.BlockSpec(v.shape, lambda i: (0,) * v.ndim)


def match_inner(image, start, fit, band, inner, all_rows):
    rows_dev, col_count = image.shape
    chunk = CHUNK3
    smem = pl.BlockSpec(memory_space=pltpu.SMEM)
    steps = col_count // chunk
    return pl.pallas_call(
        functools.partial(inner_kernel, all_rows, col_count),
        grid=(steps,),
        in_specs=[
            smem,
            smem,
            pl.BlockSpec((rows_dev, chunk), lambda i: (0, i)),
            pl.BlockSpec((rows_dev, LANE), lambda i: (0, (i + 1) % steps * (chunk // LANE))),
            whole_of(band),
            whole_of(inner),
        ],
        out_specs=pl.BlockSpec((rows_dev, chunk), lambda i: (0, i)),
        out_shape=jax.ShapeDtypeStruct((rows_dev, col_count), BF),
        compiler_params=pltpu.CompilerParams(vmem_limit_bytes=MATCH_VMEM),
        name="match_inner",
    )(start, fit, image, image, band, inner)


def edge_kernel(
    all_rows, rows_dev, start_ref, fit_ref, above_ref, top_ref, bottom_ref, below_ref, band_ref,
    edge_ref, old_ref, out_ref, made_ref, sems,
):
    col_count = made_ref.shape[1]
    tiles = col_count // LANE
    x = jnp.concatenate([ref[...] for ref in (above_ref, top_ref, bottom_ref, below_ref)], axis=0)
    rowconv = dot(edge_ref[...], x).astype(BF)
    head = rowconv[:, :LANE]
    rowconv = jnp.concatenate(
        [blank(head, lane_of(head) >= SHIFT), rowconv[:, LANE:], blank(head, lane_of(head) < SHIFT)],
        axis=1,
    )
    y = jnp.concatenate(
        [row_position(start_ref[0] + at, EDGE, all_rows) for at in (0, rows_dev - EDGE)], axis=0
    )
    both = 2 * EDGE
    parts = [
        dot(tile_windows(rowconv[both * k : both * (k + 1)], tiles), band_ref[:, LANE * k : LANE * (k + 1)])
        for k in range(BASES)
    ]
    for t in range(tiles):
        xx = col_position(LANE * t, LANE, col_count)
        total = None
        for k in range(BASES):
            term = field(fit_ref, k, y, xx) * parts[k][both * t : both * (t + 1)]
            total = term if total is None else total + term
        made_ref[:, LANE * t : LANE * (t + 1)] = total.astype(BF)
    copies = [
        pltpu.make_async_copy(
            made_ref.at[pl.ds(EDGE * i, EDGE)], out_ref.at[pl.ds(at, EDGE)], sems.at[i]
        )
        for i, at in enumerate((0, rows_dev - EDGE))
    ]
    for copy in copies:
        copy.start()
    for copy in copies:
        copy.wait()


def match_edges(matched, image, above, below, start, fit, band, edge, all_rows):
    rows_dev, col_count = matched.shape
    smem = pl.BlockSpec(memory_space=pltpu.SMEM)
    hbm = pl.BlockSpec(memory_space=pl.ANY)
    strip = lambda at: pl.BlockSpec((2 * EDGE, col_count), lambda i: (at, 0))
    return pl.pallas_call(
        functools.partial(edge_kernel, all_rows, rows_dev),
        grid=(1,),
        in_specs=[
            smem,
            smem,
            whole_of(above),
            strip(0),
            strip(rows_dev // (2 * EDGE) - 1),
            whole_of(below),
            whole_of(band),
            whole_of(edge),
            hbm,
        ],
        out_specs=hbm,
        out_shape=jax.ShapeDtypeStruct(matched.shape, BF),
        scratch_shapes=[pltpu.VMEM((2 * EDGE, col_count), BF), pltpu.SemaphoreType.DMA((2,))],
        input_output_aliases={8: 0},
        compiler_params=pltpu.CompilerParams(vmem_limit_bytes=SMALL_VMEM),
        name="match_edges",
    )(start, fit, above, image, image, below, band, edge, matched)


def shards(
    exposure, block_dest, band_offset, col_shift, block_weight, basis_width, kernel_fit, fit_owner
):
    rows_dev, _ = exposure.shape
    blocks = block_dest.shape[0]
    peers = lax.axis_size("patch")
    dets = lax.axis_size("det")
    devices = lax.axis_size(BOTH)
    cap = blocks // peers + 1
    me = lax.axis_index(BOTH)
    all_rows = rows_dev * devices
    start = jnp.full((1,), me * rows_dev, jnp.int32)
    send = lambda group, s: lax.ppermute(
        group, "patch", [(i, (i + s) % peers) for i in range(peers)]
    )
    order = sorted(range(peers), key=lambda s: (s % 2 == 0, -min(s, peers - s)))
    early_order = order[:2]
    late_order = sorted(order[2:], key=lambda s: -min(s, peers - s))
    partner_fit = lax.ppermute(kernel_fit, "patch", [(i, i ^ 1) for i in range(peers)])
    source = (exposure, block_dest, band_offset, col_shift, block_weight)
    early = resample(*source, [], peers, cap, early_order)
    groups = {s: send(group, s) for s, group in zip(early_order, early)}
    source, early, fit, partner_fit = lax.optimization_barrier(
        (source, early, kernel_fit, partner_fit)
    )
    owner = fit_owner[0]
    partner = me ^ 1
    fit = jnp.where(me == owner, fit, 0.0) + jnp.where(partner == owner, partner_fit, 0.0)
    fit = fit.reshape(1, BASES * NPOLY)
    span = 1
    while span < dets:
        fit = fit + lax.ppermute(fit, "det", [(i, i ^ span) for i in range(dets)])
        span *= 2
    fit = jnp.pad(fit, ((0, 0), (0, LANE - BASES * NPOLY)))
    fit = jnp.roll(fit, FIT0, axis=1)
    late = resample(*source, [fit], peers, cap, late_order)
    for s, group in zip(late_order, late):
        groups[s] = send(group, s) if s else group
    late, basis_width = lax.optimization_barrier((late, basis_width))
    band, inner, edge = tables(basis_width, rows_dev)
    groups = [groups[s] for s in range(peers)]
    groups, band, inner, edge = lax.optimization_barrier((groups, band, inner, edge))
    image, top, bottom, cover, fit = coadd(groups, rows_dev, rows_dev // blocks)
    down = [(i, i + 1) for i in range(devices - 1)]
    up = [(i + 1, i) for i in range(devices - 1)]
    above = lax.ppermute(bottom, BOTH, down)
    below = lax.ppermute(top, BOTH, up)
    matched = match_inner(image, start, fit, band, inner, all_rows)
    matched = match_edges(matched, image, above, below, start, fit, band, edge, all_rows)
    return matched, cover.reshape(blocks)


def solution(mesh):
    in_specs = (
        P(BOTH, None),
        P(BOTH),
        P(BOTH),
        P(BOTH),
        P(BOTH),
        P(),
        P(BOTH, None, None),
        P(),
    )
    out_specs = (P(BOTH, None), P(BOTH))
    return jax.shard_map(shards, mesh=mesh, in_specs=in_specs, out_specs=out_specs, check_vma=False)
```

time: 101 us -> 88.8 us (0.88); the launches traced: 99.6 us -> 88.6 us
  waiting for transfers between devices: 49.4 us -> 23.4 us
  starting transfers between devices: 23.2 us -> 39.4 us
    ppermute x5 -> x10, waiting for transfers between devices: 49.4 us -> 23.4 us  [the longest x7 20.4 us: shards(): lax.ppermute(group, 'patch', [(i, (i + s) % peers) for i in range(peers)])]
    ppermute x5 -> x10, starting transfers between devices: 8.62 us -> 20.1 us  [the longest x7 15 us: shards(): lax.ppermute(group, 'patch', [(i, (i + s) % peers) for i in range(peers)])]
    ppermute x1, starting transfers between devices: 4.79 us -> 12.6 us  [shards(): below = lax.ppermute(top, BOTH, up)]
    all_to_all x1 -> x0, starting transfers between devices: 6.37 us -> none  [shards(): lax.all_to_all(payload, 'patch', split_axis=0, concat_axis=0, tiled=True)]
    ppermute x1, starting transfers between devices: 3.45 us -> 6.66 us  [shards(): above = lax.ppermute(bottom, BOTH, down)]
    pallas_call x2 -> x3, Pallas kernels: 11.5 us -> 12.7 us  [the longest x2 8.62 us: resample(): pl.pallas_call(functools.partial(resample_kernel, cap, peers, order, len(...]
  transfers between devices with their start and end apart: 8 -> 12, of which waited for: 4 -> 6; matrix products, arithmetic and copies ran while one was open for 1% -> 0% of each run, Pallas kernels for 9% -> 14%
where the time goes in v3:
time: 88.8 us; the launch traced here: 88.6 us
  starting transfers between devices  39.4 us (44%)
  waiting for transfers between devices  23.4 us (26%)
  Pallas kernels  22.7 us (26%)
  local copies, waits for them, and re-layouts  1.78 us (2%)
  between operations  1.41 us (2%)
    ppermute x7, waiting for transfers between devices, shards(): lax.ppermute(group, 'patch', [(i, (i + s) % peers) for i in range(peers)])  20.4 us
    ppermute x7, starting transfers between devices, shards(): lax.ppermute(group, 'patch', [(i, (i + s) % peers) for i in range(peers)])  15 us
    ppermute x1, starting transfers between devices, shards(): below = lax.ppermute(top, BOTH, up)  12.6 us
    pallas_call x2, Pallas kernels, resample(): pl.pallas_call(functools.partial(resample_kernel, cap, peers, order, len(...  8.62 us
    pallas_call x1, Pallas kernels, match_inner(): pl.pallas_call(functools.partial(inner_kernel, all_rows, col_count), grid...  6.88 us
    ppermute x1, starting transfers between devices, shards(): above = lax.ppermute(bottom, BOTH, down)  6.66 us
    pallas_call x1, Pallas kernels, coadd(): pl.pallas_call(functools.partial(coadd_kernel, peers, rows, chunk), in_sp...  4.1 us
    ppermute x2, starting transfers between devices, shards(): fit = fit + lax.ppermute(fit, 'det', [(i, i ^ span) for i in range(dets)])  2.99 us
  transfers between devices with their start and end apart: 12, of which 6 were waited for; matrix products, arithmetic and copies ran while one was open for 0% of the time, Pallas kernels for 14%

profile of v3, /device:TPU:1, one launch (start us, length us, event | category | flops | bytes accessed | tf_op | source)
XLA Modules:
  0.0 88.6 jit_solution(1519045138695720192)
XLA Ops:
  0.7 3.8 %resample.2 = (bf16[40,4224]{1,0:T(8,128)(2,1)}, bf16[40,4224]{1,0:T(8,128)(2,1)}) custom-call(s32[32]{0:T(128)} %refs_0_.2, s32[32]{0:T(128)} %refs_1_.2, f32[1,32]{1,0:T(1,128)} %bitcast.9, f32[1,32]{1,0:T(1,128)} %bitcast.11, bf16[256,4096]{1,0:T(8,128)(2,1)} %refs_4_.2), custom_call_target="tpu_custom_call" | custom-call | tf_op jit(solution)/shard_map/resample/pallas_call | solution.py:169
  4.5 3.1 %collective-permute-start.5 = (bf16[40,4224]{1,0:T(8,128)(2,1)}, bf16[40,4224]{1,0:T(8,128)(2,1)S(1)}, u32[]{:S(2)}, u32[]{:S(2)}) collective-permute-start(bf16[40,4224]{1,0:T(8,128)(2,1)} %get-tuple-element.37), channel_id=1, source_target_pairs={{0,3},{1,4},{2,5},{3,6},{4,7},{5,0},{6,1},{7,2},{8,11},{9,12},{10,... | collective-permute-start | bytes 1013768 | tf_op jit(solution)/shard_map/ppermute | solution.py:506
  7.6 1.1 %collective-permute-start.7 = (bf16[40,4224]{1,0:T(8,128)(2,1)}, bf16[40,4224]{1,0:T(8,128)(2,1)S(1)}, u32[]{:S(2)}, u32[]{:S(2)}) collective-permute-start(bf16[40,4224]{1,0:T(8,128)(2,1)} %get-tuple-element.38), channel_id=1, source_target_pairs={{0,5},{1,6},{2,7},{3,0},{4,1},{5,2},{6,3},{7,4},{8,13},{9,14},{10,... | collective-permute-start | bytes 1013768 | tf_op jit(solution)/shard_map/ppermute | solution.py:506
  8.6 2.1 %collective-permute-start = (f32[1,3,6]{2,0,1:T(1,128)S(1)}, f32[1,3,6]{2,0,1:T(1,128)S(1)}, u32[]{:S(2)}, u32[]{:S(2)}) collective-permute-start(f32[1,3,6]{2,0,1:T(1,128)S(1)} %copy-done.6), channel_id=1, source_target_pairs={{0,1},{1,0},{2,3},{3,2},{4,5},{5,4},{6,7},{7,6},{8,9},{9,8},{10,11... | collective-permute-start | bytes 224 | tf_op jit(solution)/shard_map/ppermute | solution.py:512
  11.4 0.8 collective-permute-done
  12.2 0.1 reshape.26
  12.2 1.7 %collective-permute-start.1 = (f32[1,18]{1,0:T(1,128)S(1)}, f32[1,18]{1,0:T(1,128)S(1)}, u32[]{:S(2)}, u32[]{:S(2)}) collective-permute-start(f32[1,18]{1,0:T(1,128)S(1)} %reshape.26), channel_id=1, source_target_pairs={{0,8},{8,0},{16,24},{24,16},{1,9},{9,1},{17,25},{25,17},{2,10},{10... | collective-permute-start | bytes 224 | tf_op jit(solution)/shard_map/ppermute | solution.py:525
  14.0 0.8 collective-permute-done.1
  14.8 1.2 %collective-permute-start.2 = (f32[1,18]{1,0:T(1,128)S(1)}, f32[1,18]{1,0:T(1,128)S(1)}, u32[]{:S(2)}, u32[]{:S(2)}) collective-permute-start(f32[1,18]{1,0:T(1,128)S(1)} %add.18), channel_id=1, source_target_pairs={{0,16},{8,24},{16,0},{24,8},{1,17},{9,25},{17,1},{25,9},{2,18},{10... | collective-permute-start | bytes 224 | tf_op jit(solution)/shard_map/ppermute | solution.py:525
  16.1 1.4 %collective-permute-done.2 = f32[1,18]{1,0:T(1,128)S(1)} collective-permute-done((f32[1,18]{1,0:T(1,128)S(1)}, f32[1,18]{1,0:T(1,128)S(1)}, u32[]{:S(2)}, u32[]{:S(2)}) %collective-permute-start.2) | collective-permute-done | bytes 104 | tf_op jit(solution)/shard_map/ppermute | solution.py:525
  17.5 0.1 concatenate.4.refs_5_
  17.6 0.0 copy-start
  17.6 1.6 %copy-done = bf16[256,4096]{1,0:T(8,128)(2,1)S(1)} copy-done((bf16[256,4096]{1,0:T(8,128)(2,1)S(1)}, bf16[256,4096]{1,0:T(8,128)(2,1)}, u32[]{:S(2)}) %copy-start) | copy-done | bytes 2097176
  19.2 4.9 %resample.3 = (bf16[40,4224]{1,0:T(8,128)(2,1)S(1)}, bf16[40,4224]{1,0:T(8,128)(2,1)S(1)}, bf16[40,4224]{1,0:T(8,128)(2,1)S(1)}, bf16[40,4224]{1,0:T(8,128)(2,1)...) custom-call(s32[32]{0:T(128)S(1)} %copy-done.1, s32[32]{0:T(128)S(1)} %copy-done.2, ...), custom_call_target="tpu_custom_call" | custom-call | tf_op jit(solution)/shard_map/resample/pallas_call | solution.py:169
  24.1 1.8 %collective-permute-start.3 = (bf16[40,4224]{1,0:T(8,128)(2,1)S(1)}, bf16[40,4224]{1,0:T(8,128)(2,1)S(1)}, u32[]{:S(2)}, u32[]{:S(2)}) collective-permute-start(bf16[40,4224]{1,0:T(8,128)(2,1)S(1)} %get-tuple-element.47), channel_id=1, source_target_pairs={{0,1},{1,2},{2,3},{3,4},{4,5},{5,6},{6,7},{7,0},{8,9},{9,10},{10,1... | collective-permute-start | bytes 1013768 | tf_op jit(solution)/shard_map/ppermute | solution.py:506
  25.9 0.0 collective-permute-start.4
  25.9 1.8 %collective-permute-start.6 = (bf16[40,4224]{1,0:T(8,128)(2,1)S(1)}, bf16[40,4224]{1,0:T(8,128)(2,1)S(1)}, u32[]{:S(2)}, u32[]{:S(2)}) collective-permute-start(bf16[40,4224]{1,0:T(8,128)(2,1)S(1)} %get-tuple-element.49), channel_id=1, source_target_pairs={{0,4},{1,5},{2,6},{3,7},{4,0},{5,1},{6,2},{7,3},{8,12},{9,13},{10,... | collective-permute-start | bytes 1013768 | tf_op jit(solution)/shard_map/ppermute | solution.py:506
  27.7 0.0 collective-permute-done.5.refs_3_
  27.7 7.3 %collective-permute-start.8 = (bf16[40,4224]{1,0:T(8,128)(2,1)S(1)}, bf16[40,4224]{1,0:T(8,128)(2,1)S(1)}, u32[]{:S(2)}, u32[]{:S(2)}) collective-permute-start(bf16[40,4224]{1,0:T(8,128)(2,1)S(1)} %get-tuple-element.50), channel_id=1, source_target_pairs={{0,6},{1,7},{2,0},{3,1},{4,2},{5,3},{6,4},{7,5},{8,14},{9,15},{10,... | collective-permute-start | bytes 1013768 | tf_op jit(solution)/shard_map/ppermute | solution.py:506
  34.9 0.0 collective-permute-start.9
  34.9 0.8 tables.1
  35.8 0.8 collective-permute-done.3.refs_1_
  36.6 0.0 collective-permute-done.4.refs_2_
  36.6 17.8 %collective-permute-done.6.refs_4_ = bf16[40,4224]{1,0:T(8,128)(2,1)S(1)} collective-permute-done((bf16[40,4224]{1,0:T(8,128)(2,1)S(1)}, bf16[40,4224]{1,0:T(8,128)(2,1)S(1)}, u32[]{:S(2)}, u32[]{:S(2)}) %collective-permute-start.6) | collective-permute-done | bytes 337952 | tf_op jit(solution)/shard_map/ppermute | solution.py:506
  54.4 1.7 %collective-permute-done.9.refs_7_ = bf16[40,4224]{1,0:T(8,128)(2,1)S(1)} collective-permute-done((bf16[40,4224]{1,0:T(8,128)(2,1)S(1)}, bf16[40,4224]{1,0:T(8,128)(2,1)S(1)}, u32[]{:S(2)}, u32[]{:S(2)}) %collective-permute-start.9) | collective-permute-done | bytes 337952 | tf_op jit(solution)/shard_map/ppermute | solution.py:506
  56.1 4.1 %coadd.1 = (bf16[256,4096]{1,0:T(8,128)(2,1)S(1)}, bf16[16,4096]{1,0:T(8,128)(2,1)S(1)}, bf16[16,4096]{1,0:T(8,128)(2,1)}, f32[1,32]{1,0:T(1,128)}, f32[1,128]{1,0:T(1,128)S(1)}) custom-call(bf16[40,4224]{1,0:T(8,128)(2,1)S(1)} %get-tuple-element.56.refs_0_, bf16[40,4224]{1,0:T(8,128)(2,1)S(1)} %collective-permute-done.3.refs_1_, ...), custom_call_target="tpu_custom_call" | custom-call | tf_op jit(solution)/shard_map/coadd/pallas_call | solution.py:318
  60.2 6.7 %collective-permute-start.10 = (bf16[16,4096]{1,0:T(8,128)(2,1)}, bf16[16,4096]{1,0:T(8,128)(2,1)S(1)}, u32[]{:S(2)}, u32[]{:S(2)}) collective-permute-start(bf16[16,4096]{1,0:T(8,128)(2,1)} %get-tuple-element.65), channel_id=1, source_target_pairs={{0,1},{1,2},{2,3},{3,4},{4,5},{5,6},{6,7},{7,8},{8,9},{9,10},{10,1... | collective-permute-start | bytes 393224 | tf_op jit(solution)/shard_map/ppermute | solution.py:539
  66.9 12.6 %collective-permute-start.11 = (bf16[16,4096]{1,0:T(8,128)(2,1)S(1)}, bf16[16,4096]{1,0:T(8,128)(2,1)S(1)}, u32[]{:S(2)}, u32[]{:S(2)}) collective-permute-start(bf16[16,4096]{1,0:T(8,128)(2,1)S(1)} %get-tuple-element.67), channel_id=1, source_target_pairs={{1,0},{2,1},{3,2},{4,3},{5,4},{6,5},{7,6},{8,7},{9,8},{10,9},{11,1... | collective-permute-start | bytes 393224 | tf_op jit(solution)/shard_map/ppermute | solution.py:540
  79.5 6.9 %match_inner.1.old_ref = bf16[256,4096]{1,0:T(8,128)(2,1)} custom-call(s32[1]{0:T(128)} %bitcast.start_ref, f32[1,128]{1,0:T(1,128)S(1)} %get-tuple-element.64.fit_ref, bf16[256,4096]{1,0:T(8,128)(2,1)S(1)} %get-tuple-element.66.x_ref.next_ref.top_ref.bottom_ref, bf16[256,4096]{1,0:T(8,128)(2,1)S(1)} %get-tuple-element.66.x_ref.next_ref.top_ref.bottom_ref, ...), custom_call_target="tpu_custom_call" | custom-call | tf_op jit(solution)/shard_map/match_inner/pallas_call | solution.py:408
  86.4 0.0 collective-permute-done.10.above_ref
  86.4 0.0 collective-permute-done.11.below_ref
  86.4 2.3 %match_edges.1 = bf16[256,4096]{1,0:T(8,128)(2,1)} custom-call(s32[1]{0:T(128)} %bitcast.start_ref, f32[1,128]{1,0:T(1,128)S(1)} %get-tuple-element.64.fit_ref, bf16[16,4096]{1,0:T(8,128)(2,1)S(1)} %collective-permute-done.10.above_ref, bf16[256,4096]{1,0:T(8,128)(2,1)S(1)} %get-tuple-element.66.x_ref.next_ref.top_ref.bottom_ref, ...), custom_call_target="tpu_custom_call", output_to_operand_aliasing={{}: (8, {})} | custom-call | tf_op jit(solution)/shard_map/match_edges/pallas_call | solution.py:471
  (18 shorter events, 0.1 us)
Async XLA Ops:
  0.6 17.0 %copy-start.2 = (s32[32]{0:T(128)S(1)}, s32[32]{0:T(128)}, u32[]{:S(2)}) copy-start(s32[32]{0:T(128)} %refs_1_.2) | copy-start | bytes 388
  0.6 16.9 %copy-start.1 = (s32[32]{0:T(128)S(1)}, s32[32]{0:T(128)}, u32[]{:S(2)}) copy-start(s32[32]{0:T(128)} %refs_0_.2) | copy-start | bytes 388
  0.7 16.9 %copy-start.3 = (f32[32]{0:T(128)S(1)}, f32[32]{0:T(128)}, u32[]{:S(2)}) copy-start(f32[32]{0:T(128)} %param.11) | copy-start | bytes 388
  0.7 16.9 %copy-start.4 = (f32[32]{0:T(128)S(1)}, f32[32]{0:T(128)}, u32[]{:S(2)}) copy-start(f32[32]{0:T(128)} %param.12) | copy-start | bytes 388
  0.7 8.0 %copy-start.6 = (f32[1,3,6]{2,0,1:T(1,128)S(1)}, f32[1,3,6]{2,0,1:T(1,128)}, u32[]{:S(2)}) copy-start(f32[1,3,6]{2,0,1:T(1,128)} %param.14) | copy-start | bytes 220
  0.7 34.3 %copy-start.5 = (f32[3]{0:T(128)S(1)}, f32[3]{0:T(128)}, u32[]{:S(2)}) copy-start(f32[3]{0:T(128)} %width_ref) | copy-start | bytes 40
  4.5 23.2 %collective-permute-start.5 = (bf16[40,4224]{1,0:T(8,128)(2,1)}, bf16[40,4224]{1,0:T(8,128)(2,1)S(1)}, u32[]{:S(2)}, u32[]{:S(2)}) collective-permute-start(bf16[40,4224]{1,0:T(8,128)(2,1)} %get-tuple-element.37), channel_id=1, source_target_pairs={{0,3},{1,4},{2,5},{3,6},{4,7},{5,0},{6,1},{7,2},{8,11},{9,12},{10,... | collective-permute-start | bytes 1013768 | tf_op jit(solution)/shard_map/ppermute | solution.py:506
  7.6 27.4 %collective-permute-start.7 = (bf16[40,4224]{1,0:T(8,128)(2,1)}, bf16[40,4224]{1,0:T(8,128)(2,1)S(1)}, u32[]{:S(2)}, u32[]{:S(2)}) collective-permute-start(bf16[40,4224]{1,0:T(8,128)(2,1)} %get-tuple-element.38), channel_id=1, source_target_pairs={{0,5},{1,6},{2,7},{3,0},{4,1},{5,2},{6,3},{7,4},{8,13},{9,14},{10,... | collective-permute-start | bytes 1013768 | tf_op jit(solution)/shard_map/ppermute | solution.py:506
  8.6 3.5 %collective-permute-start = (f32[1,3,6]{2,0,1:T(1,128)S(1)}, f32[1,3,6]{2,0,1:T(1,128)S(1)}, u32[]{:S(2)}, u32[]{:S(2)}) collective-permute-start(f32[1,3,6]{2,0,1:T(1,128)S(1)} %copy-done.6), channel_id=1, source_target_pairs={{0,1},{1,0},{2,3},{3,2},{4,5},{5,4},{6,7},{7,6},{8,9},{9,8},{10,11... | collective-permute-start | bytes 224 | tf_op jit(solution)/shard_map/ppermute | solution.py:512
  12.2 2.6 %collective-permute-start.1 = (f32[1,18]{1,0:T(1,128)S(1)}, f32[1,18]{1,0:T(1,128)S(1)}, u32[]{:S(2)}, u32[]{:S(2)}) collective-permute-start(f32[1,18]{1,0:T(1,128)S(1)} %reshape.26), channel_id=1, source_target_pairs={{0,8},{8,0},{16,24},{24,16},{1,9},{9,1},{17,25},{25,17},{2,10},{10... | collective-permute-start | bytes 224 | tf_op jit(solution)/shard_map/ppermute | solution.py:525
  14.8 2.7 %collective-permute-start.2 = (f32[1,18]{1,0:T(1,128)S(1)}, f32[1,18]{1,0:T(1,128)S(1)}, u32[]{:S(2)}, u32[]{:S(2)}) collective-permute-start(f32[1,18]{1,0:T(1,128)S(1)} %add.18), channel_id=1, source_target_pairs={{0,16},{8,24},{16,0},{24,8},{1,17},{9,25},{17,1},{25,9},{2,18},{10... | collective-permute-start | bytes 224 | tf_op jit(solution)/shard_map/ppermute | solution.py:525
  17.6 1.6 %copy-start = (bf16[256,4096]{1,0:T(8,128)(2,1)S(1)}, bf16[256,4096]{1,0:T(8,128)(2,1)}, u32[]{:S(2)}) copy-start(bf16[256,4096]{1,0:T(8,128)(2,1)} %refs_4_.2) | copy-start | bytes 6291460
  24.1 12.5 %collective-permute-start.3 = (bf16[40,4224]{1,0:T(8,128)(2,1)S(1)}, bf16[40,4224]{1,0:T(8,128)(2,1)S(1)}, u32[]{:S(2)}, u32[]{:S(2)}) collective-permute-start(bf16[40,4224]{1,0:T(8,128)(2,1)S(1)} %get-tuple-element.47), channel_id=1, source_target_pairs={{0,1},{1,2},{2,3},{3,4},{4,5},{5,6},{6,7},{7,0},{8,9},{9,10},{10,1... | collective-permute-start | bytes 1013768 | tf_op jit(solution)/shard_map/ppermute | solution.py:506
  25.9 10.7 %collective-permute-start.4 = (bf16[40,4224]{1,0:T(8,128)(2,1)S(1)}, bf16[40,4224]{1,0:T(8,128)(2,1)S(1)}, u32[]{:S(2)}, u32[]{:S(2)}) collective-permute-start(bf16[40,4224]{1,0:T(8,128)(2,1)S(1)} %get-tuple-element.48), channel_id=1, source_target_pairs={{0,2},{1,3},{2,4},{3,5},{4,6},{5,7},{6,0},{7,1},{8,10},{9,11},{10,... | collective-permute-start | bytes 1013768 | tf_op jit(solution)/shard_map/ppermute | solution.py:506
  25.9 28.5 %collective-permute-start.6 = (bf16[40,4224]{1,0:T(8,128)(2,1)S(1)}, bf16[40,4224]{1,0:T(8,128)(2,1)S(1)}, u32[]{:S(2)}, u32[]{:S(2)}) collective-permute-start(bf16[40,4224]{1,0:T(8,128)(2,1)S(1)} %get-tuple-element.49), channel_id=1, source_target_pairs={{0,4},{1,5},{2,6},{3,7},{4,0},{5,1},{6,2},{7,3},{8,12},{9,13},{10,... | collective-permute-start | bytes 1013768 | tf_op jit(solution)/shard_map/ppermute | solution.py:506
  27.7 26.7 %collective-permute-start.8 = (bf16[40,4224]{1,0:T(8,128)(2,1)S(1)}, bf16[40,4224]{1,0:T(8,128)(2,1)S(1)}, u32[]{:S(2)}, u32[]{:S(2)}) collective-permute-start(bf16[40,4224]{1,0:T(8,128)(2,1)S(1)} %get-tuple-element.50), channel_id=1, source_target_pairs={{0,6},{1,7},{2,0},{3,1},{4,2},{5,3},{6,4},{7,5},{8,14},{9,15},{10,... | collective-permute-start | bytes 1013768 | tf_op jit(solution)/shard_map/ppermute | solution.py:506
  34.9 21.2 %collective-permute-start.9 = (bf16[40,4224]{1,0:T(8,128)(2,1)S(1)}, bf16[40,4224]{1,0:T(8,128)(2,1)S(1)}, u32[]{:S(2)}, u32[]{:S(2)}) collective-permute-start(bf16[40,4224]{1,0:T(8,128)(2,1)S(1)} %get-tuple-element.51), channel_id=1, source_target_pairs={{0,7},{1,0},{2,1},{3,2},{4,3},{5,4},{6,5},{7,6},{8,15},{9,8},{10,9... | collective-permute-start | bytes 1013768 | tf_op jit(solution)/shard_map/ppermute | solution.py:506
  60.2 26.1 %collective-permute-start.10 = (bf16[16,4096]{1,0:T(8,128)(2,1)}, bf16[16,4096]{1,0:T(8,128)(2,1)S(1)}, u32[]{:S(2)}, u32[]{:S(2)}) collective-permute-start(bf16[16,4096]{1,0:T(8,128)(2,1)} %get-tuple-element.65), channel_id=1, source_target_pairs={{0,1},{1,2},{2,3},{3,4},{4,5},{5,6},{6,7},{7,8},{8,9},{9,10},{10,1... | collective-permute-start | bytes 393224 | tf_op jit(solution)/shard_map/ppermute | solution.py:539
  66.9 19.5 %collective-permute-start.11 = (bf16[16,4096]{1,0:T(8,128)(2,1)S(1)}, bf16[16,4096]{1,0:T(8,128)(2,1)S(1)}, u32[]{:S(2)}, u32[]{:S(2)}) collective-permute-start(bf16[16,4096]{1,0:T(8,128)(2,1)S(1)} %get-tuple-element.67), channel_id=1, source_target_pairs={{1,0},{2,1},{3,2},{4,3},{5,4},{6,5},{7,6},{8,7},{9,8},{10,9},{11,1... | collective-permute-start | bytes 393224 | tf_op jit(solution)/shard_map/ppermute | solution.py:540

commit v4 on v3

--- a/solution.py
+++ b/solution.py
@@ -41,12 +41,12 @@
 
 def resample_kernel(cap, peers, order, with_fit, *refs):
     dest_hbm, off_hbm, shift_hbm, wgt_hbm, x_hbm = refs[:5]
-    outs = refs[5 + with_fit : -12]
+    outs = refs[5 + with_fit : -11]
     (
-        dest_ref, off_ref, src_ref, count_ref, shift_ref, wgt_ref, x_ref, xf_ref, made_ref, diff_ref,
+        dest_ref, off_ref, src_ref, count_ref, shift_ref, wgt_ref, x_ref, made_ref, diff_ref,
         fit_ref, sems,
-    ) = refs[-12:]
-    blocks, rows, width = xf_ref.shape
+    ) = refs[-11:]
+    blocks, rows, width = x_ref.shape
     tiles = width // LANE
     me = lax.axis_index("patch")
     smalls = [(dest_hbm, dest_ref), (off_hbm, off_ref), (shift_hbm, shift_ref), (wgt_hbm, wgt_ref)]
@@ -70,7 +70,7 @@
     for copy in copies[1:]:
         copy.wait()
     for b in range(blocks):
-        group = (dest_ref[b] // blocks % peers - me + peers) % peers
+        group = (dest_ref[b] // blocks % peers) ^ me
         rank = count_ref[group]
         src_ref[group * cap + rank] = b
         count_ref[group] = rank + 1
@@ -91,7 +91,6 @@
         for i, part in enumerate(three(jnp.broadcast_to(fit_ref[...], (rows, LANE)))):
             fit_note = jnp.where(line == i, part, fit_note)
     copies[0].wait()
-    xf_ref[...] = x_ref[...].astype(F32).reshape(blocks, rows, width)
 
     def one_pair(slots):
         xs, bands, notes = [], [], []
@@ -99,7 +98,7 @@
             got = src_ref[group * cap + rank]
             valid = got >= 0
             b = jnp.maximum(got, 0)
-            xs.append(xf_ref[b])
+            xs.append(x_ref[b].astype(F32))
             own = (block_lane == b) & valid
             column = jnp.sum(jnp.where(own, coefs, 0.0), axis=1, keepdims=True)
             diff = diff_ref[...] - off_ref[b]
@@ -178,8 +177,7 @@
             pltpu.SMEM((peers,), jnp.int32),
             pltpu.VMEM((1, blocks), F32),
             pltpu.VMEM((1, blocks), F32),
-            pltpu.VMEM((rows_dev, width), BF),
-            pltpu.VMEM((blocks, rows, width), F32),
+            pltpu.VMEM((blocks, rows, width), BF),
             pltpu.VMEM((len(order), cap * rows, width + LANE), BF),
             pltpu.VMEM((2 * LANE - ROW0, LANE), jnp.int32),
             pltpu.VMEM((1, LANE), F32),
@@ -187,7 +185,7 @@
         ],
         compiler_params=pltpu.CompilerParams(vmem_limit_bytes=LATE_VMEM if fit else EARLY_VMEM),
         name="resample",
-    )(dest, offset, shift.reshape(1, blocks), weight.reshape(1, blocks), exposure, *fit)
+    )(dest, offset, shift.reshape(1, blocks), weight.reshape(1, blocks), exposure.reshape(blocks, rows, width), *fit)
 
 
 def gauss_band(shape, rows_axis, width, total):
@@ -267,8 +265,9 @@
 
 
 def coadd_kernel(peers, rows, chunk, *refs):
-    groups, (image_hbm, top_ref, bottom_ref, cover_ref, fit_ref) = refs[:peers], refs[peers : peers + 5]
+    groups, (image_hbm, inward_ref, outward_ref, cover_ref, fit_ref) = refs[:peers], refs[peers : peers + 5]
     x_ref, image_ref, sems = refs[peers + 5 :]
+    odd = lax.axis_index(BOTH) % 2 == 1
     rows_dev, width = image_ref.shape
     parts = [slice(width, width + LANE)] + [slice(i, i + chunk) for i in range(0, width, chunk)]
     copies = [
@@ -298,8 +297,9 @@
             value = sums if value is None else value + sums
         value = (value * scale[:, :1]).astype(BF)
         image_ref[:, cols] = value
-        top_ref[:, cols] = value[:EDGE]
-        bottom_ref[:, cols] = value[rows_dev - EDGE :]
+        top, bottom = value[:EDGE], value[rows_dev - EDGE :]
+        inward_ref[:, cols] = jnp.where(odd, top, bottom)
+        outward_ref[:, cols] = jnp.where(odd, bottom, top)
         send = pltpu.make_async_copy(image_ref.at[:, cols], image_hbm.at[:, cols], sems.at[i + 1, peers])
         send.start()
         sends.append(send)
@@ -424,12 +424,15 @@
 
 
 def edge_kernel(
-    all_rows, rows_dev, start_ref, fit_ref, above_ref, top_ref, bottom_ref, below_ref, band_ref,
+    all_rows, rows_dev, start_ref, fit_ref, inward_ref, top_ref, bottom_ref, outward_ref, band_ref,
     edge_ref, old_ref, out_ref, made_ref, sems,
 ):
     col_count = made_ref.shape[1]
     tiles = col_count // LANE
-    x = jnp.concatenate([ref[...] for ref in (above_ref, top_ref, bottom_ref, below_ref)], axis=0)
+    odd = lax.axis_index(BOTH) % 2 == 1
+    inward, outward = inward_ref[...], outward_ref[...]
+    above, below = jnp.where(odd, inward, outward), jnp.where(odd, outward, inward)
+    x = jnp.concatenate([above, top_ref[...], bottom_ref[...], below], axis=0)
     rowconv = dot(edge_ref[...], x).astype(BF)
     head = rowconv[:, :LANE]
     rowconv = jnp.concatenate(
@@ -463,7 +466,7 @@
         copy.wait()
 
 
-def match_edges(matched, image, above, below, start, fit, band, edge, all_rows):
+def match_edges(matched, image, halos, start, fit, band, edge, all_rows):
     rows_dev, col_count = matched.shape
     smem = pl.BlockSpec(memory_space=pltpu.SMEM)
     hbm = pl.BlockSpec(memory_space=pl.ANY)
@@ -474,10 +477,10 @@
         in_specs=[
             smem,
             smem,
-            whole_of(above),
+            whole_of(halos[0]),
             strip(0),
             strip(rows_dev // (2 * EDGE) - 1),
-            whole_of(below),
+            whole_of(halos[1]),
             whole_of(band),
             whole_of(edge),
             hbm,
@@ -488,7 +491,7 @@
         input_output_aliases={8: 0},
         compiler_params=pltpu.CompilerParams(vmem_limit_bytes=SMALL_VMEM),
         name="match_edges",
-    )(start, fit, above, image, image, below, band, edge, matched)
+    )(start, fit, halos[0], image, image, halos[1], band, edge, matched)
 
 
 def shards(
@@ -504,11 +507,11 @@
     all_rows = rows_dev * devices
     start = jnp.full((1,), me * rows_dev, jnp.int32)
     send = lambda group, s: lax.ppermute(
-        group, "patch", [(i, (i + s) % peers) for i in range(peers)]
-    )
-    order = sorted(range(peers), key=lambda s: (s % 2 == 0, -min(s, peers - s)))
+        group, "patch", [(i, i ^ s) for i in range(peers)]
+    )
+    order = sorted(range(peers), key=lambda s: (s % 2 == 0, -s))
     early_order = order[:2]
-    late_order = sorted(order[2:], key=lambda s: -min(s, peers - s))
+    late_order = sorted(order[2:], key=lambda s: -s)
     partner_fit = lax.ppermute(kernel_fit, "patch", [(i, i ^ 1) for i in range(peers)])
     source = (exposure, block_dest, band_offset, col_shift, block_weight)
     early = resample(*source, [], peers, cap, early_order)
@@ -533,13 +536,12 @@
     band, inner, edge = tables(basis_width, rows_dev)
     groups = [groups[s] for s in range(peers)]
     groups, band, inner, edge = lax.optimization_barrier((groups, band, inner, edge))
-    image, top, bottom, cover, fit = coadd(groups, rows_dev, rows_dev // blocks)
-    down = [(i, i + 1) for i in range(devices - 1)]
-    up = [(i + 1, i) for i in range(devices - 1)]
-    above = lax.ppermute(bottom, BOTH, down)
-    below = lax.ppermute(top, BOTH, up)
+    image, inward, outward, cover, fit = coadd(groups, rows_dev, rows_dev // blocks)
+    even = [(i, i ^ 1) for i in range(devices)]
+    odd = [(i, j) for j in range(2, devices, 2) for i, j in ((j, j - 1), (j - 1, j))]
+    halos = (lax.ppermute(inward, BOTH, even), lax.ppermute(outward, BOTH, odd))
     matched = match_inner(image, start, fit, band, inner, all_rows)
-    matched = match_edges(matched, image, above, below, start, fit, band, edge, all_rows)
+    matched = match_edges(matched, image, halos, start, fit, band, edge, all_rows)
     return matched, cover.reshape(blocks)
 
 

time: 88.8 us -> 83.3 us (0.938)
  starting transfers between devices: 39.4 us -> 26.4 us
  waiting for transfers between devices: 23.4 us -> 31.5 us
    ppermute x9, starting transfers between devices: 34.3 us -> 23.1 us  [the longest x7 15.2 us: shards(): lax.ppermute(group, 'patch', [(i, i ^ s) for i in range(peers)])]
    ppermute x9, waiting for transfers between devices: 20.4 us -> 27.3 us  [the longest x7 27.3 us: shards(): lax.ppermute(group, 'patch', [(i, i ^ s) for i in range(peers)])]
    ppermute x1, starting transfers between devices: 2.07 us -> 0.34 us  [shards(): lax.ppermute(kernel_fit, 'patch', [(i, i ^ 1) for i in range(peers)])]
    ppermute x1, waiting for transfers between devices: 0.76 us -> 1.88 us  [shards(): lax.ppermute(kernel_fit, 'patch', [(i, i ^ 1) for i in range(peers)])]
  transfers between devices with their start and end apart: 12 -> 12, of which waited for: 6 -> 6; matrix products, arithmetic and copies ran while one was open for 0% -> 0% of each run, Pallas kernels for 14% -> 15%
where the time goes in v4:
time: 83.3 us; the launch traced here: 83.1 us
  waiting for transfers between devices  31.5 us (38%)
  starting transfers between devices  26.4 us (32%)
  Pallas kernels  22 us (26%)
  local copies, waits for them, and re-layouts  1.78 us (2%)
  between operations  1.41 us (2%)
    ppermute x7, waiting for transfers between devices, shards(): lax.ppermute(group, 'patch', [(i, i ^ s) for i in range(peers)])  27.3 us
    ppermute x7, starting transfers between devices, shards(): lax.ppermute(group, 'patch', [(i, i ^ s) for i in range(peers)])  15.2 us
    pallas_call x2, Pallas kernels, resample(): pl.pallas_call(functools.partial(resample_kernel, cap, peers, order, len(...  7.92 us
    ppermute x2, starting transfers between devices, shards(): halos = (lax.ppermute(inward, BOTH, even), lax.ppermute(outward, BOTH, odd))  7.87 us
    pallas_call x1, Pallas kernels, match_inner(): pl.pallas_call(functools.partial(inner_kernel, all_rows, col_count), grid...  6.88 us
    pallas_call x1, Pallas kernels, coadd(): pl.pallas_call(functools.partial(coadd_kernel, peers, rows, chunk), in_sp...  4.13 us
    ppermute x2, starting transfers between devices, shards(): fit = fit + lax.ppermute(fit, 'det', [(i, i ^ span) for i in range(dets)])  3 us
    ppermute x2, waiting for transfers between devices, shards(): fit = fit + lax.ppermute(fit, 'det', [(i, i ^ span) for i in range(dets)])  2.26 us
  transfers between devices with their start and end apart: 12, of which 6 were waited for; matrix products, arithmetic and copies ran while one was open for 0% of the time, Pallas kernels for 15%

profile of v4, /device:TPU:1, one launch (start us, length us, event | category | flops | bytes accessed | tf_op | source)
XLA Modules:
  0.0 83.1 jit_solution(4267277575804232230)
XLA Ops:
  0.7 3.4 %resample.2 = (bf16[40,4224]{1,0:T(8,128)(2,1)}, bf16[40,4224]{1,0:T(8,128)(2,1)}) custom-call(s32[32]{0:T(128)} %refs_0_.2, s32[32]{0:T(128)} %refs_1_.2, f32[1,32]{1,0:T(1,128)} %bitcast.13, f32[1,32]{1,0:T(1,128)} %bitcast.15, bf16[32,8,4096]{2,1,0:T(8,128)(2,1)} %bitcast.11), custom_call_target="tpu_custom_call" | custom-call | tf_op jit(solution)/shard_map/resample/pallas_call | solution.py:168
  4.1 5.1 %collective-permute-start.9 = (bf16[40,4224]{1,0:T(8,128)(2,1)}, bf16[40,4224]{1,0:T(8,128)(2,1)S(1)}, u32[]{:S(2)}, u32[]{:S(2)}) collective-permute-start(bf16[40,4224]{1,0:T(8,128)(2,1)} %get-tuple-element.37), channel_id=1, source_target_pairs={{0,7},{1,6},{2,5},{3,4},{4,3},{5,2},{6,1},{7,0},{8,15},{9,14},{10,... | collective-permute-start | bytes 1013768 | tf_op jit(solution)/shard_map/ppermute | solution.py:509
  9.3 0.3 collective-permute-start
  10.3 1.9 %collective-permute-done = f32[1,3,6]{2,0,1:T(1,128)S(1)} collective-permute-done((f32[1,3,6]{2,0,1:T(1,128)S(1)}, f32[1,3,6]{2,0,1:T(1,128)S(1)}, u32[]{:S(2)}, u32[]{:S(2)}) %collective-permute-start) | collective-permute-done | bytes 104 | tf_op jit(solution)/shard_map/ppermute | solution.py:515
  12.2 0.1 reshape.34
  12.2 1.8 %collective-permute-start.1 = (f32[1,18]{1,0:T(1,128)S(1)}, f32[1,18]{1,0:T(1,128)S(1)}, u32[]{:S(2)}, u32[]{:S(2)}) collective-permute-start(f32[1,18]{1,0:T(1,128)S(1)} %reshape.34), channel_id=1, source_target_pairs={{0,8},{8,0},{16,24},{24,16},{1,9},{9,1},{17,25},{25,17},{2,10},{10... | collective-permute-start | bytes 224 | tf_op jit(solution)/shard_map/ppermute | solution.py:528
  14.0 0.8 collective-permute-done.1
  14.8 1.2 %collective-permute-start.2 = (f32[1,18]{1,0:T(1,128)S(1)}, f32[1,18]{1,0:T(1,128)S(1)}, u32[]{:S(2)}, u32[]{:S(2)}) collective-permute-start(f32[1,18]{1,0:T(1,128)S(1)} %add.18), channel_id=1, source_target_pairs={{0,16},{8,24},{16,0},{24,8},{1,17},{9,25},{17,1},{25,9},{2,18},{10... | collective-permute-start | bytes 224 | tf_op jit(solution)/shard_map/ppermute | solution.py:528
  16.1 1.4 %collective-permute-done.2 = f32[1,18]{1,0:T(1,128)S(1)} collective-permute-done((f32[1,18]{1,0:T(1,128)S(1)}, f32[1,18]{1,0:T(1,128)S(1)}, u32[]{:S(2)}, u32[]{:S(2)}) %collective-permute-start.2) | collective-permute-done | bytes 104 | tf_op jit(solution)/shard_map/ppermute | solution.py:528
  17.5 0.1 concatenate.4.refs_5_
  17.6 0.0 copy-start
  17.6 1.6 %copy-done = bf16[256,4096]{1,0:T(8,128)(2,1)S(1)} copy-done((bf16[256,4096]{1,0:T(8,128)(2,1)S(1)}, bf16[256,4096]{1,0:T(8,128)(2,1)}, u32[]{:S(2)}) %copy-start) | copy-done | bytes 2097176
  19.2 4.5 %resample.3 = (bf16[40,4224]{1,0:T(8,128)(2,1)S(1)}, bf16[40,4224]{1,0:T(8,128)(2,1)S(1)}, bf16[40,4224]{1,0:T(8,128)(2,1)S(1)}, bf16[40,4224]{1,0:T(8,128)(2,1)...) custom-call(s32[32]{0:T(128)S(1)} %copy-done.1, s32[32]{0:T(128)S(1)} %copy-done.2, ...), custom_call_target="tpu_custom_call" | custom-call | tf_op jit(solution)/shard_map/resample/pallas_call | solution.py:168
  23.7 0.7 collective-permute-start.3
  24.4 0.7 collective-permute-start.4
  25.1 1.4 %collective-permute-start.5 = (bf16[40,4224]{1,0:T(8,128)(2,1)S(1)}, bf16[40,4224]{1,0:T(8,128)(2,1)S(1)}, u32[]{:S(2)}, u32[]{:S(2)}) collective-permute-start(bf16[40,4224]{1,0:T(8,128)(2,1)S(1)} %get-tuple-element.49), channel_id=1, source_target_pairs={{0,3},{1,2},{2,1},{3,0},{4,7},{5,6},{6,5},{7,4},{8,11},{9,10},{10,... | collective-permute-start | bytes 1013768 | tf_op jit(solution)/shard_map/ppermute | solution.py:509
  26.4 0.0 collective-permute-done.9.refs_7_
  26.4 5.3 %collective-permute-start.6 = (bf16[40,4224]{1,0:T(8,128)(2,1)S(1)}, bf16[40,4224]{1,0:T(8,128)(2,1)S(1)}, u32[]{:S(2)}, u32[]{:S(2)}) collective-permute-start(bf16[40,4224]{1,0:T(8,128)(2,1)S(1)} %get-tuple-element.50), channel_id=1, source_target_pairs={{0,4},{1,5},{2,6},{3,7},{4,0},{5,1},{6,2},{7,3},{8,12},{9,13},{10,... | collective-permute-start | bytes 1013768 | tf_op jit(solution)/shard_map/ppermute | solution.py:509
  31.7 6.1 %collective-permute-done.7.refs_5_ = bf16[40,4224]{1,0:T(8,128)(2,1)S(1)} collective-permute-done((bf16[40,4224]{1,0:T(8,128)(2,1)}, bf16[40,4224]{1,0:T(8,128)(2,1)S(1)}, u32[]{:S(2)}, u32[]{:S(2)}) %collective-permute-start.7) | collective-permute-done | bytes 337952 | tf_op jit(solution)/shard_map/ppermute | solution.py:509
  37.9 2.0 %collective-permute-start.8 = (bf16[40,4224]{1,0:T(8,128)(2,1)S(1)}, bf16[40,4224]{1,0:T(8,128)(2,1)S(1)}, u32[]{:S(2)}, u32[]{:S(2)}) collective-permute-start(bf16[40,4224]{1,0:T(8,128)(2,1)S(1)} %get-tuple-element.51), channel_id=1, source_target_pairs={{0,6},{1,7},{2,4},{3,5},{4,2},{5,3},{6,0},{7,1},{8,14},{9,15},{10,... | collective-permute-start | bytes 1013768 | tf_op jit(solution)/shard_map/ppermute | solution.py:509
  39.9 0.8 tables.1
  40.8 0.0 collective-permute-done.3.refs_1_
  40.8 3.1 %collective-permute-done.4.refs_2_ = bf16[40,4224]{1,0:T(8,128)(2,1)S(1)} collective-permute-done((bf16[40,4224]{1,0:T(8,128)(2,1)S(1)}, bf16[40,4224]{1,0:T(8,128)(2,1)S(1)}, u32[]{:S(2)}, u32[]{:S(2)}) %collective-permute-start.4) | collective-permute-done | bytes 337952 | tf_op jit(solution)/shard_map/ppermute | solution.py:509
  43.9 18.1 %collective-permute-done.5.refs_3_ = bf16[40,4224]{1,0:T(8,128)(2,1)S(1)} collective-permute-done((bf16[40,4224]{1,0:T(8,128)(2,1)S(1)}, bf16[40,4224]{1,0:T(8,128)(2,1)S(1)}, u32[]{:S(2)}, u32[]{:S(2)}) %collective-permute-start.5) | collective-permute-done | bytes 337952 | tf_op jit(solution)/shard_map/ppermute | solution.py:509
  61.9 0.0 collective-permute-done.6.refs_4_
  61.9 0.0 collective-permute-done.8.refs_6_
  61.9 4.1 %coadd.1 = (bf16[256,4096]{1,0:T(8,128)(2,1)S(1)}, bf16[16,4096]{1,0:T(8,128)(2,1)}, bf16[16,4096]{1,0:T(8,128)(2,1)S(1)}, f32[1,32]{1,0:T(1,128)}, f32[1,128]{1,0:T(1,128)S(1)}) custom-call(bf16[40,4224]{1,0:T(8,128)(2,1)S(1)} %get-tuple-element.56.refs_0_, bf16[40,4224]{1,0:T(8,128)(2,1)S(1)} %collective-permute-done.3.refs_1_, ...), custom_call_target="tpu_custom_call" | custom-call | tf_op jit(solution)/shard_map/coadd/pallas_call | solution.py:318
  66.1 0.4 collective-permute-start.10
  66.5 7.5 %collective-permute-start.11 = (bf16[16,4096]{1,0:T(8,128)(2,1)S(1)}, bf16[16,4096]{1,0:T(8,128)(2,1)S(1)}, u32[]{:S(2)}, u32[]{:S(2)}) collective-permute-start(bf16[16,4096]{1,0:T(8,128)(2,1)S(1)} %get-tuple-element.67), channel_id=1, source_target_pairs={{2,1},{1,2},{4,3},{3,4},{6,5},{5,6},{8,7},{7,8},{10,9},{9,10},{12,... | collective-permute-start | bytes 393224 | tf_op jit(solution)/shard_map/ppermute | solution.py:542
  74.0 6.9 %match_inner.1.old_ref = bf16[256,4096]{1,0:T(8,128)(2,1)} custom-call(s32[1]{0:T(128)} %bitcast.start_ref, f32[1,128]{1,0:T(1,128)S(1)} %get-tuple-element.64.fit_ref, bf16[256,4096]{1,0:T(8,128)(2,1)S(1)} %get-tuple-element.66.x_ref.next_ref.top_ref.bottom_ref, bf16[256,4096]{1,0:T(8,128)(2,1)S(1)} %get-tuple-element.66.x_ref.next_ref.top_ref.bottom_ref, ...), custom_call_target="tpu_custom_call" | custom-call | tf_op jit(solution)/shard_map/match_inner/pallas_call | solution.py:408
  80.8 0.0 collective-permute-done.10.inward_ref
  80.9 2.2 %match_edges.1 = bf16[256,4096]{1,0:T(8,128)(2,1)} custom-call(s32[1]{0:T(128)} %bitcast.start_ref, f32[1,128]{1,0:T(1,128)S(1)} %get-tuple-element.64.fit_ref, bf16[16,4096]{1,0:T(8,128)(2,1)S(1)} %collective-permute-done.10.inward_ref, bf16[256,4096]{1,0:T(8,128)(2,1)S(1)} %get-tuple-element.66.x_ref.next_ref.top_ref.bottom_ref, ...), custom_call_target="tpu_custom_call", output_to_operand_aliasing={{}: (8, {})} | custom-call | tf_op jit(solution)/shard_map/match_edges/pallas_call | solution.py:474
  (18 shorter events, 0.1 us)
Async XLA Ops:
  0.6 17.0 %copy-start.2 = (s32[32]{0:T(128)S(1)}, s32[32]{0:T(128)}, u32[]{:S(2)}) copy-start(s32[32]{0:T(128)} %refs_1_.2) | copy-start | bytes 388
  0.6 17.0 %copy-start.1 = (s32[32]{0:T(128)S(1)}, s32[32]{0:T(128)}, u32[]{:S(2)}) copy-start(s32[32]{0:T(128)} %refs_0_.2) | copy-start | bytes 388
  0.7 17.0 %copy-start.3 = (f32[32]{0:T(128)S(1)}, f32[32]{0:T(128)}, u32[]{:S(2)}) copy-start(f32[32]{0:T(128)} %param.11) | copy-start | bytes 388
  0.7 16.9 %copy-start.4 = (f32[32]{0:T(128)S(1)}, f32[32]{0:T(128)}, u32[]{:S(2)}) copy-start(f32[32]{0:T(128)} %param.12) | copy-start | bytes 388
  0.7 8.6 %copy-start.6 = (f32[1,3,6]{2,0,1:T(1,128)S(1)}, f32[1,3,6]{2,0,1:T(1,128)}, u32[]{:S(2)}) copy-start(f32[1,3,6]{2,0,1:T(1,128)} %param.14) | copy-start | bytes 220
  0.7 39.3 %copy-start.5 = (f32[3]{0:T(128)S(1)}, f32[3]{0:T(128)}, u32[]{:S(2)}) copy-start(f32[3]{0:T(128)} %width_ref) | copy-start | bytes 40
  4.1 22.3 %collective-permute-start.9 = (bf16[40,4224]{1,0:T(8,128)(2,1)}, bf16[40,4224]{1,0:T(8,128)(2,1)S(1)}, u32[]{:S(2)}, u32[]{:S(2)}) collective-permute-start(bf16[40,4224]{1,0:T(8,128)(2,1)} %get-tuple-element.37), channel_id=1, source_target_pairs={{0,7},{1,6},{2,5},{3,4},{4,3},{5,2},{6,1},{7,0},{8,15},{9,14},{10,... | collective-permute-start | bytes 1013768 | tf_op jit(solution)/shard_map/ppermute | solution.py:509
  9.3 28.6 %collective-permute-start.7 = (bf16[40,4224]{1,0:T(8,128)(2,1)}, bf16[40,4224]{1,0:T(8,128)(2,1)S(1)}, u32[]{:S(2)}, u32[]{:S(2)}) collective-permute-start(bf16[40,4224]{1,0:T(8,128)(2,1)} %get-tuple-element.38), channel_id=1, source_target_pairs={{0,5},{1,4},{2,7},{3,6},{4,1},{5,0},{6,3},{7,2},{8,13},{9,12},{10,... | collective-permute-start | bytes 1013768 | tf_op jit(solution)/shard_map/ppermute | solution.py:509
  9.3 2.9 %collective-permute-start = (f32[1,3,6]{2,0,1:T(1,128)S(1)}, f32[1,3,6]{2,0,1:T(1,128)S(1)}, u32[]{:S(2)}, u32[]{:S(2)}) collective-permute-start(f32[1,3,6]{2,0,1:T(1,128)S(1)} %copy-done.6), channel_id=1, source_target_pairs={{0,1},{1,0},{2,3},{3,2},{4,5},{5,4},{6,7},{7,6},{8,9},{9,8},{10,11... | collective-permute-start | bytes 224 | tf_op jit(solution)/shard_map/ppermute | solution.py:515
  12.2 2.6 %collective-permute-start.1 = (f32[1,18]{1,0:T(1,128)S(1)}, f32[1,18]{1,0:T(1,128)S(1)}, u32[]{:S(2)}, u32[]{:S(2)}) collective-permute-start(f32[1,18]{1,0:T(1,128)S(1)} %reshape.34), channel_id=1, source_target_pairs={{0,8},{8,0},{16,24},{24,16},{1,9},{9,1},{17,25},{25,17},{2,10},{10... | collective-permute-start | bytes 224 | tf_op jit(solution)/shard_map/ppermute | solution.py:528
  14.8 2.7 %collective-permute-start.2 = (f32[1,18]{1,0:T(1,128)S(1)}, f32[1,18]{1,0:T(1,128)S(1)}, u32[]{:S(2)}, u32[]{:S(2)}) collective-permute-start(f32[1,18]{1,0:T(1,128)S(1)} %add.18), channel_id=1, source_target_pairs={{0,16},{8,24},{16,0},{24,8},{1,17},{9,25},{17,1},{25,9},{2,18},{10... | collective-permute-start | bytes 224 | tf_op jit(solution)/shard_map/ppermute | solution.py:528
  17.6 1.6 %copy-start = (bf16[256,4096]{1,0:T(8,128)(2,1)S(1)}, bf16[256,4096]{1,0:T(8,128)(2,1)}, u32[]{:S(2)}) copy-start(bf16[256,4096]{1,0:T(8,128)(2,1)} %param.8) | copy-start | bytes 6291460
  23.7 17.0 %collective-permute-start.3 = (bf16[40,4224]{1,0:T(8,128)(2,1)S(1)}, bf16[40,4224]{1,0:T(8,128)(2,1)S(1)}, u32[]{:S(2)}, u32[]{:S(2)}) collective-permute-start(bf16[40,4224]{1,0:T(8,128)(2,1)S(1)} %get-tuple-element.47), channel_id=1, source_target_pairs={{0,1},{1,0},{2,3},{3,2},{4,5},{5,4},{6,7},{7,6},{8,9},{9,8},{10,11... | collective-permute-start | bytes 1013768 | tf_op jit(solution)/shard_map/ppermute | solution.py:509
  24.4 19.5 %collective-permute-start.4 = (bf16[40,4224]{1,0:T(8,128)(2,1)S(1)}, bf16[40,4224]{1,0:T(8,128)(2,1)S(1)}, u32[]{:S(2)}, u32[]{:S(2)}) collective-permute-start(bf16[40,4224]{1,0:T(8,128)(2,1)S(1)} %get-tuple-element.48), channel_id=1, source_target_pairs={{0,2},{1,3},{2,0},{3,1},{4,6},{5,7},{6,4},{7,5},{8,10},{9,11},{10,... | collective-permute-start | bytes 1013768 | tf_op jit(solution)/shard_map/ppermute | solution.py:509
  25.1 36.9 %collective-permute-start.5 = (bf16[40,4224]{1,0:T(8,128)(2,1)S(1)}, bf16[40,4224]{1,0:T(8,128)(2,1)S(1)}, u32[]{:S(2)}, u32[]{:S(2)}) collective-permute-start(bf16[40,4224]{1,0:T(8,128)(2,1)S(1)} %get-tuple-element.49), channel_id=1, source_target_pairs={{0,3},{1,2},{2,1},{3,0},{4,7},{5,6},{6,5},{7,4},{8,11},{9,10},{10,... | collective-permute-start | bytes 1013768 | tf_op jit(solution)/shard_map/ppermute | solution.py:509
  26.4 35.5 %collective-permute-start.6 = (bf16[40,4224]{1,0:T(8,128)(2,1)S(1)}, bf16[40,4224]{1,0:T(8,128)(2,1)S(1)}, u32[]{:S(2)}, u32[]{:S(2)}) collective-permute-start(bf16[40,4224]{1,0:T(8,128)(2,1)S(1)} %get-tuple-element.50), channel_id=1, source_target_pairs={{0,4},{1,5},{2,6},{3,7},{4,0},{5,1},{6,2},{7,3},{8,12},{9,13},{10,... | collective-permute-start | bytes 1013768 | tf_op jit(solution)/shard_map/ppermute | solution.py:509
  37.9 24.0 %collective-permute-start.8 = (bf16[40,4224]{1,0:T(8,128)(2,1)S(1)}, bf16[40,4224]{1,0:T(8,128)(2,1)S(1)}, u32[]{:S(2)}, u32[]{:S(2)}) collective-permute-start(bf16[40,4224]{1,0:T(8,128)(2,1)S(1)} %get-tuple-element.51), channel_id=1, source_target_pairs={{0,6},{1,7},{2,4},{3,5},{4,2},{5,3},{6,0},{7,1},{8,14},{9,15},{10,... | collective-permute-start | bytes 1013768 | tf_op jit(solution)/shard_map/ppermute | solution.py:509
  66.1 14.8 %collective-permute-start.10 = (bf16[16,4096]{1,0:T(8,128)(2,1)}, bf16[16,4096]{1,0:T(8,128)(2,1)S(1)}, u32[]{:S(2)}, u32[]{:S(2)}) collective-permute-start(bf16[16,4096]{1,0:T(8,128)(2,1)} %get-tuple-element.65), channel_id=1, source_target_pairs={{0,1},{1,0},{2,3},{3,2},{4,5},{5,4},{6,7},{7,6},{8,9},{9,8},{10,11... | collective-permute-start | bytes 393224 | tf_op jit(solution)/shard_map/ppermute | solution.py:542
  66.5 14.4 %collective-permute-start.11 = (bf16[16,4096]{1,0:T(8,128)(2,1)S(1)}, bf16[16,4096]{1,0:T(8,128)(2,1)S(1)}, u32[]{:S(2)}, u32[]{:S(2)}) collective-permute-start(bf16[16,4096]{1,0:T(8,128)(2,1)S(1)} %get-tuple-element.67), channel_id=1, source_target_pairs={{2,1},{1,2},{4,3},{3,4},{6,5},{5,6},{8,7},{7,8},{10,9},{9,10},{12,... | collective-permute-start | bytes 393224 | tf_op jit(solution)/shard_map/ppermute | solution.py:542

commit v5 on v4

--- a/solution.py
+++ b/solution.py
@@ -23,8 +23,8 @@
 SMALL_VMEM, MATCH_VMEM = 24 * MIB, 32 * MIB
 ROW0 = 96
 FIT0 = 32
-CHUNK2 = 1024
-CHUNK3 = 1024
+CHUNK2 = 2048
+CHUNK3 = 2048
 
 
 def dot(a, b):
@@ -265,34 +265,17 @@
 
 
 def coadd_kernel(peers, rows, chunk, *refs):
-    groups, (image_hbm, inward_ref, outward_ref, cover_ref, fit_ref) = refs[:peers], refs[peers : peers + 5]
-    x_ref, image_ref, sems = refs[peers + 5 :]
+    groups = refs[:peers]
+    image_ref, inward_ref, outward_ref, cover_ref, fit_ref = refs[peers:]
+    rows_dev, width = image_ref.shape
     odd = lax.axis_index(BOTH) % 2 == 1
-    rows_dev, width = image_ref.shape
-    parts = [slice(width, width + LANE)] + [slice(i, i + chunk) for i in range(0, width, chunk)]
-    copies = [
-        [
-            pltpu.make_async_copy(groups[g].at[:, cols], x_ref.at[g, :, cols], sems.at[i, g])
-            for g in range(peers)
-        ]
-        for i, cols in enumerate(parts)
-    ]
-    for part in copies:
-        for copy in part:
-            copy.start()
-
-    def arrived(i):
-        for copy in copies[i]:
-            copy.wait()
-        return [x_ref[g, :, parts[i]] for g in range(peers)]
-
-    places, scale, cover, fit = plan_slots(arrived(0), rows, rows_dev)
+    places, scale, cover, fit = plan_slots([g[:, width:] for g in groups], rows, rows_dev)
     cover_ref[...] = cover
     fit_ref[...] = fit
-    sends = []
-    for i, cols in enumerate(parts[1:]):
+    for at in range(0, width, chunk):
+        cols = slice(at, at + chunk)
         value = None
-        for part, place in zip(split_rows(arrived(i + 1), rows), places):
+        for part, place in zip(split_rows([g[:, cols] for g in groups], rows), places):
             sums = dot(place, part)
             value = sums if value is None else value + sums
         value = (value * scale[:, :1]).astype(BF)
@@ -300,36 +283,23 @@
         top, bottom = value[:EDGE], value[rows_dev - EDGE :]
         inward_ref[:, cols] = jnp.where(odd, top, bottom)
         outward_ref[:, cols] = jnp.where(odd, bottom, top)
-        send = pltpu.make_async_copy(image_ref.at[:, cols], image_hbm.at[:, cols], sems.at[i + 1, peers])
-        send.start()
-        sends.append(send)
-    for send in sends:
-        send.wait()
 
 
 def coadd(groups, rows_dev, rows):
     peers = len(groups)
-    count, cols = groups[0].shape
-    width = cols - LANE
-    chunk = CHUNK2
+    width = groups[0].shape[1] - LANE
     sd = jax.ShapeDtypeStruct
-    hbm = pl.BlockSpec(memory_space=pl.ANY)
     vmem = pl.BlockSpec(memory_space=pltpu.VMEM)
     return pl.pallas_call(
-        functools.partial(coadd_kernel, peers, rows, chunk),
-        in_specs=[hbm] * peers,
-        out_specs=[hbm] + [vmem] * 4,
+        functools.partial(coadd_kernel, peers, rows, CHUNK2),
+        in_specs=[vmem] * peers,
+        out_specs=[vmem] * 5,
         out_shape=[
             sd((rows_dev, width), BF),
             sd((EDGE, width), BF),
             sd((EDGE, width), BF),
             sd((1, rows_dev // rows), F32),
             sd((1, LANE), F32),
-        ],
-        scratch_shapes=[
-            pltpu.VMEM((peers, count, cols), BF),
-            pltpu.VMEM((rows_dev, width), BF),
-            pltpu.SemaphoreType.DMA((1 + width // chunk, peers + 1)),
         ],
         compiler_params=pltpu.CompilerParams(vmem_limit_bytes=SMALL_VMEM),
         name="coadd",
@@ -382,18 +352,33 @@
 
 
 def inner_kernel(
-    all_rows, col_count, start_ref, fit_ref, x_ref, next_ref, band_ref, inner_ref, out_ref
+    all_rows, chunk, start_ref, fit_ref, image_ref, band_ref, inner_ref, out_ref, made_ref, sems
 ):
-    rows_dev, chunk = out_ref.shape
-    first = pl.program_id(0) * chunk
-    x = x_ref[...]
-    head = blank(x[:, :LANE], (lane_of(x[:, :LANE]) >= SHIFT) | (first > 0))
-    tail = next_ref[...]
-    tail = blank(tail, (lane_of(tail) < SHIFT) | (first + chunk < col_count))
-    image = jnp.concatenate([head, x[:, LANE:], tail], axis=1)
-    out_ref[EDGE : rows_dev - EDGE, :] = inner_rows(
-        image, first, start_ref[0], fit_ref, band_ref, inner_ref, all_rows, col_count
-    )
+    rows_dev, col_count = image_ref.shape
+    inner = rows_dev - 2 * EDGE
+    sends = []
+    for at in range(0, col_count, chunk):
+        x = image_ref[:, at : at + chunk]
+        head, tail = x[:, :LANE], image_ref[:, (at + chunk) % col_count :][:, :LANE]
+        if at == 0:
+            head = blank(head, lane_of(head) >= SHIFT)
+        if at + chunk == col_count:
+            tail = blank(tail, lane_of(tail) < SHIFT)
+        image = jnp.concatenate([head, x[:, LANE:], tail], axis=1)
+        value = inner_rows(
+            image, at, start_ref[0], fit_ref, band_ref, inner_ref, all_rows, col_count
+        )
+        slot = len(sends) % 2
+        if len(sends) >= 2:
+            sends[-2].wait()
+        made_ref[slot] = value
+        send = pltpu.make_async_copy(
+            made_ref.at[slot], out_ref.at[pl.ds(EDGE, inner), pl.ds(at, chunk)], sems.at[slot]
+        )
+        send.start()
+        sends.append(send)
+    for send in sends[-2:]:
+        send.wait()
 
 
 def whole_of(v):
@@ -404,27 +389,23 @@
     rows_dev, col_count = image.shape
     chunk = CHUNK3
     smem = pl.BlockSpec(memory_space=pltpu.SMEM)
-    steps = col_count // chunk
+    vmem = pl.BlockSpec(memory_space=pltpu.VMEM)
     return pl.pallas_call(
-        functools.partial(inner_kernel, all_rows, col_count),
-        grid=(steps,),
-        in_specs=[
-            smem,
-            smem,
-            pl.BlockSpec((rows_dev, chunk), lambda i: (0, i)),
-            pl.BlockSpec((rows_dev, LANE), lambda i: (0, (i + 1) % steps * (chunk // LANE))),
-            whole_of(band),
-            whole_of(inner),
+        functools.partial(inner_kernel, all_rows, chunk),
+        in_specs=[smem, smem, vmem, vmem, vmem],
+        out_specs=pl.BlockSpec(memory_space=pl.ANY),
+        out_shape=jax.ShapeDtypeStruct((rows_dev, col_count), BF),
+        scratch_shapes=[
+            pltpu.VMEM((2, rows_dev - 2 * EDGE, chunk), BF),
+            pltpu.SemaphoreType.DMA((2,)),
         ],
-        out_specs=pl.BlockSpec((rows_dev, chunk), lambda i: (0, i)),
-        out_shape=jax.ShapeDtypeStruct((rows_dev, col_count), BF),
         compiler_params=pltpu.CompilerParams(vmem_limit_bytes=MATCH_VMEM),
         name="match_inner",
-    )(start, fit, image, image, band, inner)
+    )(start, fit, image, band, inner)
 
 
 def edge_kernel(
-    all_rows, rows_dev, start_ref, fit_ref, inward_ref, top_ref, bottom_ref, outward_ref, band_ref,
+    all_rows, rows_dev, start_ref, fit_ref, inward_ref, image_ref, outward_ref, band_ref,
     edge_ref, old_ref, out_ref, made_ref, sems,
 ):
     col_count = made_ref.shape[1]
@@ -432,7 +413,8 @@
     odd = lax.axis_index(BOTH) % 2 == 1
     inward, outward = inward_ref[...], outward_ref[...]
     above, below = jnp.where(odd, inward, outward), jnp.where(odd, outward, inward)
-    x = jnp.concatenate([above, top_ref[...], bottom_ref[...], below], axis=0)
+    top, bottom = image_ref[: 2 * EDGE], image_ref[rows_dev - 2 * EDGE :]
+    x = jnp.concatenate([above, top, bottom, below], axis=0)
     rowconv = dot(edge_ref[...], x).astype(BF)
     head = rowconv[:, :LANE]
     rowconv = jnp.concatenate(
@@ -469,29 +451,18 @@
 def match_edges(matched, image, halos, start, fit, band, edge, all_rows):
     rows_dev, col_count = matched.shape
     smem = pl.BlockSpec(memory_space=pltpu.SMEM)
+    vmem = pl.BlockSpec(memory_space=pltpu.VMEM)
     hbm = pl.BlockSpec(memory_space=pl.ANY)
-    strip = lambda at: pl.BlockSpec((2 * EDGE, col_count), lambda i: (at, 0))
     return pl.pallas_call(
         functools.partial(edge_kernel, all_rows, rows_dev),
-        grid=(1,),
-        in_specs=[
-            smem,
-            smem,
-            whole_of(halos[0]),
-            strip(0),
-            strip(rows_dev // (2 * EDGE) - 1),
-            whole_of(halos[1]),
-            whole_of(band),
-            whole_of(edge),
-            hbm,
-        ],
+        in_specs=[smem, smem] + [vmem] * 5 + [hbm],
         out_specs=hbm,
         out_shape=jax.ShapeDtypeStruct(matched.shape, BF),
         scratch_shapes=[pltpu.VMEM((2 * EDGE, col_count), BF), pltpu.SemaphoreType.DMA((2,))],
-        input_output_aliases={8: 0},
+        input_output_aliases={7: 0},
         compiler_params=pltpu.CompilerParams(vmem_limit_bytes=SMALL_VMEM),
         name="match_edges",
-    )(start, fit, halos[0], image, image, halos[1], band, edge, matched)
+    )(start, fit, halos[0], image, halos[1], band, edge, matched)
 
 
 def shards(

time: 83.3 us -> 81 us (0.972)
  Pallas kernels: 22 us -> 19.4 us
    pallas_call x3, Pallas kernels: 13.3 us -> 10.7 us  [the longest x1 6.29 us: match_inner(): pl.pallas_call(functools.partial(inner_kernel, all_rows, chunk), in_specs...]
  transfers between devices with their start and end apart: 12 -> 12, of which waited for: 6 -> 6; matrix products, arithmetic and copies ran while one was open for 0% -> 0% of each run, Pallas kernels for 15% -> 14%
where the time goes in v5:
time: 81 us; the launch traced here: 80.8 us
  waiting for transfers between devices  31.5 us (39%)
  starting transfers between devices  26.5 us (33%)
  Pallas kernels  19.4 us (24%)
  local copies, waits for them, and re-layouts  1.78 us (2%)
  between operations  1.58 us (2%)
    ppermute x7, waiting for transfers between devices, shards(): lax.ppermute(group, 'patch', [(i, i ^ s) for i in range(peers)])  27.3 us
    ppermute x7, starting transfers between devices, shards(): lax.ppermute(group, 'patch', [(i, i ^ s) for i in range(peers)])  15.2 us
    ppermute x2, starting transfers between devices, shards(): halos = (lax.ppermute(inward, BOTH, even), lax.ppermute(outward, BOTH, odd))  8.01 us
    pallas_call x2, Pallas kernels, resample(): pl.pallas_call(functools.partial(resample_kernel, cap, peers, order, len(...  7.92 us
    pallas_call x1, Pallas kernels, match_inner(): pl.pallas_call(functools.partial(inner_kernel, all_rows, chunk), in_specs...  6.29 us
    ppermute x2, starting transfers between devices, shards(): fit = fit + lax.ppermute(fit, 'det', [(i, i ^ span) for i in range(dets)])  2.99 us
    ppermute x2, waiting for transfers between devices, shards(): fit = fit + lax.ppermute(fit, 'det', [(i, i ^ span) for i in range(dets)])  2.27 us
    pallas_call x1, Pallas kernels, match_edges(): pl.pallas_call(functools.partial(edge_kernel, all_rows, rows_dev), in_spe...  2.25 us
  transfers between devices with their start and end apart: 12, of which 6 were waited for; matrix products, arithmetic and copies ran while one was open for 0% of the time, Pallas kernels for 14%

profile of v5, /device:TPU:1, one launch (start us, length us, event | category | flops | bytes accessed | tf_op | source)
XLA Modules:
  0.0 80.8 jit_solution(60294798492422669)
XLA Ops:
  0.7 3.4 %resample.2 = (bf16[40,4224]{1,0:T(8,128)(2,1)}, bf16[40,4224]{1,0:T(8,128)(2,1)}) custom-call(s32[32]{0:T(128)} %refs_0_.2, s32[32]{0:T(128)} %refs_1_.2, f32[1,32]{1,0:T(1,128)} %bitcast.13, f32[1,32]{1,0:T(1,128)} %bitcast.15, bf16[32,8,4096]{2,1,0:T(8,128)(2,1)} %bitcast.11), custom_call_target="tpu_custom_call" | custom-call | tf_op jit(solution)/shard_map/resample/pallas_call | solution.py:168
  4.1 5.1 %collective-permute-start.9 = (bf16[40,4224]{1,0:T(8,128)(2,1)}, bf16[40,4224]{1,0:T(8,128)(2,1)S(1)}, u32[]{:S(2)}, u32[]{:S(2)}) collective-permute-start(bf16[40,4224]{1,0:T(8,128)(2,1)} %get-tuple-element.37), channel_id=1, source_target_pairs={{0,7},{1,6},{2,5},{3,4},{4,3},{5,2},{6,1},{7,0},{8,15},{9,14},{10,... | collective-permute-start | bytes 1013768 | tf_op jit(solution)/shard_map/ppermute | solution.py:480
  9.3 0.0 collective-permute-start.7
  9.3 0.3 collective-permute-start
  10.3 1.9 %collective-permute-done = f32[1,3,6]{2,0,1:T(1,128)S(1)} collective-permute-done((f32[1,3,6]{2,0,1:T(1,128)S(1)}, f32[1,3,6]{2,0,1:T(1,128)S(1)}, u32[]{:S(2)}, u32[]{:S(2)}) %collective-permute-start) | collective-permute-done | bytes 104 | tf_op jit(solution)/shard_map/ppermute | solution.py:486
  12.2 0.1 reshape.34
  12.2 1.8 %collective-permute-start.1 = (f32[1,18]{1,0:T(1,128)S(1)}, f32[1,18]{1,0:T(1,128)S(1)}, u32[]{:S(2)}, u32[]{:S(2)}) collective-permute-start(f32[1,18]{1,0:T(1,128)S(1)} %reshape.34), channel_id=1, source_target_pairs={{0,8},{8,0},{16,24},{24,16},{1,9},{9,1},{17,25},{25,17},{2,10},{10... | collective-permute-start | bytes 224 | tf_op jit(solution)/shard_map/ppermute | solution.py:499
  14.0 0.8 %collective-permute-done.1 = f32[1,18]{1,0:T(1,128)S(1)} collective-permute-done((f32[1,18]{1,0:T(1,128)S(1)}, f32[1,18]{1,0:T(1,128)S(1)}, u32[]{:S(2)}, u32[]{:S(2)}) %collective-permute-start.1) | collective-permute-done | bytes 104 | tf_op jit(solution)/shard_map/ppermute | solution.py:499
  14.8 1.2 %collective-permute-start.2 = (f32[1,18]{1,0:T(1,128)S(1)}, f32[1,18]{1,0:T(1,128)S(1)}, u32[]{:S(2)}, u32[]{:S(2)}) collective-permute-start(f32[1,18]{1,0:T(1,128)S(1)} %add.18), channel_id=1, source_target_pairs={{0,16},{8,24},{16,0},{24,8},{1,17},{9,25},{17,1},{25,9},{2,18},{10... | collective-permute-start | bytes 224 | tf_op jit(solution)/shard_map/ppermute | solution.py:499
  16.1 1.4 %collective-permute-done.2 = f32[1,18]{1,0:T(1,128)S(1)} collective-permute-done((f32[1,18]{1,0:T(1,128)S(1)}, f32[1,18]{1,0:T(1,128)S(1)}, u32[]{:S(2)}, u32[]{:S(2)}) %collective-permute-start.2) | collective-permute-done | bytes 104 | tf_op jit(solution)/shard_map/ppermute | solution.py:499
  17.5 0.1 concatenate.4.refs_5_
  17.6 0.0 copy-start
  17.6 1.6 %copy-done = bf16[256,4096]{1,0:T(8,128)(2,1)S(1)} copy-done((bf16[256,4096]{1,0:T(8,128)(2,1)S(1)}, bf16[256,4096]{1,0:T(8,128)(2,1)}, u32[]{:S(2)}) %copy-start) | copy-done | bytes 2097176
  19.2 4.5 %resample.3 = (bf16[40,4224]{1,0:T(8,128)(2,1)S(1)}, bf16[40,4224]{1,0:T(8,128)(2,1)S(1)}, bf16[40,4224]{1,0:T(8,128)(2,1)S(1)}, bf16[40,4224]{1,0:T(8,128)(2,1)...) custom-call(s32[32]{0:T(128)S(1)} %copy-done.1, s32[32]{0:T(128)S(1)} %copy-done.2, ...), custom_call_target="tpu_custom_call" | custom-call | tf_op jit(solution)/shard_map/resample/pallas_call | solution.py:168
  23.7 0.7 collective-permute-start.3
  24.4 0.7 collective-permute-start.4
  25.1 1.4 %collective-permute-start.5 = (bf16[40,4224]{1,0:T(8,128)(2,1)S(1)}, bf16[40,4224]{1,0:T(8,128)(2,1)S(1)}, u32[]{:S(2)}, u32[]{:S(2)}) collective-permute-start(bf16[40,4224]{1,0:T(8,128)(2,1)S(1)} %get-tuple-element.49), channel_id=1, source_target_pairs={{0,3},{1,2},{2,1},{3,0},{4,7},{5,6},{6,5},{7,4},{8,11},{9,10},{10,... | collective-permute-start | bytes 1013768 | tf_op jit(solution)/shard_map/ppermute | solution.py:480
  26.4 0.0 collective-permute-done.9.refs_7_
  26.4 5.3 %collective-permute-start.6 = (bf16[40,4224]{1,0:T(8,128)(2,1)S(1)}, bf16[40,4224]{1,0:T(8,128)(2,1)S(1)}, u32[]{:S(2)}, u32[]{:S(2)}) collective-permute-start(bf16[40,4224]{1,0:T(8,128)(2,1)S(1)} %get-tuple-element.50), channel_id=1, source_target_pairs={{0,4},{1,5},{2,6},{3,7},{4,0},{5,1},{6,2},{7,3},{8,12},{9,13},{10,... | collective-permute-start | bytes 1013768 | tf_op jit(solution)/shard_map/ppermute | solution.py:480
  31.7 6.2 %collective-permute-done.7.refs_5_ = bf16[40,4224]{1,0:T(8,128)(2,1)S(1)} collective-permute-done((bf16[40,4224]{1,0:T(8,128)(2,1)}, bf16[40,4224]{1,0:T(8,128)(2,1)S(1)}, u32[]{:S(2)}, u32[]{:S(2)}) %collective-permute-start.7) | collective-permute-done | bytes 337952 | tf_op jit(solution)/shard_map/ppermute | solution.py:480
  37.9 2.0 %collective-permute-start.8 = (bf16[40,4224]{1,0:T(8,128)(2,1)S(1)}, bf16[40,4224]{1,0:T(8,128)(2,1)S(1)}, u32[]{:S(2)}, u32[]{:S(2)}) collective-permute-start(bf16[40,4224]{1,0:T(8,128)(2,1)S(1)} %get-tuple-element.51), channel_id=1, source_target_pairs={{0,6},{1,7},{2,4},{3,5},{4,2},{5,3},{6,0},{7,1},{8,14},{9,15},{10,... | collective-permute-start | bytes 1013768 | tf_op jit(solution)/shard_map/ppermute | solution.py:480
  39.9 0.8 %tables.1 = (bf16[256,384]{1,0:T(8,128)(2,1)S(1)}, bf16[3,224,256]{2,1,0:T(8,128)(2,1)S(1)}, bf16[96,96]{1,0:T(8,128)(2,1)S(1)}) custom-call(f32[3]{0:T(128)S(1)} %copy-done.5), custom_call_target="tpu_custom_call" | custom-call | tf_op jit(solution)/shard_map/tables/pallas_call | solution.py:218
  40.7 0.0 collective-permute-done.3.refs_1_
  40.8 3.2 %collective-permute-done.4.refs_2_ = bf16[40,4224]{1,0:T(8,128)(2,1)S(1)} collective-permute-done((bf16[40,4224]{1,0:T(8,128)(2,1)S(1)}, bf16[40,4224]{1,0:T(8,128)(2,1)S(1)}, u32[]{:S(2)}, u32[]{:S(2)}) %collective-permute-start.4) | collective-permute-done | bytes 337952 | tf_op jit(solution)/shard_map/ppermute | solution.py:480
  43.9 18.0 %collective-permute-done.5.refs_3_ = bf16[40,4224]{1,0:T(8,128)(2,1)S(1)} collective-permute-done((bf16[40,4224]{1,0:T(8,128)(2,1)S(1)}, bf16[40,4224]{1,0:T(8,128)(2,1)S(1)}, u32[]{:S(2)}, u32[]{:S(2)}) %collective-permute-start.5) | collective-permute-done | bytes 337952 | tf_op jit(solution)/shard_map/ppermute | solution.py:480
  61.9 0.0 collective-permute-done.6.refs_4_
  61.9 2.1 %coadd.1 = (bf16[256,4096]{1,0:T(8,128)(2,1)S(1)}, bf16[16,4096]{1,0:T(8,128)(2,1)}, bf16[16,4096]{1,0:T(8,128)(2,1)S(1)}, f32[1,32]{1,0:T(1,128)}, f32[1,128]{1,0:T(1,128)S(1)}) custom-call(bf16[40,4224]{1,0:T(8,128)(2,1)S(1)} %get-tuple-element.56.refs_0_, bf16[40,4224]{1,0:T(8,128)(2,1)S(1)} %collective-permute-done.3.refs_1_, ...), custom_call_target="tpu_custom_call" | custom-call | tf_op jit(solution)/shard_map/coadd/pallas_call | solution.py:293
  64.1 0.4 collective-permute-start.10
  64.4 7.6 %collective-permute-start.11 = (bf16[16,4096]{1,0:T(8,128)(2,1)S(1)}, bf16[16,4096]{1,0:T(8,128)(2,1)S(1)}, u32[]{:S(2)}, u32[]{:S(2)}) collective-permute-start(bf16[16,4096]{1,0:T(8,128)(2,1)S(1)} %get-tuple-element.67), channel_id=1, source_target_pairs={{2,1},{1,2},{4,3},{3,4},{6,5},{5,6},{8,7},{7,8},{10,9},{9,10},{12,... | collective-permute-start | bytes 393224 | tf_op jit(solution)/shard_map/ppermute | solution.py:513
  72.1 6.3 %match_inner.1.old_ref = bf16[256,4096]{1,0:T(8,128)(2,1)} custom-call(s32[1]{0:T(128)} %bitcast.start_ref, f32[1,128]{1,0:T(1,128)S(1)} %get-tuple-element.64.fit_ref, bf16[256,4096]{1,0:T(8,128)(2,1)S(1)} %get-tuple-element.66.image_ref, bf16[256,384]{1,0:T(8,128)(2,1)S(1)} %get-tuple-element.68.band_ref, bf16[3,224,256]{2,1,0:T(8,128)(2,1)S(1)} %get-tuple-element.70.inner_ref), custom_call_target="tpu_custom_call" | custom-call | tf_op jit(solution)/shard_map/match_inner/pallas_call | solution.py:393
  78.4 0.0 collective-permute-done.10.inward_ref
  78.4 2.2 %match_edges.1 = bf16[256,4096]{1,0:T(8,128)(2,1)} custom-call(s32[1]{0:T(128)} %bitcast.start_ref, f32[1,128]{1,0:T(1,128)S(1)} %get-tuple-element.64.fit_ref, bf16[16,4096]{1,0:T(8,128)(2,1)S(1)} %collective-permute-done.10.inward_ref, bf16[256,4096]{1,0:T(8,128)(2,1)S(1)} %get-tuple-element.66.image_ref, ...), custom_call_target="tpu_custom_call", output_to_operand_aliasing={{}: (7, {})} | custom-call | tf_op jit(solution)/shard_map/match_edges/pallas_call | solution.py:456
  (18 shorter events, 0.1 us)
Async XLA Ops:
  0.6 17.0 %copy-start.2 = (s32[32]{0:T(128)S(1)}, s32[32]{0:T(128)}, u32[]{:S(2)}) copy-start(s32[32]{0:T(128)} %refs_1_.2) | copy-start | bytes 388
  0.6 17.0 %copy-start.1 = (s32[32]{0:T(128)S(1)}, s32[32]{0:T(128)}, u32[]{:S(2)}) copy-start(s32[32]{0:T(128)} %refs_0_.2) | copy-start | bytes 388
  0.7 17.0 %copy-start.3 = (f32[32]{0:T(128)S(1)}, f32[32]{0:T(128)}, u32[]{:S(2)}) copy-start(f32[32]{0:T(128)} %param.11) | copy-start | bytes 388
  0.7 16.9 %copy-start.4 = (f32[32]{0:T(128)S(1)}, f32[32]{0:T(128)}, u32[]{:S(2)}) copy-start(f32[32]{0:T(128)} %param.12) | copy-start | bytes 388
  0.7 8.6 %copy-start.6 = (f32[1,3,6]{2,0,1:T(1,128)S(1)}, f32[1,3,6]{2,0,1:T(1,128)}, u32[]{:S(2)}) copy-start(f32[1,3,6]{2,0,1:T(1,128)} %param.14) | copy-start | bytes 220
  0.7 39.2 %copy-start.5 = (f32[3]{0:T(128)S(1)}, f32[3]{0:T(128)}, u32[]{:S(2)}) copy-start(f32[3]{0:T(128)} %width_ref) | copy-start | bytes 40
  4.1 22.3 %collective-permute-start.9 = (bf16[40,4224]{1,0:T(8,128)(2,1)}, bf16[40,4224]{1,0:T(8,128)(2,1)S(1)}, u32[]{:S(2)}, u32[]{:S(2)}) collective-permute-start(bf16[40,4224]{1,0:T(8,128)(2,1)} %get-tuple-element.37), channel_id=1, source_target_pairs={{0,7},{1,6},{2,5},{3,4},{4,3},{5,2},{6,1},{7,0},{8,15},{9,14},{10,... | collective-permute-start | bytes 1013768 | tf_op jit(solution)/shard_map/ppermute | solution.py:480
  9.3 28.6 %collective-permute-start.7 = (bf16[40,4224]{1,0:T(8,128)(2,1)}, bf16[40,4224]{1,0:T(8,128)(2,1)S(1)}, u32[]{:S(2)}, u32[]{:S(2)}) collective-permute-start(bf16[40,4224]{1,0:T(8,128)(2,1)} %get-tuple-element.38), channel_id=1, source_target_pairs={{0,5},{1,4},{2,7},{3,6},{4,1},{5,0},{6,3},{7,2},{8,13},{9,12},{10,... | collective-permute-start | bytes 1013768 | tf_op jit(solution)/shard_map/ppermute | solution.py:480
  9.3 2.9 %collective-permute-start = (f32[1,3,6]{2,0,1:T(1,128)S(1)}, f32[1,3,6]{2,0,1:T(1,128)S(1)}, u32[]{:S(2)}, u32[]{:S(2)}) collective-permute-start(f32[1,3,6]{2,0,1:T(1,128)S(1)} %copy-done.6), channel_id=1, source_target_pairs={{0,1},{1,0},{2,3},{3,2},{4,5},{5,4},{6,7},{7,6},{8,9},{9,8},{10,11... | collective-permute-start | bytes 224 | tf_op jit(solution)/shard_map/ppermute | solution.py:486
  12.2 2.6 %collective-permute-start.1 = (f32[1,18]{1,0:T(1,128)S(1)}, f32[1,18]{1,0:T(1,128)S(1)}, u32[]{:S(2)}, u32[]{:S(2)}) collective-permute-start(f32[1,18]{1,0:T(1,128)S(1)} %reshape.34), channel_id=1, source_target_pairs={{0,8},{8,0},{16,24},{24,16},{1,9},{9,1},{17,25},{25,17},{2,10},{10... | collective-permute-start | bytes 224 | tf_op jit(solution)/shard_map/ppermute | solution.py:499
  14.8 2.7 %collective-permute-start.2 = (f32[1,18]{1,0:T(1,128)S(1)}, f32[1,18]{1,0:T(1,128)S(1)}, u32[]{:S(2)}, u32[]{:S(2)}) collective-permute-start(f32[1,18]{1,0:T(1,128)S(1)} %add.18), channel_id=1, source_target_pairs={{0,16},{8,24},{16,0},{24,8},{1,17},{9,25},{17,1},{25,9},{2,18},{10... | collective-permute-start | bytes 224 | tf_op jit(solution)/shard_map/ppermute | solution.py:499
  17.6 1.6 %copy-start = (bf16[256,4096]{1,0:T(8,128)(2,1)S(1)}, bf16[256,4096]{1,0:T(8,128)(2,1)}, u32[]{:S(2)}) copy-start(bf16[256,4096]{1,0:T(8,128)(2,1)} %param.8) | copy-start | bytes 6291460
  23.7 17.0 %collective-permute-start.3 = (bf16[40,4224]{1,0:T(8,128)(2,1)S(1)}, bf16[40,4224]{1,0:T(8,128)(2,1)S(1)}, u32[]{:S(2)}, u32[]{:S(2)}) collective-permute-start(bf16[40,4224]{1,0:T(8,128)(2,1)S(1)} %get-tuple-element.47), channel_id=1, source_target_pairs={{0,1},{1,0},{2,3},{3,2},{4,5},{5,4},{6,7},{7,6},{8,9},{9,8},{10,11... | collective-permute-start | bytes 1013768 | tf_op jit(solution)/shard_map/ppermute | solution.py:480
  24.4 19.5 %collective-permute-start.4 = (bf16[40,4224]{1,0:T(8,128)(2,1)S(1)}, bf16[40,4224]{1,0:T(8,128)(2,1)S(1)}, u32[]{:S(2)}, u32[]{:S(2)}) collective-permute-start(bf16[40,4224]{1,0:T(8,128)(2,1)S(1)} %get-tuple-element.48), channel_id=1, source_target_pairs={{0,2},{1,3},{2,0},{3,1},{4,6},{5,7},{6,4},{7,5},{8,10},{9,11},{10,... | collective-permute-start | bytes 1013768 | tf_op jit(solution)/shard_map/ppermute | solution.py:480
  25.1 36.9 %collective-permute-start.5 = (bf16[40,4224]{1,0:T(8,128)(2,1)S(1)}, bf16[40,4224]{1,0:T(8,128)(2,1)S(1)}, u32[]{:S(2)}, u32[]{:S(2)}) collective-permute-start(bf16[40,4224]{1,0:T(8,128)(2,1)S(1)} %get-tuple-element.49), channel_id=1, source_target_pairs={{0,3},{1,2},{2,1},{3,0},{4,7},{5,6},{6,5},{7,4},{8,11},{9,10},{10,... | collective-permute-start | bytes 1013768 | tf_op jit(solution)/shard_map/ppermute | solution.py:480
  26.4 35.5 %collective-permute-start.6 = (bf16[40,4224]{1,0:T(8,128)(2,1)S(1)}, bf16[40,4224]{1,0:T(8,128)(2,1)S(1)}, u32[]{:S(2)}, u32[]{:S(2)}) collective-permute-start(bf16[40,4224]{1,0:T(8,128)(2,1)S(1)} %get-tuple-element.50), channel_id=1, source_target_pairs={{0,4},{1,5},{2,6},{3,7},{4,0},{5,1},{6,2},{7,3},{8,12},{9,13},{10,... | collective-permute-start | bytes 1013768 | tf_op jit(solution)/shard_map/ppermute | solution.py:480
  37.9 24.0 %collective-permute-start.8 = (bf16[40,4224]{1,0:T(8,128)(2,1)S(1)}, bf16[40,4224]{1,0:T(8,128)(2,1)S(1)}, u32[]{:S(2)}, u32[]{:S(2)}) collective-permute-start(bf16[40,4224]{1,0:T(8,128)(2,1)S(1)} %get-tuple-element.51), channel_id=1, source_target_pairs={{0,6},{1,7},{2,4},{3,5},{4,2},{5,3},{6,0},{7,1},{8,14},{9,15},{10,... | collective-permute-start | bytes 1013768 | tf_op jit(solution)/shard_map/ppermute | solution.py:480
  64.1 14.3 %collective-permute-start.10 = (bf16[16,4096]{1,0:T(8,128)(2,1)}, bf16[16,4096]{1,0:T(8,128)(2,1)S(1)}, u32[]{:S(2)}, u32[]{:S(2)}) collective-permute-start(bf16[16,4096]{1,0:T(8,128)(2,1)} %get-tuple-element.65), channel_id=1, source_target_pairs={{0,1},{1,0},{2,3},{3,2},{4,5},{5,4},{6,7},{7,6},{8,9},{9,8},{10,11... | collective-permute-start | bytes 393224 | tf_op jit(solution)/shard_map/ppermute | solution.py:513
  64.4 14.0 %collective-permute-start.11 = (bf16[16,4096]{1,0:T(8,128)(2,1)S(1)}, bf16[16,4096]{1,0:T(8,128)(2,1)S(1)}, u32[]{:S(2)}, u32[]{:S(2)}) collective-permute-start(bf16[16,4096]{1,0:T(8,128)(2,1)S(1)} %get-tuple-element.67), channel_id=1, source_target_pairs={{2,1},{1,2},{4,3},{3,4},{6,5},{5,6},{8,7},{7,8},{10,9},{9,10},{12,... | collective-permute-start | bytes 393224 | tf_op jit(solution)/shard_map/ppermute | solution.py:513

commit v6 on v5

--- a/solution.py
+++ b/solution.py
@@ -46,7 +46,7 @@
         dest_ref, off_ref, src_ref, count_ref, shift_ref, wgt_ref, x_ref, made_ref, diff_ref,
         fit_ref, sems,
     ) = refs[-11:]
-    blocks, rows, width = x_ref.shape
+    blocks, rows, width = dest_ref.shape[0], x_ref.shape[0] // dest_ref.shape[0], x_ref.shape[1]
     tiles = width // LANE
     me = lax.axis_index("patch")
     smalls = [(dest_hbm, dest_ref), (off_hbm, off_ref), (shift_hbm, shift_ref), (wgt_hbm, wgt_ref)]
@@ -98,7 +98,8 @@
             got = src_ref[group * cap + rank]
             valid = got >= 0
             b = jnp.maximum(got, 0)
-            xs.append(x_ref[b].astype(F32))
+            two = x_ref[pl.ds(pl.multiple_of(b // 2 * 2 * rows, 2 * rows), 2 * rows), :].astype(F32)
+            xs.append(jnp.where(b % 2 == 1, two[rows:], two[:rows]))
             own = (block_lane == b) & valid
             column = jnp.sum(jnp.where(own, coefs, 0.0), axis=1, keepdims=True)
             diff = diff_ref[...] - off_ref[b]
@@ -125,26 +126,27 @@
             at = made[2 * rows * i : 2 * rows * (i + 1)]
             return at[:rows, :LANE], at[rows:, LANE:]
 
-        for t in range(tiles):
-            top, bottom = piece(t)
-            if t == 0:
-                last = piece(tiles)
-                top = jnp.where(lane < SHIFT, last[0], top)
-                bottom = jnp.where(lane < SHIFT, last[1], bottom)
-            put(slots, t, top, bottom)
-        put(slots, tiles, notes[0], notes[1])
-
-    def put(slots, t, top, bottom):
-        cols = slice(LANE * t, LANE * (t + 1))
+        tops, bottoms = [list(half) for half in zip(*(piece(t) for t in range(tiles)))]
+        last = piece(tiles)
+        tops[0] = jnp.where(lane < SHIFT, last[0], tops[0])
+        bottoms[0] = jnp.where(lane < SHIFT, last[1], bottoms[0])
+        tops.append(notes[0])
+        bottoms.append(notes[1])
         (group0, rank0), (group1, rank1) = slots
-        group0, group1 = order.index(group0), order.index(group1)
         if group0 == group1:
-            made_ref[group0, rows * rank0 : rows * (rank0 + 2), cols] = jnp.concatenate(
-                [top, bottom], axis=0
-            ).astype(BF)
+            for t in range(tiles + 1):
+                put(group0, rank0 // 2 * (tiles + 1) + t, tops[t], bottoms[t])
         else:
-            made_ref[group0, rows * rank0 : rows * (rank0 + 1), cols] = top.astype(BF)
-            made_ref[group1, rows * rank1 : rows * (rank1 + 1), cols] = bottom.astype(BF)
+            half = tiles // 2 + 1
+            for group, pieces in ((group0, tops), (group1, bottoms)):
+                pieces = pieces + [jnp.zeros((rows, LANE), F32)] * (2 * half - len(pieces))
+                for t in range(half):
+                    put(group, cap // 2 * (tiles + 1) + t, pieces[t], pieces[t + half])
+
+    def put(group, tile, top, bottom):
+        made_ref[order.index(group), :, LANE * tile : LANE * (tile + 1)] = jnp.concatenate(
+            [top, bottom], axis=0
+        ).astype(BF)
 
     sends = [pltpu.make_async_copy(made_ref.at[i], outs[i], sems.at[6 + i]) for i in range(len(order))]
     for at in range(0, len(order), 2):
@@ -160,6 +162,11 @@
         send.wait()
 
 
+def message_shape(cap, rows, width):
+    tiles = width // LANE
+    return 2 * rows, LANE * (cap // 2 * (tiles + 1) + cap % 2 * (tiles // 2 + 1))
+
+
 def resample(exposure, dest, offset, shift, weight, fit, peers, cap, order):
     rows_dev, width = exposure.shape
     blocks = dest.shape[0]
@@ -169,7 +176,7 @@
         functools.partial(resample_kernel, cap, peers, order, len(fit)),
         in_specs=[hbm] * (5 + len(fit)),
         out_specs=[hbm] * len(order),
-        out_shape=[jax.ShapeDtypeStruct((cap * rows, width + LANE), BF)] * len(order),
+        out_shape=[jax.ShapeDtypeStruct(message_shape(cap, rows, width), BF)] * len(order),
         scratch_shapes=[
             pltpu.SMEM((blocks,), jnp.int32),
             pltpu.SMEM((blocks,), jnp.int32),
@@ -177,15 +184,15 @@
             pltpu.SMEM((peers,), jnp.int32),
             pltpu.VMEM((1, blocks), F32),
             pltpu.VMEM((1, blocks), F32),
-            pltpu.VMEM((blocks, rows, width), BF),
-            pltpu.VMEM((len(order), cap * rows, width + LANE), BF),
+            pltpu.VMEM((rows_dev, width), BF),
+            pltpu.VMEM((len(order),) + message_shape(cap, rows, width), BF),
             pltpu.VMEM((2 * LANE - ROW0, LANE), jnp.int32),
             pltpu.VMEM((1, LANE), F32),
             pltpu.SemaphoreType.DMA((6 + len(order),)),
         ],
         compiler_params=pltpu.CompilerParams(vmem_limit_bytes=LATE_VMEM if fit else EARLY_VMEM),
         name="resample",
-    )(dest, offset, shift.reshape(1, blocks), weight.reshape(1, blocks), exposure.reshape(blocks, rows, width), *fit)
+    )(dest, offset, shift.reshape(1, blocks), weight.reshape(1, blocks), exposure, *fit)
 
 
 def gauss_band(shape, rows_axis, width, total):
@@ -228,19 +235,38 @@
     )(basis_width)
 
 
-def split_rows(groups, rows):
-    even = groups[0].shape[0] // (2 * rows) * (2 * rows)
-    parts = [jnp.concatenate([g[:even] for g in groups], axis=0)]
-    if even < groups[0].shape[0]:
-        parts.append(jnp.concatenate([g[even:].astype(F32) for g in groups], axis=0).astype(BF))
+def split_rows(groups, cap, tiles, first, count):
+    parts = []
+    at = [LANE * (pair * (tiles + 1) + first) for pair in range(cap // 2)]
+    if at:
+        pairs = [g[:, a : a + LANE * count] for g in groups for a in at]
+        parts.append(jnp.concatenate(pairs, axis=0))
+    if cap % 2:
+        half, base = tiles // 2 + 1, cap // 2 * (tiles + 1)
+        upper, lower = max(0, min(half, first + count) - first), max(0, first + count - max(first, half))
+        alone = []
+        for g in groups:
+            rows = g.shape[0] // 2
+            pieces = []
+            if upper:
+                a = LANE * (base + first)
+                pieces.append(g[:, a : a + LANE * upper].astype(F32)[:rows])
+            if lower:
+                a = LANE * (base + max(first, half) - half)
+                pieces.append(g[:, a : a + LANE * lower].astype(F32)[rows:])
+            alone.append(jnp.concatenate(pieces, axis=1))
+        parts.append(jnp.concatenate(alone, axis=0).astype(BF))
     return parts
 
 
-def plan_slots(notes, rows, rows_dev):
+def plan_slots(notes, rows, rows_dev, cap, peers):
     slots = rows_dev // rows
-    fit = sum(sum(g[i : i + 1].astype(F32) for i in range(3)) for g in notes[::2])
+    size = cap // 2 * 2 * rows
+    fit = sum(
+        notes[0][size * g + i : size * g + i + 1].astype(F32) for g in range(0, peers, 2) for i in range(3)
+    )
     places, column, lined = [], None, None
-    for part in split_rows(notes, rows):
+    for part in notes:
         count = part.shape[0]
         slot = part[:, :1].astype(F32)
         across = jnp.broadcast_to(slot, (count, LANE)).T[:1].astype(jnp.int32)
@@ -264,18 +290,20 @@
     return places, scale, lined[1:2] + lined[2:3] + lined[3:4], fit
 
 
-def coadd_kernel(peers, rows, chunk, *refs):
+def coadd_kernel(peers, cap, rows, chunk, *refs):
     groups = refs[:peers]
     image_ref, inward_ref, outward_ref, cover_ref, fit_ref = refs[peers:]
     rows_dev, width = image_ref.shape
+    tiles = width // LANE
     odd = lax.axis_index(BOTH) % 2 == 1
-    places, scale, cover, fit = plan_slots([g[:, width:] for g in groups], rows, rows_dev)
+    notes = split_rows(groups, cap, tiles, tiles, 1)
+    places, scale, cover, fit = plan_slots(notes, rows, rows_dev, cap, peers)
     cover_ref[...] = cover
     fit_ref[...] = fit
     for at in range(0, width, chunk):
         cols = slice(at, at + chunk)
         value = None
-        for part, place in zip(split_rows([g[:, cols] for g in groups], rows), places):
+        for part, place in zip(split_rows(groups, cap, tiles, at // LANE, chunk // LANE), places):
             sums = dot(place, part)
             value = sums if value is None else value + sums
         value = (value * scale[:, :1]).astype(BF)
@@ -285,13 +313,12 @@
         outward_ref[:, cols] = jnp.where(odd, bottom, top)
 
 
-def coadd(groups, rows_dev, rows):
+def coadd(groups, cap, rows_dev, rows, width):
     peers = len(groups)
-    width = groups[0].shape[1] - LANE
     sd = jax.ShapeDtypeStruct
     vmem = pl.BlockSpec(memory_space=pltpu.VMEM)
     return pl.pallas_call(
-        functools.partial(coadd_kernel, peers, rows, CHUNK2),
+        functools.partial(coadd_kernel, peers, cap, rows, CHUNK2),
         in_specs=[vmem] * peers,
         out_specs=[vmem] * 5,
         out_shape=[
@@ -468,7 +495,7 @@
 def shards(
     exposure, block_dest, band_offset, col_shift, block_weight, basis_width, kernel_fit, fit_owner
 ):
-    rows_dev, _ = exposure.shape
+    rows_dev, col_count = exposure.shape
     blocks = block_dest.shape[0]
     peers = lax.axis_size("patch")
     dets = lax.axis_size("det")
@@ -507,7 +534,7 @@
     band, inner, edge = tables(basis_width, rows_dev)
     groups = [groups[s] for s in range(peers)]
     groups, band, inner, edge = lax.optimization_barrier((groups, band, inner, edge))
-    image, inward, outward, cover, fit = coadd(groups, rows_dev, rows_dev // blocks)
+    image, inward, outward, cover, fit = coadd(groups, cap, rows_dev, rows_dev // blocks, col_count)
     even = [(i, i ^ 1) for i in range(devices)]
     odd = [(i, j) for j in range(2, devices, 2) for i, j in ((j, j - 1), (j - 1, j))]
     halos = (lax.ppermute(inward, BOTH, even), lax.ppermute(outward, BOTH, odd))

time: 81 us -> 81.5 us (level)
  transfers between devices with their start and end apart: 12 -> 12, of which waited for: 6 -> 6; matrix products, arithmetic and copies ran while one was open for 0% -> 0% of each run, Pallas kernels for 14% -> 15%
where the time goes in v6:
time: 81.5 us; the launch traced here: 81.3 us
  waiting for transfers between devices  31.8 us (39%)
  starting transfers between devices  26.5 us (33%)
  Pallas kernels  19.6 us (24%)
  local copies, waits for them, and re-layouts  1.78 us (2%)
  between operations  1.58 us (2%)
    ppermute x7, waiting for transfers between devices, shards(): lax.ppermute(group, 'patch', [(i, i ^ s) for i in range(peers)])  27.6 us
    ppermute x7, starting transfers between devices, shards(): lax.ppermute(group, 'patch', [(i, i ^ s) for i in range(peers)])  15.1 us
    pallas_call x2, Pallas kernels, resample(): pl.pallas_call(functools.partial(resample_kernel, cap, peers, order, len(...  8.15 us
    ppermute x2, starting transfers between devices, shards(): halos = (lax.ppermute(inward, BOTH, even), lax.ppermute(outward, BOTH, odd))  8.01 us
    pallas_call x1, Pallas kernels, match_inner(): pl.pallas_call(functools.partial(inner_kernel, all_rows, chunk), in_specs...  6.29 us
    ppermute x2, starting transfers between devices, shards(): fit = fit + lax.ppermute(fit, 'det', [(i, i ^ span) for i in range(dets)])  3 us
    ppermute x2, waiting for transfers between devices, shards(): fit = fit + lax.ppermute(fit, 'det', [(i, i ^ span) for i in range(dets)])  2.27 us
    pallas_call x1, Pallas kernels, match_edges(): pl.pallas_call(functools.partial(edge_kernel, all_rows, rows_dev), in_spe...  2.25 us
  transfers between devices with their start and end apart: 12, of which 6 were waited for; matrix products, arithmetic and copies ran while one was open for 0% of the time, Pallas kernels for 15%

profile of v6, /device:TPU:1, one launch (start us, length us, event | category | flops | bytes accessed | tf_op | source)
XLA Modules:
  0.0 81.3 jit_solution(3069311700500510516)
XLA Ops:
  0.7 3.5 %resample.2 = (bf16[16,10624]{1,0:T(8,128)(2,1)}, bf16[16,10624]{1,0:T(8,128)(2,1)}) custom-call(s32[32]{0:T(128)} %refs_0_.2, s32[32]{0:T(128)} %refs_1_.2, f32[1,32]{1,0:T(1,128)} %bitcast.9, f32[1,32]{1,0:T(1,128)} %bitcast.11, bf16[256,4096]{1,0:T(8,128)(2,1)} %refs_4_.2), custom_call_target="tpu_custom_call" | custom-call | tf_op jit(solution)/shard_map/resample/pallas_call | solution.py:175
  4.2 5.1 %collective-permute-start.9 = (bf16[16,10624]{1,0:T(8,128)(2,1)}, bf16[16,10624]{1,0:T(8,128)(2,1)S(1)}, u32[]{:S(2)}, u32[]{:S(2)}) collective-permute-start(bf16[16,10624]{1,0:T(8,128)(2,1)} %get-tuple-element.37), channel_id=1, source_target_pairs={{0,7},{1,6},{2,5},{3,4},{4,3},{5,2},{6,1},{7,0},{8,15},{9,14},{10,... | collective-permute-start | bytes 1019912 | tf_op jit(solution)/shard_map/ppermute | solution.py:507
  9.3 0.0 collective-permute-start.7
  9.3 0.3 collective-permute-start
  10.3 1.9 %collective-permute-done = f32[1,3,6]{2,0,1:T(1,128)S(1)} collective-permute-done((f32[1,3,6]{2,0,1:T(1,128)S(1)}, f32[1,3,6]{2,0,1:T(1,128)S(1)}, u32[]{:S(2)}, u32[]{:S(2)}) %collective-permute-start) | collective-permute-done | bytes 104 | tf_op jit(solution)/shard_map/ppermute | solution.py:513
  12.2 0.1 reshape.26
  12.3 1.8 %collective-permute-start.1 = (f32[1,18]{1,0:T(1,128)S(1)}, f32[1,18]{1,0:T(1,128)S(1)}, u32[]{:S(2)}, u32[]{:S(2)}) collective-permute-start(f32[1,18]{1,0:T(1,128)S(1)} %reshape.26), channel_id=1, source_target_pairs={{0,8},{8,0},{16,24},{24,16},{1,9},{9,1},{17,25},{25,17},{2,10},{10... | collective-permute-start | bytes 224 | tf_op jit(solution)/shard_map/ppermute | solution.py:526
  14.1 0.8 %collective-permute-done.1 = f32[1,18]{1,0:T(1,128)S(1)} collective-permute-done((f32[1,18]{1,0:T(1,128)S(1)}, f32[1,18]{1,0:T(1,128)S(1)}, u32[]{:S(2)}, u32[]{:S(2)}) %collective-permute-start.1) | collective-permute-done | bytes 104 | tf_op jit(solution)/shard_map/ppermute | solution.py:526
  14.9 1.2 %collective-permute-start.2 = (f32[1,18]{1,0:T(1,128)S(1)}, f32[1,18]{1,0:T(1,128)S(1)}, u32[]{:S(2)}, u32[]{:S(2)}) collective-permute-start(f32[1,18]{1,0:T(1,128)S(1)} %add.18), channel_id=1, source_target_pairs={{0,16},{8,24},{16,0},{24,8},{1,17},{9,25},{17,1},{25,9},{2,18},{10... | collective-permute-start | bytes 224 | tf_op jit(solution)/shard_map/ppermute | solution.py:526
  16.1 1.4 %collective-permute-done.2 = f32[1,18]{1,0:T(1,128)S(1)} collective-permute-done((f32[1,18]{1,0:T(1,128)S(1)}, f32[1,18]{1,0:T(1,128)S(1)}, u32[]{:S(2)}, u32[]{:S(2)}) %collective-permute-start.2) | collective-permute-done | bytes 104 | tf_op jit(solution)/shard_map/ppermute | solution.py:526
  17.6 0.1 concatenate.4.refs_5_
  17.7 0.0 copy-start
  17.7 1.6 %copy-done = bf16[256,4096]{1,0:T(8,128)(2,1)S(1)} copy-done((bf16[256,4096]{1,0:T(8,128)(2,1)S(1)}, bf16[256,4096]{1,0:T(8,128)(2,1)}, u32[]{:S(2)}) %copy-start) | copy-done | bytes 2097176
  19.3 4.7 %resample.3 = (bf16[16,10624]{1,0:T(8,128)(2,1)S(1)}, bf16[16,10624]{1,0:T(8,128)(2,1)S(1)}, bf16[16,10624]{1,0:T(8,128)(2,1)S(1)}, bf16[16,10624]{1,0:T(8,128)(...) custom-call(s32[32]{0:T(128)S(1)} %copy-done.1, s32[32]{0:T(128)S(1)} %copy-done.2, ...), custom_call_target="tpu_custom_call" | custom-call | tf_op jit(solution)/shard_map/resample/pallas_call | solution.py:175
  24.0 0.7 collective-permute-start.3
  24.6 0.7 collective-permute-start.4
  25.3 1.4 %collective-permute-start.5 = (bf16[16,10624]{1,0:T(8,128)(2,1)S(1)}, bf16[16,10624]{1,0:T(8,128)(2,1)S(1)}, u32[]{:S(2)}, u32[]{:S(2)}) collective-permute-start(bf16[16,10624]{1,0:T(8,128)(2,1)S(1)} %get-tuple-element.49), channel_id=1, source_target_pairs={{0,3},{1,2},{2,1},{3,0},{4,7},{5,6},{6,5},{7,4},{8,11},{9,10},{10,... | collective-permute-start | bytes 1019912 | tf_op jit(solution)/shard_map/ppermute | solution.py:507
  26.7 5.2 %collective-permute-start.6 = (bf16[16,10624]{1,0:T(8,128)(2,1)S(1)}, bf16[16,10624]{1,0:T(8,128)(2,1)S(1)}, u32[]{:S(2)}, u32[]{:S(2)}) collective-permute-start(bf16[16,10624]{1,0:T(8,128)(2,1)S(1)} %get-tuple-element.50), channel_id=1, source_target_pairs={{0,4},{1,5},{2,6},{3,7},{4,0},{5,1},{6,2},{7,3},{8,12},{9,13},{10,... | collective-permute-start | bytes 1019912 | tf_op jit(solution)/shard_map/ppermute | solution.py:507
  31.9 6.2 %collective-permute-done.7.refs_5_ = bf16[16,10624]{1,0:T(8,128)(2,1)S(1)} collective-permute-done((bf16[16,10624]{1,0:T(8,128)(2,1)}, bf16[16,10624]{1,0:T(8,128)(2,1)S(1)}, u32[]{:S(2)}, u32[]{:S(2)}) %collective-permute-start.7) | collective-permute-done | bytes 340000 | tf_op jit(solution)/shard_map/ppermute | solution.py:507
  38.1 2.0 %collective-permute-start.8 = (bf16[16,10624]{1,0:T(8,128)(2,1)S(1)}, bf16[16,10624]{1,0:T(8,128)(2,1)S(1)}, u32[]{:S(2)}, u32[]{:S(2)}) collective-permute-start(bf16[16,10624]{1,0:T(8,128)(2,1)S(1)} %get-tuple-element.51), channel_id=1, source_target_pairs={{0,6},{1,7},{2,4},{3,5},{4,2},{5,3},{6,0},{7,1},{8,14},{9,15},{10,... | collective-permute-start | bytes 1019912 | tf_op jit(solution)/shard_map/ppermute | solution.py:507
  40.2 0.8 %tables.1 = (bf16[256,384]{1,0:T(8,128)(2,1)S(1)}, bf16[3,224,256]{2,1,0:T(8,128)(2,1)S(1)}, bf16[96,96]{1,0:T(8,128)(2,1)S(1)}) custom-call(f32[3]{0:T(128)S(1)} %copy-done.5), custom_call_target="tpu_custom_call" | custom-call | tf_op jit(solution)/shard_map/tables/pallas_call | solution.py:225
  41.0 0.0 collective-permute-done.3.refs_1_
  41.0 3.5 %collective-permute-done.4.refs_2_ = bf16[16,10624]{1,0:T(8,128)(2,1)S(1)} collective-permute-done((bf16[16,10624]{1,0:T(8,128)(2,1)S(1)}, bf16[16,10624]{1,0:T(8,128)(2,1)S(1)}, u32[]{:S(2)}, u32[]{:S(2)}) %collective-permute-start.4) | collective-permute-done | bytes 340000 | tf_op jit(solution)/shard_map/ppermute | solution.py:507
  44.5 17.9 %collective-permute-done.5.refs_3_ = bf16[16,10624]{1,0:T(8,128)(2,1)S(1)} collective-permute-done((bf16[16,10624]{1,0:T(8,128)(2,1)S(1)}, bf16[16,10624]{1,0:T(8,128)(2,1)S(1)}, u32[]{:S(2)}, u32[]{:S(2)}) %collective-permute-start.5) | collective-permute-done | bytes 340000 | tf_op jit(solution)/shard_map/ppermute | solution.py:507
  62.4 0.0 collective-permute-done.6.refs_4_
  62.4 0.0 collective-permute-done.8.refs_6_
  62.4 2.1 %coadd.1 = (bf16[256,4096]{1,0:T(8,128)(2,1)S(1)}, bf16[16,4096]{1,0:T(8,128)(2,1)}, bf16[16,4096]{1,0:T(8,128)(2,1)S(1)}, f32[1,32]{1,0:T(1,128)}, f32[1,128]{1,0:T(1,128)S(1)}) custom-call(bf16[16,10624]{1,0:T(8,128)(2,1)S(1)} %get-tuple-element.56.refs_0_, bf16[16,10624]{1,0:T(8,128)(2,1)S(1)} %collective-permute-done.3.refs_1_, ...), custom_call_target="tpu_custom_call" | custom-call | tf_op jit(solution)/shard_map/coadd/pallas_call | solution.py:320
  64.5 0.5 collective-permute-start.10
  65.0 7.5 %collective-permute-start.11 = (bf16[16,4096]{1,0:T(8,128)(2,1)S(1)}, bf16[16,4096]{1,0:T(8,128)(2,1)S(1)}, u32[]{:S(2)}, u32[]{:S(2)}) collective-permute-start(bf16[16,4096]{1,0:T(8,128)(2,1)S(1)} %get-tuple-element.67), channel_id=1, source_target_pairs={{2,1},{1,2},{4,3},{3,4},{6,5},{5,6},{8,7},{7,8},{10,9},{9,10},{12,... | collective-permute-start | bytes 393224 | tf_op jit(solution)/shard_map/ppermute | solution.py:540
  72.5 6.3 %match_inner.1.old_ref = bf16[256,4096]{1,0:T(8,128)(2,1)} custom-call(s32[1]{0:T(128)} %bitcast.start_ref, f32[1,128]{1,0:T(1,128)S(1)} %get-tuple-element.64.fit_ref, bf16[256,4096]{1,0:T(8,128)(2,1)S(1)} %get-tuple-element.66.image_ref, bf16[256,384]{1,0:T(8,128)(2,1)S(1)} %get-tuple-element.68.band_ref, bf16[3,224,256]{2,1,0:T(8,128)(2,1)S(1)} %get-tuple-element.70.inner_ref), custom_call_target="tpu_custom_call" | custom-call | tf_op jit(solution)/shard_map/match_inner/pallas_call | solution.py:420
  78.8 0.0 collective-permute-done.10.inward_ref
  78.9 2.2 %match_edges.1 = bf16[256,4096]{1,0:T(8,128)(2,1)} custom-call(s32[1]{0:T(128)} %bitcast.start_ref, f32[1,128]{1,0:T(1,128)S(1)} %get-tuple-element.64.fit_ref, bf16[16,4096]{1,0:T(8,128)(2,1)S(1)} %collective-permute-done.10.inward_ref, bf16[256,4096]{1,0:T(8,128)(2,1)S(1)} %get-tuple-element.66.image_ref, ...), custom_call_target="tpu_custom_call", output_to_operand_aliasing={{}: (7, {})} | custom-call | tf_op jit(solution)/shard_map/match_edges/pallas_call | solution.py:483
  (18 shorter events, 0.1 us)
Async XLA Ops:
  0.6 17.0 %copy-start.2 = (s32[32]{0:T(128)S(1)}, s32[32]{0:T(128)}, u32[]{:S(2)}) copy-start(s32[32]{0:T(128)} %refs_1_.2) | copy-start | bytes 388
  0.6 17.0 %copy-start.1 = (s32[32]{0:T(128)S(1)}, s32[32]{0:T(128)}, u32[]{:S(2)}) copy-start(s32[32]{0:T(128)} %refs_0_.2) | copy-start | bytes 388
  0.7 17.0 %copy-start.3 = (f32[32]{0:T(128)S(1)}, f32[32]{0:T(128)}, u32[]{:S(2)}) copy-start(f32[32]{0:T(128)} %param.11) | copy-start | bytes 388
  0.7 17.0 %copy-start.4 = (f32[32]{0:T(128)S(1)}, f32[32]{0:T(128)}, u32[]{:S(2)}) copy-start(f32[32]{0:T(128)} %param.12) | copy-start | bytes 388
  0.7 8.6 %copy-start.6 = (f32[1,3,6]{2,0,1:T(1,128)S(1)}, f32[1,3,6]{2,0,1:T(1,128)}, u32[]{:S(2)}) copy-start(f32[1,3,6]{2,0,1:T(1,128)} %param.14) | copy-start | bytes 220
  0.7 39.5 %copy-start.5 = (f32[3]{0:T(128)S(1)}, f32[3]{0:T(128)}, u32[]{:S(2)}) copy-start(f32[3]{0:T(128)} %width_ref) | copy-start | bytes 40
  4.2 22.5 %collective-permute-start.9 = (bf16[16,10624]{1,0:T(8,128)(2,1)}, bf16[16,10624]{1,0:T(8,128)(2,1)S(1)}, u32[]{:S(2)}, u32[]{:S(2)}) collective-permute-start(bf16[16,10624]{1,0:T(8,128)(2,1)} %get-tuple-element.37), channel_id=1, source_target_pairs={{0,7},{1,6},{2,5},{3,4},{4,3},{5,2},{6,1},{7,0},{8,15},{9,14},{10,... | collective-permute-start | bytes 1019912 | tf_op jit(solution)/shard_map/ppermute | solution.py:507
  9.3 28.8 %collective-permute-start.7 = (bf16[16,10624]{1,0:T(8,128)(2,1)}, bf16[16,10624]{1,0:T(8,128)(2,1)S(1)}, u32[]{:S(2)}, u32[]{:S(2)}) collective-permute-start(bf16[16,10624]{1,0:T(8,128)(2,1)} %get-tuple-element.38), channel_id=1, source_target_pairs={{0,5},{1,4},{2,7},{3,6},{4,1},{5,0},{6,3},{7,2},{8,13},{9,12},{10,... | collective-permute-start | bytes 1019912 | tf_op jit(solution)/shard_map/ppermute | solution.py:507
  9.3 2.9 %collective-permute-start = (f32[1,3,6]{2,0,1:T(1,128)S(1)}, f32[1,3,6]{2,0,1:T(1,128)S(1)}, u32[]{:S(2)}, u32[]{:S(2)}) collective-permute-start(f32[1,3,6]{2,0,1:T(1,128)S(1)} %copy-done.6), channel_id=1, source_target_pairs={{0,1},{1,0},{2,3},{3,2},{4,5},{5,4},{6,7},{7,6},{8,9},{9,8},{10,11... | collective-permute-start | bytes 224 | tf_op jit(solution)/shard_map/ppermute | solution.py:513
  12.3 2.6 %collective-permute-start.1 = (f32[1,18]{1,0:T(1,128)S(1)}, f32[1,18]{1,0:T(1,128)S(1)}, u32[]{:S(2)}, u32[]{:S(2)}) collective-permute-start(f32[1,18]{1,0:T(1,128)S(1)} %reshape.26), channel_id=1, source_target_pairs={{0,8},{8,0},{16,24},{24,16},{1,9},{9,1},{17,25},{25,17},{2,10},{10... | collective-permute-start | bytes 224 | tf_op jit(solution)/shard_map/ppermute | solution.py:526
  14.9 2.7 %collective-permute-start.2 = (f32[1,18]{1,0:T(1,128)S(1)}, f32[1,18]{1,0:T(1,128)S(1)}, u32[]{:S(2)}, u32[]{:S(2)}) collective-permute-start(f32[1,18]{1,0:T(1,128)S(1)} %add.18), channel_id=1, source_target_pairs={{0,16},{8,24},{16,0},{24,8},{1,17},{9,25},{17,1},{25,9},{2,18},{10... | collective-permute-start | bytes 224 | tf_op jit(solution)/shard_map/ppermute | solution.py:526
  17.7 1.6 %copy-start = (bf16[256,4096]{1,0:T(8,128)(2,1)S(1)}, bf16[256,4096]{1,0:T(8,128)(2,1)}, u32[]{:S(2)}) copy-start(bf16[256,4096]{1,0:T(8,128)(2,1)} %refs_4_.2) | copy-start | bytes 6291460
  24.0 17.0 %collective-permute-start.3 = (bf16[16,10624]{1,0:T(8,128)(2,1)S(1)}, bf16[16,10624]{1,0:T(8,128)(2,1)S(1)}, u32[]{:S(2)}, u32[]{:S(2)}) collective-permute-start(bf16[16,10624]{1,0:T(8,128)(2,1)S(1)} %get-tuple-element.47), channel_id=1, source_target_pairs={{0,1},{1,0},{2,3},{3,2},{4,5},{5,4},{6,7},{7,6},{8,9},{9,8},{10,11... | collective-permute-start | bytes 1019912 | tf_op jit(solution)/shard_map/ppermute | solution.py:507
  24.6 19.8 %collective-permute-start.4 = (bf16[16,10624]{1,0:T(8,128)(2,1)S(1)}, bf16[16,10624]{1,0:T(8,128)(2,1)S(1)}, u32[]{:S(2)}, u32[]{:S(2)}) collective-permute-start(bf16[16,10624]{1,0:T(8,128)(2,1)S(1)} %get-tuple-element.48), channel_id=1, source_target_pairs={{0,2},{1,3},{2,0},{3,1},{4,6},{5,7},{6,4},{7,5},{8,10},{9,11},{10,... | collective-permute-start | bytes 1019912 | tf_op jit(solution)/shard_map/ppermute | solution.py:507
  25.3 37.1 %collective-permute-start.5 = (bf16[16,10624]{1,0:T(8,128)(2,1)S(1)}, bf16[16,10624]{1,0:T(8,128)(2,1)S(1)}, u32[]{:S(2)}, u32[]{:S(2)}) collective-permute-start(bf16[16,10624]{1,0:T(8,128)(2,1)S(1)} %get-tuple-element.49), channel_id=1, source_target_pairs={{0,3},{1,2},{2,1},{3,0},{4,7},{5,6},{6,5},{7,4},{8,11},{9,10},{10,... | collective-permute-start | bytes 1019912 | tf_op jit(solution)/shard_map/ppermute | solution.py:507
  26.7 35.7 %collective-permute-start.6 = (bf16[16,10624]{1,0:T(8,128)(2,1)S(1)}, bf16[16,10624]{1,0:T(8,128)(2,1)S(1)}, u32[]{:S(2)}, u32[]{:S(2)}) collective-permute-start(bf16[16,10624]{1,0:T(8,128)(2,1)S(1)} %get-tuple-element.50), channel_id=1, source_target_pairs={{0,4},{1,5},{2,6},{3,7},{4,0},{5,1},{6,2},{7,3},{8,12},{9,13},{10,... | collective-permute-start | bytes 1019912 | tf_op jit(solution)/shard_map/ppermute | solution.py:507
  38.1 24.3 %collective-permute-start.8 = (bf16[16,10624]{1,0:T(8,128)(2,1)S(1)}, bf16[16,10624]{1,0:T(8,128)(2,1)S(1)}, u32[]{:S(2)}, u32[]{:S(2)}) collective-permute-start(bf16[16,10624]{1,0:T(8,128)(2,1)S(1)} %get-tuple-element.51), channel_id=1, source_target_pairs={{0,6},{1,7},{2,4},{3,5},{4,2},{5,3},{6,0},{7,1},{8,14},{9,15},{10,... | collective-permute-start | bytes 1019912 | tf_op jit(solution)/shard_map/ppermute | solution.py:507
  64.5 14.3 %collective-permute-start.10 = (bf16[16,4096]{1,0:T(8,128)(2,1)}, bf16[16,4096]{1,0:T(8,128)(2,1)S(1)}, u32[]{:S(2)}, u32[]{:S(2)}) collective-permute-start(bf16[16,4096]{1,0:T(8,128)(2,1)} %get-tuple-element.65), channel_id=1, source_target_pairs={{0,1},{1,0},{2,3},{3,2},{4,5},{5,4},{6,7},{7,6},{8,9},{9,8},{10,11... | collective-permute-start | bytes 393224 | tf_op jit(solution)/shard_map/ppermute | solution.py:540
  65.0 13.8 %collective-permute-start.11 = (bf16[16,4096]{1,0:T(8,128)(2,1)S(1)}, bf16[16,4096]{1,0:T(8,128)(2,1)S(1)}, u32[]{:S(2)}, u32[]{:S(2)}) collective-permute-start(bf16[16,4096]{1,0:T(8,128)(2,1)S(1)} %get-tuple-element.67), channel_id=1, source_target_pairs={{2,1},{1,2},{4,3},{3,4},{6,5},{5,6},{8,7},{7,8},{10,9},{9,10},{12,... | collective-permute-start | bytes 393224 | tf_op jit(solution)/shard_map/ppermute | solution.py:540

commit v7 on v6

--- a/solution.py
+++ b/solution.py
@@ -92,8 +92,10 @@
             fit_note = jnp.where(line == i, part, fit_note)
     copies[0].wait()
 
+    noted = {}
+
     def one_pair(slots):
-        xs, bands, notes = [], [], []
+        xs, bands = [], []
         for group, rank in slots:
             got = src_ref[group * cap + rank]
             valid = got >= 0
@@ -112,7 +114,7 @@
             note = jnp.where(lane == 0, slot, 0.0)
             for i, part in enumerate(three(jnp.broadcast_to(weight, (rows, LANE)))):
                 note = jnp.where(lane == i + 1, part, note)
-            notes.append(note + fit_note if rank == 0 else note)
+            noted[group] = jnp.where(line == rank, note, noted.get(group, 0.0))
         x16 = jnp.concatenate(xs, axis=0).astype(BF)
         padded = jnp.concatenate([zero, x16, zero], axis=1)
         windows = jnp.concatenate(
@@ -130,18 +132,15 @@
         last = piece(tiles)
         tops[0] = jnp.where(lane < SHIFT, last[0], tops[0])
         bottoms[0] = jnp.where(lane < SHIFT, last[1], bottoms[0])
-        tops.append(notes[0])
-        bottoms.append(notes[1])
         (group0, rank0), (group1, rank1) = slots
         if group0 == group1:
-            for t in range(tiles + 1):
-                put(group0, rank0 // 2 * (tiles + 1) + t, tops[t], bottoms[t])
+            for t in range(tiles):
+                put(group0, rank0 // 2 * tiles + t, tops[t], bottoms[t])
         else:
-            half = tiles // 2 + 1
+            half = tiles // 2
             for group, pieces in ((group0, tops), (group1, bottoms)):
-                pieces = pieces + [jnp.zeros((rows, LANE), F32)] * (2 * half - len(pieces))
                 for t in range(half):
-                    put(group, cap // 2 * (tiles + 1) + t, pieces[t], pieces[t + half])
+                    put(group, cap // 2 * tiles + t, pieces[t], pieces[t + half])
 
     def put(group, tile, top, bottom):
         made_ref[order.index(group), :, LANE * tile : LANE * (tile + 1)] = jnp.concatenate(
@@ -156,6 +155,8 @@
                 one_pair([(group, rank), (group, rank + 1)])
         if cap % 2:
             one_pair([(two[0], cap - 1), (two[1], cap - 1)])
+        for group in two:
+            put(group, made_ref.shape[2] // LANE - 1, noted[group], fit_note)
         for i in range(2):
             sends[at + i].start()
     for send in sends:
@@ -164,7 +165,7 @@
 
 def message_shape(cap, rows, width):
     tiles = width // LANE
-    return 2 * rows, LANE * (cap // 2 * (tiles + 1) + cap % 2 * (tiles // 2 + 1))
+    return 2 * rows, LANE * (cap // 2 * tiles + cap % 2 * (tiles // 2) + 1)
 
 
 def resample(exposure, dest, offset, shift, weight, fit, peers, cap, order):
@@ -237,12 +238,12 @@
 
 def split_rows(groups, cap, tiles, first, count):
     parts = []
-    at = [LANE * (pair * (tiles + 1) + first) for pair in range(cap // 2)]
+    at = [LANE * (pair * tiles + first) for pair in range(cap // 2)]
     if at:
         pairs = [g[:, a : a + LANE * count] for g in groups for a in at]
         parts.append(jnp.concatenate(pairs, axis=0))
     if cap % 2:
-        half, base = tiles // 2 + 1, cap // 2 * (tiles + 1)
+        half, base = tiles // 2, cap // 2 * tiles
         upper, lower = max(0, min(half, first + count) - first), max(0, first + count - max(first, half))
         alone = []
         for g in groups:
@@ -260,33 +261,33 @@
 
 
 def plan_slots(notes, rows, rows_dev, cap, peers):
-    slots = rows_dev // rows
-    size = cap // 2 * 2 * rows
+    slots, size = rows_dev // rows, 2 * rows
     fit = sum(
-        notes[0][size * g + i : size * g + i + 1].astype(F32) for g in range(0, peers, 2) for i in range(3)
-    )
-    places, column, lined = [], None, None
-    for part in notes:
-        count = part.shape[0]
-        slot = part[:, :1].astype(F32)
-        across = jnp.broadcast_to(slot, (count, LANE)).T[:1].astype(jnp.int32)
-        row = lax.broadcasted_iota(jnp.int32, (rows_dev, 1), 0)
-        lane = lax.broadcasted_iota(jnp.int32, (1, count), 1)
-        match = (across == row // rows) & (lane % rows == row % rows)
-        place = jnp.where(match, 1.0, 0.0).astype(BF)
-        sums = dot(place, part)
-        column = sums if column is None else column + sums
-        places.append(place)
-        source = lax.broadcasted_iota(jnp.int32, (count, 1), 0)
-        index = lax.broadcasted_iota(jnp.int32, (1, slots), 1)
-        match = (slot.astype(jnp.int32) == index) & (source % rows == 0)
-        sums = lax.dot_general(
-            part, jnp.where(match, 1.0, 0.0).astype(BF), (((0,), (0,)), ((), ())),
-            preferred_element_type=F32,
-        )
-        lined = sums if lined is None else lined + sums
-    cover = column[:, 1:2] + column[:, 2:3] + column[:, 3:4]
+        notes[size * g + rows + i : size * g + rows + i + 1].astype(F32)
+        for g in range(0, peers, 2)
+        for i in range(3)
+    )
+    spread = lambda at: lax.dot_general(
+        notes, jnp.where(at, 1.0, 0.0).astype(BF), (((0,), (0,)), ((), ())), preferred_element_type=F32
+    )
+    source = lax.broadcasted_iota(jnp.int32, (size * peers, 1), 0)
+    row = lax.broadcasted_iota(jnp.int32, (rows_dev, 1), 0)
+    even = cap // 2 * 2
+    places, cover = [], 0.0
+    for first, held in ((0, even), (even, cap - even)):
+        if not held:
+            continue
+        lane = lax.broadcasted_iota(jnp.int32, (1, peers * held * rows), 1)
+        block = lane // rows
+        told = spread(source == block // held * size + first + block % held)
+        match = (told[:1].astype(jnp.int32) == row // rows) & (lane % rows == row % rows)
+        places.append(jnp.where(match, 1.0, 0.0).astype(BF))
+        weight = told[1:2] + told[2:3] + told[3:4]
+        cover = cover + jnp.sum(jnp.where(match, weight, 0.0), axis=1, keepdims=True)
     scale = jnp.broadcast_to(1.0 / jnp.maximum(cover, 1.0), (rows_dev, LANE))
+    index = lax.broadcasted_iota(jnp.int32, (1, slots), 1)
+    mine = (notes[:, :1].astype(F32).astype(jnp.int32) == index) & (source % size < cap)
+    lined = spread(mine)
     return places, scale, lined[1:2] + lined[2:3] + lined[3:4], fit
 
 
@@ -296,7 +297,7 @@
     rows_dev, width = image_ref.shape
     tiles = width // LANE
     odd = lax.axis_index(BOTH) % 2 == 1
-    notes = split_rows(groups, cap, tiles, tiles, 1)
+    notes = jnp.concatenate([g[:, g.shape[1] - LANE :] for g in groups], axis=0)
     places, scale, cover, fit = plan_slots(notes, rows, rows_dev, cap, peers)
     cover_ref[...] = cover
     fit_ref[...] = fit

time: 81.5 us -> 80.5 us (0.988)
  no operation moved by 1% of the time
where the time goes in v7:
time: 80.5 us; the launch traced here: 80.3 us
  waiting for transfers between devices  31.4 us (39%)
  starting transfers between devices  26 us (32%)
  Pallas kernels  19.5 us (24%)
  local copies, waits for them, and re-layouts  1.78 us (2%)
  between operations  1.58 us (2%)
    ppermute x7, waiting for transfers between devices, shards(): lax.ppermute(group, 'patch', [(i, i ^ s) for i in range(peers)])  27.2 us
    ppermute x7, starting transfers between devices, shards(): lax.ppermute(group, 'patch', [(i, i ^ s) for i in range(peers)])  14.7 us
    pallas_call x2, Pallas kernels, resample(): pl.pallas_call(functools.partial(resample_kernel, cap, peers, order, len(...  8.1 us
    ppermute x2, starting transfers between devices, shards(): halos = (lax.ppermute(inward, BOTH, even), lax.ppermute(outward, BOTH, odd))  7.99 us
    pallas_call x1, Pallas kernels, match_inner(): pl.pallas_call(functools.partial(inner_kernel, all_rows, chunk), in_specs...  6.29 us
    ppermute x2, starting transfers between devices, shards(): fit = fit + lax.ppermute(fit, 'det', [(i, i ^ span) for i in range(dets)])  2.99 us
    ppermute x2, waiting for transfers between devices, shards(): fit = fit + lax.ppermute(fit, 'det', [(i, i ^ span) for i in range(dets)])  2.27 us
    pallas_call x1, Pallas kernels, match_edges(): pl.pallas_call(functools.partial(edge_kernel, all_rows, rows_dev), in_spe...  2.25 us
  transfers between devices with their start and end apart: 12, of which 6 were waited for; matrix products, arithmetic and copies ran while one was open for 0% of the time, Pallas kernels for 15%

profile of v7, /device:TPU:1, one launch (start us, length us, event | category | flops | bytes accessed | tf_op | source)
XLA Modules:
  0.0 80.3 jit_solution(14788765793871891988)
XLA Ops:
  0.7 3.5 %resample.2 = (bf16[16,10368]{1,0:T(8,128)(2,1)}, bf16[16,10368]{1,0:T(8,128)(2,1)}) custom-call(s32[32]{0:T(128)} %refs_0_.2, s32[32]{0:T(128)} %refs_1_.2, f32[1,32]{1,0:T(1,128)} %bitcast.9, f32[1,32]{1,0:T(1,128)} %bitcast.11, bf16[256,4096]{1,0:T(8,128)(2,1)} %refs_4_.2), custom_call_target="tpu_custom_call" | custom-call | tf_op jit(solution)/shard_map/resample/pallas_call | solution.py:176
  4.2 5.1 %collective-permute-start.9 = (bf16[16,10368]{1,0:T(8,128)(2,1)}, bf16[16,10368]{1,0:T(8,128)(2,1)S(1)}, u32[]{:S(2)}, u32[]{:S(2)}) collective-permute-start(bf16[16,10368]{1,0:T(8,128)(2,1)} %get-tuple-element.37), channel_id=1, source_target_pairs={{0,7},{1,6},{2,5},{3,4},{4,3},{5,2},{6,1},{7,0},{8,15},{9,14},{10,... | collective-permute-start | bytes 995336 | tf_op jit(solution)/shard_map/ppermute | solution.py:508
  9.3 0.0 collective-permute-start.7
  9.3 0.3 collective-permute-start
  10.3 1.9 %collective-permute-done = f32[1,3,6]{2,0,1:T(1,128)S(1)} collective-permute-done((f32[1,3,6]{2,0,1:T(1,128)S(1)}, f32[1,3,6]{2,0,1:T(1,128)S(1)}, u32[]{:S(2)}, u32[]{:S(2)}) %collective-permute-start) | collective-permute-done | bytes 104 | tf_op jit(solution)/shard_map/ppermute | solution.py:514
  12.2 0.1 reshape.26
  12.3 1.8 %collective-permute-start.1 = (f32[1,18]{1,0:T(1,128)S(1)}, f32[1,18]{1,0:T(1,128)S(1)}, u32[]{:S(2)}, u32[]{:S(2)}) collective-permute-start(f32[1,18]{1,0:T(1,128)S(1)} %reshape.26), channel_id=1, source_target_pairs={{0,8},{8,0},{16,24},{24,16},{1,9},{9,1},{17,25},{25,17},{2,10},{10... | collective-permute-start | bytes 224 | tf_op jit(solution)/shard_map/ppermute | solution.py:527
  14.1 0.8 %collective-permute-done.1 = f32[1,18]{1,0:T(1,128)S(1)} collective-permute-done((f32[1,18]{1,0:T(1,128)S(1)}, f32[1,18]{1,0:T(1,128)S(1)}, u32[]{:S(2)}, u32[]{:S(2)}) %collective-permute-start.1) | collective-permute-done | bytes 104 | tf_op jit(solution)/shard_map/ppermute | solution.py:527
  14.9 1.2 %collective-permute-start.2 = (f32[1,18]{1,0:T(1,128)S(1)}, f32[1,18]{1,0:T(1,128)S(1)}, u32[]{:S(2)}, u32[]{:S(2)}) collective-permute-start(f32[1,18]{1,0:T(1,128)S(1)} %add.18), channel_id=1, source_target_pairs={{0,16},{8,24},{16,0},{24,8},{1,17},{9,25},{17,1},{25,9},{2,18},{10... | collective-permute-start | bytes 224 | tf_op jit(solution)/shard_map/ppermute | solution.py:527
  16.1 1.4 %collective-permute-done.2 = f32[1,18]{1,0:T(1,128)S(1)} collective-permute-done((f32[1,18]{1,0:T(1,128)S(1)}, f32[1,18]{1,0:T(1,128)S(1)}, u32[]{:S(2)}, u32[]{:S(2)}) %collective-permute-start.2) | collective-permute-done | bytes 104 | tf_op jit(solution)/shard_map/ppermute | solution.py:527
  17.6 0.1 concatenate.4.refs_5_
  17.7 0.0 copy-start
  17.7 1.6 %copy-done = bf16[256,4096]{1,0:T(8,128)(2,1)S(1)} copy-done((bf16[256,4096]{1,0:T(8,128)(2,1)S(1)}, bf16[256,4096]{1,0:T(8,128)(2,1)}, u32[]{:S(2)}) %copy-start) | copy-done | bytes 2097176
  19.3 4.6 %resample.3 = (bf16[16,10368]{1,0:T(8,128)(2,1)S(1)}, bf16[16,10368]{1,0:T(8,128)(2,1)S(1)}, bf16[16,10368]{1,0:T(8,128)(2,1)S(1)}, bf16[16,10368]{1,0:T(8,128)(...) custom-call(s32[32]{0:T(128)S(1)} %copy-done.1, s32[32]{0:T(128)S(1)} %copy-done.2, ...), custom_call_target="tpu_custom_call" | custom-call | tf_op jit(solution)/shard_map/resample/pallas_call | solution.py:176
  23.9 0.7 collective-permute-start.3
  24.6 0.7 collective-permute-start.4
  25.3 1.4 %collective-permute-start.5 = (bf16[16,10368]{1,0:T(8,128)(2,1)S(1)}, bf16[16,10368]{1,0:T(8,128)(2,1)S(1)}, u32[]{:S(2)}, u32[]{:S(2)}) collective-permute-start(bf16[16,10368]{1,0:T(8,128)(2,1)S(1)} %get-tuple-element.49), channel_id=1, source_target_pairs={{0,3},{1,2},{2,1},{3,0},{4,7},{5,6},{6,5},{7,4},{8,11},{9,10},{10,... | collective-permute-start | bytes 995336 | tf_op jit(solution)/shard_map/ppermute | solution.py:508
  26.6 0.0 collective-permute-done.9.refs_7_
  26.6 4.8 %collective-permute-start.6 = (bf16[16,10368]{1,0:T(8,128)(2,1)S(1)}, bf16[16,10368]{1,0:T(8,128)(2,1)S(1)}, u32[]{:S(2)}, u32[]{:S(2)}) collective-permute-start(bf16[16,10368]{1,0:T(8,128)(2,1)S(1)} %get-tuple-element.50), channel_id=1, source_target_pairs={{0,4},{1,5},{2,6},{3,7},{4,0},{5,1},{6,2},{7,3},{8,12},{9,13},{10,... | collective-permute-start | bytes 995336 | tf_op jit(solution)/shard_map/ppermute | solution.py:508
  31.4 6.0 %collective-permute-done.7.refs_5_ = bf16[16,10368]{1,0:T(8,128)(2,1)S(1)} collective-permute-done((bf16[16,10368]{1,0:T(8,128)(2,1)}, bf16[16,10368]{1,0:T(8,128)(2,1)S(1)}, u32[]{:S(2)}, u32[]{:S(2)}) %collective-permute-start.7) | collective-permute-done | bytes 331808 | tf_op jit(solution)/shard_map/ppermute | solution.py:508
  37.4 2.0 %collective-permute-start.8 = (bf16[16,10368]{1,0:T(8,128)(2,1)S(1)}, bf16[16,10368]{1,0:T(8,128)(2,1)S(1)}, u32[]{:S(2)}, u32[]{:S(2)}) collective-permute-start(bf16[16,10368]{1,0:T(8,128)(2,1)S(1)} %get-tuple-element.51), channel_id=1, source_target_pairs={{0,6},{1,7},{2,4},{3,5},{4,2},{5,3},{6,0},{7,1},{8,14},{9,15},{10,... | collective-permute-start | bytes 995336 | tf_op jit(solution)/shard_map/ppermute | solution.py:508
  39.5 0.8 %tables.1 = (bf16[256,384]{1,0:T(8,128)(2,1)S(1)}, bf16[3,224,256]{2,1,0:T(8,128)(2,1)S(1)}, bf16[96,96]{1,0:T(8,128)(2,1)S(1)}) custom-call(f32[3]{0:T(128)S(1)} %copy-done.5), custom_call_target="tpu_custom_call" | custom-call | tf_op jit(solution)/shard_map/tables/pallas_call | solution.py:226
  40.3 0.0 collective-permute-done.3.refs_1_
  40.3 4.3 %collective-permute-done.4.refs_2_ = bf16[16,10368]{1,0:T(8,128)(2,1)S(1)} collective-permute-done((bf16[16,10368]{1,0:T(8,128)(2,1)S(1)}, bf16[16,10368]{1,0:T(8,128)(2,1)S(1)}, u32[]{:S(2)}, u32[]{:S(2)}) %collective-permute-start.4) | collective-permute-done | bytes 331808 | tf_op jit(solution)/shard_map/ppermute | solution.py:508
  44.6 16.9 %collective-permute-done.5.refs_3_ = bf16[16,10368]{1,0:T(8,128)(2,1)S(1)} collective-permute-done((bf16[16,10368]{1,0:T(8,128)(2,1)S(1)}, bf16[16,10368]{1,0:T(8,128)(2,1)S(1)}, u32[]{:S(2)}, u32[]{:S(2)}) %collective-permute-start.5) | collective-permute-done | bytes 331808 | tf_op jit(solution)/shard_map/ppermute | solution.py:508
  61.5 0.0 collective-permute-done.6.refs_4_
  61.5 0.0 collective-permute-done.8.refs_6_
  61.5 2.1 %coadd.1 = (bf16[256,4096]{1,0:T(8,128)(2,1)S(1)}, bf16[16,4096]{1,0:T(8,128)(2,1)}, bf16[16,4096]{1,0:T(8,128)(2,1)S(1)}, f32[1,32]{1,0:T(1,128)}, f32[1,128]{1,0:T(1,128)S(1)}) custom-call(bf16[16,10368]{1,0:T(8,128)(2,1)S(1)} %get-tuple-element.56.refs_0_, bf16[16,10368]{1,0:T(8,128)(2,1)S(1)} %collective-permute-done.3.refs_1_, ...), custom_call_target="tpu_custom_call" | custom-call | tf_op jit(solution)/shard_map/coadd/pallas_call | solution.py:321
  63.6 0.6 collective-permute-start.10
  64.1 7.4 %collective-permute-start.11 = (bf16[16,4096]{1,0:T(8,128)(2,1)S(1)}, bf16[16,4096]{1,0:T(8,128)(2,1)S(1)}, u32[]{:S(2)}, u32[]{:S(2)}) collective-permute-start(bf16[16,4096]{1,0:T(8,128)(2,1)S(1)} %get-tuple-element.67), channel_id=1, source_target_pairs={{2,1},{1,2},{4,3},{3,4},{6,5},{5,6},{8,7},{7,8},{10,9},{9,10},{12,... | collective-permute-start | bytes 393224 | tf_op jit(solution)/shard_map/ppermute | solution.py:541
  71.6 6.3 %match_inner.1.old_ref = bf16[256,4096]{1,0:T(8,128)(2,1)} custom-call(s32[1]{0:T(128)} %bitcast.start_ref, f32[1,128]{1,0:T(1,128)S(1)} %get-tuple-element.64.fit_ref, bf16[256,4096]{1,0:T(8,128)(2,1)S(1)} %get-tuple-element.66.image_ref, bf16[256,384]{1,0:T(8,128)(2,1)S(1)} %get-tuple-element.68.band_ref, bf16[3,224,256]{2,1,0:T(8,128)(2,1)S(1)} %get-tuple-element.70.inner_ref), custom_call_target="tpu_custom_call" | custom-call | tf_op jit(solution)/shard_map/match_inner/pallas_call | solution.py:421
  77.9 2.2 %match_edges.1 = bf16[256,4096]{1,0:T(8,128)(2,1)} custom-call(s32[1]{0:T(128)} %bitcast.start_ref, f32[1,128]{1,0:T(1,128)S(1)} %get-tuple-element.64.fit_ref, bf16[16,4096]{1,0:T(8,128)(2,1)S(1)} %collective-permute-done.10.inward_ref, bf16[256,4096]{1,0:T(8,128)(2,1)S(1)} %get-tuple-element.66.image_ref, ...), custom_call_target="tpu_custom_call", output_to_operand_aliasing={{}: (7, {})} | custom-call | tf_op jit(solution)/shard_map/match_edges/pallas_call | solution.py:484
  (18 shorter events, 0.1 us)
Async XLA Ops:
  0.6 17.0 %copy-start.2 = (s32[32]{0:T(128)S(1)}, s32[32]{0:T(128)}, u32[]{:S(2)}) copy-start(s32[32]{0:T(128)} %refs_1_.2) | copy-start | bytes 388
  0.6 17.0 %copy-start.1 = (s32[32]{0:T(128)S(1)}, s32[32]{0:T(128)}, u32[]{:S(2)}) copy-start(s32[32]{0:T(128)} %refs_0_.2) | copy-start | bytes 388
  0.7 17.0 %copy-start.3 = (f32[32]{0:T(128)S(1)}, f32[32]{0:T(128)}, u32[]{:S(2)}) copy-start(f32[32]{0:T(128)} %param.11) | copy-start | bytes 388
  0.7 17.0 %copy-start.4 = (f32[32]{0:T(128)S(1)}, f32[32]{0:T(128)}, u32[]{:S(2)}) copy-start(f32[32]{0:T(128)} %param.12) | copy-start | bytes 388
  0.7 8.6 %copy-start.6 = (f32[1,3,6]{2,0,1:T(1,128)S(1)}, f32[1,3,6]{2,0,1:T(1,128)}, u32[]{:S(2)}) copy-start(f32[1,3,6]{2,0,1:T(1,128)} %param.14) | copy-start | bytes 220
  0.7 38.8 %copy-start.5 = (f32[3]{0:T(128)S(1)}, f32[3]{0:T(128)}, u32[]{:S(2)}) copy-start(f32[3]{0:T(128)} %width_ref) | copy-start | bytes 40
  4.2 22.5 %collective-permute-start.9 = (bf16[16,10368]{1,0:T(8,128)(2,1)}, bf16[16,10368]{1,0:T(8,128)(2,1)S(1)}, u32[]{:S(2)}, u32[]{:S(2)}) collective-permute-start(bf16[16,10368]{1,0:T(8,128)(2,1)} %get-tuple-element.37), channel_id=1, source_target_pairs={{0,7},{1,6},{2,5},{3,4},{4,3},{5,2},{6,1},{7,0},{8,15},{9,14},{10,... | collective-permute-start | bytes 995336 | tf_op jit(solution)/shard_map/ppermute | solution.py:508
  9.3 28.1 %collective-permute-start.7 = (bf16[16,10368]{1,0:T(8,128)(2,1)}, bf16[16,10368]{1,0:T(8,128)(2,1)S(1)}, u32[]{:S(2)}, u32[]{:S(2)}) collective-permute-start(bf16[16,10368]{1,0:T(8,128)(2,1)} %get-tuple-element.38), channel_id=1, source_target_pairs={{0,5},{1,4},{2,7},{3,6},{4,1},{5,0},{6,3},{7,2},{8,13},{9,12},{10,... | collective-permute-start | bytes 995336 | tf_op jit(solution)/shard_map/ppermute | solution.py:508
  9.3 2.9 %collective-permute-start = (f32[1,3,6]{2,0,1:T(1,128)S(1)}, f32[1,3,6]{2,0,1:T(1,128)S(1)}, u32[]{:S(2)}, u32[]{:S(2)}) collective-permute-start(f32[1,3,6]{2,0,1:T(1,128)S(1)} %copy-done.6), channel_id=1, source_target_pairs={{0,1},{1,0},{2,3},{3,2},{4,5},{5,4},{6,7},{7,6},{8,9},{9,8},{10,11... | collective-permute-start | bytes 224 | tf_op jit(solution)/shard_map/ppermute | solution.py:514
  12.3 2.6 %collective-permute-start.1 = (f32[1,18]{1,0:T(1,128)S(1)}, f32[1,18]{1,0:T(1,128)S(1)}, u32[]{:S(2)}, u32[]{:S(2)}) collective-permute-start(f32[1,18]{1,0:T(1,128)S(1)} %reshape.26), channel_id=1, source_target_pairs={{0,8},{8,0},{16,24},{24,16},{1,9},{9,1},{17,25},{25,17},{2,10},{10... | collective-permute-start | bytes 224 | tf_op jit(solution)/shard_map/ppermute | solution.py:527
  14.9 2.7 %collective-permute-start.2 = (f32[1,18]{1,0:T(1,128)S(1)}, f32[1,18]{1,0:T(1,128)S(1)}, u32[]{:S(2)}, u32[]{:S(2)}) collective-permute-start(f32[1,18]{1,0:T(1,128)S(1)} %add.18), channel_id=1, source_target_pairs={{0,16},{8,24},{16,0},{24,8},{1,17},{9,25},{17,1},{25,9},{2,18},{10... | collective-permute-start | bytes 224 | tf_op jit(solution)/shard_map/ppermute | solution.py:527
  17.7 1.6 %copy-start = (bf16[256,4096]{1,0:T(8,128)(2,1)S(1)}, bf16[256,4096]{1,0:T(8,128)(2,1)}, u32[]{:S(2)}) copy-start(bf16[256,4096]{1,0:T(8,128)(2,1)} %refs_4_.2) | copy-start | bytes 6291460
  23.9 16.4 %collective-permute-start.3 = (bf16[16,10368]{1,0:T(8,128)(2,1)S(1)}, bf16[16,10368]{1,0:T(8,128)(2,1)S(1)}, u32[]{:S(2)}, u32[]{:S(2)}) collective-permute-start(bf16[16,10368]{1,0:T(8,128)(2,1)S(1)} %get-tuple-element.47), channel_id=1, source_target_pairs={{0,1},{1,0},{2,3},{3,2},{4,5},{5,4},{6,7},{7,6},{8,9},{9,8},{10,11... | collective-permute-start | bytes 995336 | tf_op jit(solution)/shard_map/ppermute | solution.py:508
  24.6 20.0 %collective-permute-start.4 = (bf16[16,10368]{1,0:T(8,128)(2,1)S(1)}, bf16[16,10368]{1,0:T(8,128)(2,1)S(1)}, u32[]{:S(2)}, u32[]{:S(2)}) collective-permute-start(bf16[16,10368]{1,0:T(8,128)(2,1)S(1)} %get-tuple-element.48), channel_id=1, source_target_pairs={{0,2},{1,3},{2,0},{3,1},{4,6},{5,7},{6,4},{7,5},{8,10},{9,11},{10,... | collective-permute-start | bytes 995336 | tf_op jit(solution)/shard_map/ppermute | solution.py:508
  25.3 36.2 %collective-permute-start.5 = (bf16[16,10368]{1,0:T(8,128)(2,1)S(1)}, bf16[16,10368]{1,0:T(8,128)(2,1)S(1)}, u32[]{:S(2)}, u32[]{:S(2)}) collective-permute-start(bf16[16,10368]{1,0:T(8,128)(2,1)S(1)} %get-tuple-element.49), channel_id=1, source_target_pairs={{0,3},{1,2},{2,1},{3,0},{4,7},{5,6},{6,5},{7,4},{8,11},{9,10},{10,... | collective-permute-start | bytes 995336 | tf_op jit(solution)/shard_map/ppermute | solution.py:508
  26.6 34.8 %collective-permute-start.6 = (bf16[16,10368]{1,0:T(8,128)(2,1)S(1)}, bf16[16,10368]{1,0:T(8,128)(2,1)S(1)}, u32[]{:S(2)}, u32[]{:S(2)}) collective-permute-start(bf16[16,10368]{1,0:T(8,128)(2,1)S(1)} %get-tuple-element.50), channel_id=1, source_target_pairs={{0,4},{1,5},{2,6},{3,7},{4,0},{5,1},{6,2},{7,3},{8,12},{9,13},{10,... | collective-permute-start | bytes 995336 | tf_op jit(solution)/shard_map/ppermute | solution.py:508
  37.4 24.1 %collective-permute-start.8 = (bf16[16,10368]{1,0:T(8,128)(2,1)S(1)}, bf16[16,10368]{1,0:T(8,128)(2,1)S(1)}, u32[]{:S(2)}, u32[]{:S(2)}) collective-permute-start(bf16[16,10368]{1,0:T(8,128)(2,1)S(1)} %get-tuple-element.51), channel_id=1, source_target_pairs={{0,6},{1,7},{2,4},{3,5},{4,2},{5,3},{6,0},{7,1},{8,14},{9,15},{10,... | collective-permute-start | bytes 995336 | tf_op jit(solution)/shard_map/ppermute | solution.py:508
  63.6 14.3 %collective-permute-start.10 = (bf16[16,4096]{1,0:T(8,128)(2,1)}, bf16[16,4096]{1,0:T(8,128)(2,1)S(1)}, u32[]{:S(2)}, u32[]{:S(2)}) collective-permute-start(bf16[16,4096]{1,0:T(8,128)(2,1)} %get-tuple-element.65), channel_id=1, source_target_pairs={{0,1},{1,0},{2,3},{3,2},{4,5},{5,4},{6,7},{7,6},{8,9},{9,8},{10,11... | collective-permute-start | bytes 393224 | tf_op jit(solution)/shard_map/ppermute | solution.py:541
  64.1 13.7 %collective-permute-start.11 = (bf16[16,4096]{1,0:T(8,128)(2,1)S(1)}, bf16[16,4096]{1,0:T(8,128)(2,1)S(1)}, u32[]{:S(2)}, u32[]{:S(2)}) collective-permute-start(bf16[16,4096]{1,0:T(8,128)(2,1)S(1)} %get-tuple-element.67), channel_id=1, source_target_pairs={{2,1},{1,2},{4,3},{3,4},{6,5},{5,6},{8,7},{7,8},{10,9},{9,10},{12,... | collective-permute-start | bytes 393224 | tf_op jit(solution)/shard_map/ppermute | solution.py:541

commit v8 on v7

--- a/solution.py
+++ b/solution.py
@@ -23,7 +23,7 @@
 SMALL_VMEM, MATCH_VMEM = 24 * MIB, 32 * MIB
 ROW0 = 96
 FIT0 = 32
-CHUNK2 = 2048
+CHUNK2 = 4096
 CHUNK3 = 2048
 
 

time: 80.5 us -> 80.5 us (level)
  no operation moved by 1% of the time
where the time goes in v8:
time: 80.5 us; the launch traced here: 80.3 us
  waiting for transfers between devices  31.4 us (39%)
  starting transfers between devices  26 us (32%)
  Pallas kernels  19.6 us (24%)
  local copies, waits for them, and re-layouts  1.78 us (2%)
  between operations  1.58 us (2%)
    ppermute x7, waiting for transfers between devices, shards(): lax.ppermute(group, 'patch', [(i, i ^ s) for i in range(peers)])  27.2 us
    ppermute x7, starting transfers between devices, shards(): lax.ppermute(group, 'patch', [(i, i ^ s) for i in range(peers)])  14.7 us
    pallas_call x2, Pallas kernels, resample(): pl.pallas_call(functools.partial(resample_kernel, cap, peers, order, len(...  8.1 us
    ppermute x2, starting transfers between devices, shards(): halos = (lax.ppermute(inward, BOTH, even), lax.ppermute(outward, BOTH, odd))  7.99 us
    pallas_call x1, Pallas kernels, match_inner(): pl.pallas_call(functools.partial(inner_kernel, all_rows, chunk), in_specs...  6.29 us
    ppermute x2, starting transfers between devices, shards(): fit = fit + lax.ppermute(fit, 'det', [(i, i ^ span) for i in range(dets)])  2.99 us
    ppermute x2, waiting for transfers between devices, shards(): fit = fit + lax.ppermute(fit, 'det', [(i, i ^ span) for i in range(dets)])  2.27 us
    pallas_call x1, Pallas kernels, match_edges(): pl.pallas_call(functools.partial(edge_kernel, all_rows, rows_dev), in_spe...  2.25 us
  transfers between devices with their start and end apart: 12, of which 6 were waited for; matrix products, arithmetic and copies ran while one was open for 0% of the time, Pallas kernels for 15%

profile of v8, /device:TPU:1, one launch (start us, length us, event | category | flops | bytes accessed | tf_op | source)
XLA Modules:
  0.0 80.3 jit_solution(14488466991180381647)
XLA Ops:
  0.7 3.5 %resample.2 = (bf16[16,10368]{1,0:T(8,128)(2,1)}, bf16[16,10368]{1,0:T(8,128)(2,1)}) custom-call(s32[32]{0:T(128)} %refs_0_.2, s32[32]{0:T(128)} %refs_1_.2, f32[1,32]{1,0:T(1,128)} %bitcast.9, f32[1,32]{1,0:T(1,128)} %bitcast.11, bf16[256,4096]{1,0:T(8,128)(2,1)} %refs_4_.2), custom_call_target="tpu_custom_call" | custom-call | tf_op jit(solution)/shard_map/resample/pallas_call | solution.py:176
  4.2 5.1 %collective-permute-start.9 = (bf16[16,10368]{1,0:T(8,128)(2,1)}, bf16[16,10368]{1,0:T(8,128)(2,1)S(1)}, u32[]{:S(2)}, u32[]{:S(2)}) collective-permute-start(bf16[16,10368]{1,0:T(8,128)(2,1)} %get-tuple-element.37), channel_id=1, source_target_pairs={{0,7},{1,6},{2,5},{3,4},{4,3},{5,2},{6,1},{7,0},{8,15},{9,14},{10,... | collective-permute-start | bytes 995336 | tf_op jit(solution)/shard_map/ppermute | solution.py:508
  9.3 0.0 collective-permute-start.7
  9.3 0.3 collective-permute-start
  10.3 1.9 %collective-permute-done = f32[1,3,6]{2,0,1:T(1,128)S(1)} collective-permute-done((f32[1,3,6]{2,0,1:T(1,128)S(1)}, f32[1,3,6]{2,0,1:T(1,128)S(1)}, u32[]{:S(2)}, u32[]{:S(2)}) %collective-permute-start) | collective-permute-done | bytes 104 | tf_op jit(solution)/shard_map/ppermute | solution.py:514
  12.2 0.1 reshape.26
  12.3 1.8 %collective-permute-start.1 = (f32[1,18]{1,0:T(1,128)S(1)}, f32[1,18]{1,0:T(1,128)S(1)}, u32[]{:S(2)}, u32[]{:S(2)}) collective-permute-start(f32[1,18]{1,0:T(1,128)S(1)} %reshape.26), channel_id=1, source_target_pairs={{0,8},{8,0},{16,24},{24,16},{1,9},{9,1},{17,25},{25,17},{2,10},{10... | collective-permute-start | bytes 224 | tf_op jit(solution)/shard_map/ppermute | solution.py:527
  14.1 0.8 %collective-permute-done.1 = f32[1,18]{1,0:T(1,128)S(1)} collective-permute-done((f32[1,18]{1,0:T(1,128)S(1)}, f32[1,18]{1,0:T(1,128)S(1)}, u32[]{:S(2)}, u32[]{:S(2)}) %collective-permute-start.1) | collective-permute-done | bytes 104 | tf_op jit(solution)/shard_map/ppermute | solution.py:527
  14.9 1.2 %collective-permute-start.2 = (f32[1,18]{1,0:T(1,128)S(1)}, f32[1,18]{1,0:T(1,128)S(1)}, u32[]{:S(2)}, u32[]{:S(2)}) collective-permute-start(f32[1,18]{1,0:T(1,128)S(1)} %add.18), channel_id=1, source_target_pairs={{0,16},{8,24},{16,0},{24,8},{1,17},{9,25},{17,1},{25,9},{2,18},{10... | collective-permute-start | bytes 224 | tf_op jit(solution)/shard_map/ppermute | solution.py:527
  16.1 1.4 %collective-permute-done.2 = f32[1,18]{1,0:T(1,128)S(1)} collective-permute-done((f32[1,18]{1,0:T(1,128)S(1)}, f32[1,18]{1,0:T(1,128)S(1)}, u32[]{:S(2)}, u32[]{:S(2)}) %collective-permute-start.2) | collective-permute-done | bytes 104 | tf_op jit(solution)/shard_map/ppermute | solution.py:527
  17.6 0.1 concatenate.4.refs_5_
  17.7 0.0 copy-start
  17.7 1.6 %copy-done = bf16[256,4096]{1,0:T(8,128)(2,1)S(1)} copy-done((bf16[256,4096]{1,0:T(8,128)(2,1)S(1)}, bf16[256,4096]{1,0:T(8,128)(2,1)}, u32[]{:S(2)}) %copy-start) | copy-done | bytes 2097176
  19.3 4.6 %resample.3 = (bf16[16,10368]{1,0:T(8,128)(2,1)S(1)}, bf16[16,10368]{1,0:T(8,128)(2,1)S(1)}, bf16[16,10368]{1,0:T(8,128)(2,1)S(1)}, bf16[16,10368]{1,0:T(8,128)(...) custom-call(s32[32]{0:T(128)S(1)} %copy-done.1, s32[32]{0:T(128)S(1)} %copy-done.2, ...), custom_call_target="tpu_custom_call" | custom-call | tf_op jit(solution)/shard_map/resample/pallas_call | solution.py:176
  23.9 0.7 collective-permute-start.3
  24.6 0.7 collective-permute-start.4
  25.3 1.4 %collective-permute-start.5 = (bf16[16,10368]{1,0:T(8,128)(2,1)S(1)}, bf16[16,10368]{1,0:T(8,128)(2,1)S(1)}, u32[]{:S(2)}, u32[]{:S(2)}) collective-permute-start(bf16[16,10368]{1,0:T(8,128)(2,1)S(1)} %get-tuple-element.49), channel_id=1, source_target_pairs={{0,3},{1,2},{2,1},{3,0},{4,7},{5,6},{6,5},{7,4},{8,11},{9,10},{10,... | collective-permute-start | bytes 995336 | tf_op jit(solution)/shard_map/ppermute | solution.py:508
  26.6 0.0 collective-permute-done.9.refs_7_
  26.6 4.8 %collective-permute-start.6 = (bf16[16,10368]{1,0:T(8,128)(2,1)S(1)}, bf16[16,10368]{1,0:T(8,128)(2,1)S(1)}, u32[]{:S(2)}, u32[]{:S(2)}) collective-permute-start(bf16[16,10368]{1,0:T(8,128)(2,1)S(1)} %get-tuple-element.50), channel_id=1, source_target_pairs={{0,4},{1,5},{2,6},{3,7},{4,0},{5,1},{6,2},{7,3},{8,12},{9,13},{10,... | collective-permute-start | bytes 995336 | tf_op jit(solution)/shard_map/ppermute | solution.py:508
  31.4 6.0 %collective-permute-done.7.refs_5_ = bf16[16,10368]{1,0:T(8,128)(2,1)S(1)} collective-permute-done((bf16[16,10368]{1,0:T(8,128)(2,1)}, bf16[16,10368]{1,0:T(8,128)(2,1)S(1)}, u32[]{:S(2)}, u32[]{:S(2)}) %collective-permute-start.7) | collective-permute-done | bytes 331808 | tf_op jit(solution)/shard_map/ppermute | solution.py:508
  37.4 2.0 %collective-permute-start.8 = (bf16[16,10368]{1,0:T(8,128)(2,1)S(1)}, bf16[16,10368]{1,0:T(8,128)(2,1)S(1)}, u32[]{:S(2)}, u32[]{:S(2)}) collective-permute-start(bf16[16,10368]{1,0:T(8,128)(2,1)S(1)} %get-tuple-element.51), channel_id=1, source_target_pairs={{0,6},{1,7},{2,4},{3,5},{4,2},{5,3},{6,0},{7,1},{8,14},{9,15},{10,... | collective-permute-start | bytes 995336 | tf_op jit(solution)/shard_map/ppermute | solution.py:508
  39.5 0.8 %tables.1 = (bf16[256,384]{1,0:T(8,128)(2,1)S(1)}, bf16[3,224,256]{2,1,0:T(8,128)(2,1)S(1)}, bf16[96,96]{1,0:T(8,128)(2,1)S(1)}) custom-call(f32[3]{0:T(128)S(1)} %copy-done.5), custom_call_target="tpu_custom_call" | custom-call | tf_op jit(solution)/shard_map/tables/pallas_call | solution.py:226
  40.3 0.0 collective-permute-done.3.refs_1_
  40.3 4.3 %collective-permute-done.4.refs_2_ = bf16[16,10368]{1,0:T(8,128)(2,1)S(1)} collective-permute-done((bf16[16,10368]{1,0:T(8,128)(2,1)S(1)}, bf16[16,10368]{1,0:T(8,128)(2,1)S(1)}, u32[]{:S(2)}, u32[]{:S(2)}) %collective-permute-start.4) | collective-permute-done | bytes 331808 | tf_op jit(solution)/shard_map/ppermute | solution.py:508
  44.6 16.9 %collective-permute-done.5.refs_3_ = bf16[16,10368]{1,0:T(8,128)(2,1)S(1)} collective-permute-done((bf16[16,10368]{1,0:T(8,128)(2,1)S(1)}, bf16[16,10368]{1,0:T(8,128)(2,1)S(1)}, u32[]{:S(2)}, u32[]{:S(2)}) %collective-permute-start.5) | collective-permute-done | bytes 331808 | tf_op jit(solution)/shard_map/ppermute | solution.py:508
  61.5 0.0 collective-permute-done.6.refs_4_
  61.5 2.1 %coadd.1 = (bf16[256,4096]{1,0:T(8,128)(2,1)S(1)}, bf16[16,4096]{1,0:T(8,128)(2,1)}, bf16[16,4096]{1,0:T(8,128)(2,1)S(1)}, f32[1,32]{1,0:T(1,128)}, f32[1,128]{1,0:T(1,128)S(1)}) custom-call(bf16[16,10368]{1,0:T(8,128)(2,1)S(1)} %get-tuple-element.56.refs_0_, bf16[16,10368]{1,0:T(8,128)(2,1)S(1)} %collective-permute-done.3.refs_1_, ...), custom_call_target="tpu_custom_call" | custom-call | tf_op jit(solution)/shard_map/coadd/pallas_call | solution.py:321
  63.6 0.6 collective-permute-start.10
  64.2 7.4 %collective-permute-start.11 = (bf16[16,4096]{1,0:T(8,128)(2,1)S(1)}, bf16[16,4096]{1,0:T(8,128)(2,1)S(1)}, u32[]{:S(2)}, u32[]{:S(2)}) collective-permute-start(bf16[16,4096]{1,0:T(8,128)(2,1)S(1)} %get-tuple-element.67), channel_id=1, source_target_pairs={{2,1},{1,2},{4,3},{3,4},{6,5},{5,6},{8,7},{7,8},{10,9},{9,10},{12,... | collective-permute-start | bytes 393224 | tf_op jit(solution)/shard_map/ppermute | solution.py:541
  71.6 6.3 %match_inner.1.old_ref = bf16[256,4096]{1,0:T(8,128)(2,1)} custom-call(s32[1]{0:T(128)} %bitcast.start_ref, f32[1,128]{1,0:T(1,128)S(1)} %get-tuple-element.64.fit_ref, bf16[256,4096]{1,0:T(8,128)(2,1)S(1)} %get-tuple-element.66.image_ref, bf16[256,384]{1,0:T(8,128)(2,1)S(1)} %get-tuple-element.68.band_ref, bf16[3,224,256]{2,1,0:T(8,128)(2,1)S(1)} %get-tuple-element.70.inner_ref), custom_call_target="tpu_custom_call" | custom-call | tf_op jit(solution)/shard_map/match_inner/pallas_call | solution.py:421
  77.9 0.0 collective-permute-done.11.outward_ref
  77.9 2.2 %match_edges.1 = bf16[256,4096]{1,0:T(8,128)(2,1)} custom-call(s32[1]{0:T(128)} %bitcast.start_ref, f32[1,128]{1,0:T(1,128)S(1)} %get-tuple-element.64.fit_ref, bf16[16,4096]{1,0:T(8,128)(2,1)S(1)} %collective-permute-done.10.inward_ref, bf16[256,4096]{1,0:T(8,128)(2,1)S(1)} %get-tuple-element.66.image_ref, ...), custom_call_target="tpu_custom_call", output_to_operand_aliasing={{}: (7, {})} | custom-call | tf_op jit(solution)/shard_map/match_edges/pallas_call | solution.py:484
  (18 shorter events, 0.1 us)
Async XLA Ops:
  0.6 17.0 %copy-start.2 = (s32[32]{0:T(128)S(1)}, s32[32]{0:T(128)}, u32[]{:S(2)}) copy-start(s32[32]{0:T(128)} %refs_1_.2) | copy-start | bytes 388
  0.6 17.0 %copy-start.1 = (s32[32]{0:T(128)S(1)}, s32[32]{0:T(128)}, u32[]{:S(2)}) copy-start(s32[32]{0:T(128)} %refs_0_.2) | copy-start | bytes 388
  0.7 17.0 %copy-start.3 = (f32[32]{0:T(128)S(1)}, f32[32]{0:T(128)}, u32[]{:S(2)}) copy-start(f32[32]{0:T(128)} %param.11) | copy-start | bytes 388
  0.7 17.0 %copy-start.4 = (f32[32]{0:T(128)S(1)}, f32[32]{0:T(128)}, u32[]{:S(2)}) copy-start(f32[32]{0:T(128)} %param.12) | copy-start | bytes 388
  0.7 8.6 %copy-start.6 = (f32[1,3,6]{2,0,1:T(1,128)S(1)}, f32[1,3,6]{2,0,1:T(1,128)}, u32[]{:S(2)}) copy-start(f32[1,3,6]{2,0,1:T(1,128)} %param.14) | copy-start | bytes 220
  0.7 38.8 %copy-start.5 = (f32[3]{0:T(128)S(1)}, f32[3]{0:T(128)}, u32[]{:S(2)}) copy-start(f32[3]{0:T(128)} %width_ref) | copy-start | bytes 40
  4.2 22.5 %collective-permute-start.9 = (bf16[16,10368]{1,0:T(8,128)(2,1)}, bf16[16,10368]{1,0:T(8,128)(2,1)S(1)}, u32[]{:S(2)}, u32[]{:S(2)}) collective-permute-start(bf16[16,10368]{1,0:T(8,128)(2,1)} %get-tuple-element.37), channel_id=1, source_target_pairs={{0,7},{1,6},{2,5},{3,4},{4,3},{5,2},{6,1},{7,0},{8,15},{9,14},{10,... | collective-permute-start | bytes 995336 | tf_op jit(solution)/shard_map/ppermute | solution.py:508
  9.3 28.1 %collective-permute-start.7 = (bf16[16,10368]{1,0:T(8,128)(2,1)}, bf16[16,10368]{1,0:T(8,128)(2,1)S(1)}, u32[]{:S(2)}, u32[]{:S(2)}) collective-permute-start(bf16[16,10368]{1,0:T(8,128)(2,1)} %get-tuple-element.38), channel_id=1, source_target_pairs={{0,5},{1,4},{2,7},{3,6},{4,1},{5,0},{6,3},{7,2},{8,13},{9,12},{10,... | collective-permute-start | bytes 995336 | tf_op jit(solution)/shard_map/ppermute | solution.py:508
  9.3 2.9 %collective-permute-start = (f32[1,3,6]{2,0,1:T(1,128)S(1)}, f32[1,3,6]{2,0,1:T(1,128)S(1)}, u32[]{:S(2)}, u32[]{:S(2)}) collective-permute-start(f32[1,3,6]{2,0,1:T(1,128)S(1)} %copy-done.6), channel_id=1, source_target_pairs={{0,1},{1,0},{2,3},{3,2},{4,5},{5,4},{6,7},{7,6},{8,9},{9,8},{10,11... | collective-permute-start | bytes 224 | tf_op jit(solution)/shard_map/ppermute | solution.py:514
  12.3 2.6 %collective-permute-start.1 = (f32[1,18]{1,0:T(1,128)S(1)}, f32[1,18]{1,0:T(1,128)S(1)}, u32[]{:S(2)}, u32[]{:S(2)}) collective-permute-start(f32[1,18]{1,0:T(1,128)S(1)} %reshape.26), channel_id=1, source_target_pairs={{0,8},{8,0},{16,24},{24,16},{1,9},{9,1},{17,25},{25,17},{2,10},{10... | collective-permute-start | bytes 224 | tf_op jit(solution)/shard_map/ppermute | solution.py:527
  14.9 2.7 %collective-permute-start.2 = (f32[1,18]{1,0:T(1,128)S(1)}, f32[1,18]{1,0:T(1,128)S(1)}, u32[]{:S(2)}, u32[]{:S(2)}) collective-permute-start(f32[1,18]{1,0:T(1,128)S(1)} %add.18), channel_id=1, source_target_pairs={{0,16},{8,24},{16,0},{24,8},{1,17},{9,25},{17,1},{25,9},{2,18},{10... | collective-permute-start | bytes 224 | tf_op jit(solution)/shard_map/ppermute | solution.py:527
  17.7 1.6 %copy-start = (bf16[256,4096]{1,0:T(8,128)(2,1)S(1)}, bf16[256,4096]{1,0:T(8,128)(2,1)}, u32[]{:S(2)}) copy-start(bf16[256,4096]{1,0:T(8,128)(2,1)} %refs_4_.2) | copy-start | bytes 6291460
  23.9 16.4 %collective-permute-start.3 = (bf16[16,10368]{1,0:T(8,128)(2,1)S(1)}, bf16[16,10368]{1,0:T(8,128)(2,1)S(1)}, u32[]{:S(2)}, u32[]{:S(2)}) collective-permute-start(bf16[16,10368]{1,0:T(8,128)(2,1)S(1)} %get-tuple-element.47), channel_id=1, source_target_pairs={{0,1},{1,0},{2,3},{3,2},{4,5},{5,4},{6,7},{7,6},{8,9},{9,8},{10,11... | collective-permute-start | bytes 995336 | tf_op jit(solution)/shard_map/ppermute | solution.py:508
  24.6 20.0 %collective-permute-start.4 = (bf16[16,10368]{1,0:T(8,128)(2,1)S(1)}, bf16[16,10368]{1,0:T(8,128)(2,1)S(1)}, u32[]{:S(2)}, u32[]{:S(2)}) collective-permute-start(bf16[16,10368]{1,0:T(8,128)(2,1)S(1)} %get-tuple-element.48), channel_id=1, source_target_pairs={{0,2},{1,3},{2,0},{3,1},{4,6},{5,7},{6,4},{7,5},{8,10},{9,11},{10,... | collective-permute-start | bytes 995336 | tf_op jit(solution)/shard_map/ppermute | solution.py:508
  25.3 36.2 %collective-permute-start.5 = (bf16[16,10368]{1,0:T(8,128)(2,1)S(1)}, bf16[16,10368]{1,0:T(8,128)(2,1)S(1)}, u32[]{:S(2)}, u32[]{:S(2)}) collective-permute-start(bf16[16,10368]{1,0:T(8,128)(2,1)S(1)} %get-tuple-element.49), channel_id=1, source_target_pairs={{0,3},{1,2},{2,1},{3,0},{4,7},{5,6},{6,5},{7,4},{8,11},{9,10},{10,... | collective-permute-start | bytes 995336 | tf_op jit(solution)/shard_map/ppermute | solution.py:508
  26.6 34.8 %collective-permute-start.6 = (bf16[16,10368]{1,0:T(8,128)(2,1)S(1)}, bf16[16,10368]{1,0:T(8,128)(2,1)S(1)}, u32[]{:S(2)}, u32[]{:S(2)}) collective-permute-start(bf16[16,10368]{1,0:T(8,128)(2,1)S(1)} %get-tuple-element.50), channel_id=1, source_target_pairs={{0,4},{1,5},{2,6},{3,7},{4,0},{5,1},{6,2},{7,3},{8,12},{9,13},{10,... | collective-permute-start | bytes 995336 | tf_op jit(solution)/shard_map/ppermute | solution.py:508
  37.4 24.1 %collective-permute-start.8 = (bf16[16,10368]{1,0:T(8,128)(2,1)S(1)}, bf16[16,10368]{1,0:T(8,128)(2,1)S(1)}, u32[]{:S(2)}, u32[]{:S(2)}) collective-permute-start(bf16[16,10368]{1,0:T(8,128)(2,1)S(1)} %get-tuple-element.51), channel_id=1, source_target_pairs={{0,6},{1,7},{2,4},{3,5},{4,2},{5,3},{6,0},{7,1},{8,14},{9,15},{10,... | collective-permute-start | bytes 995336 | tf_op jit(solution)/shard_map/ppermute | solution.py:508
  63.6 14.3 %collective-permute-start.10 = (bf16[16,4096]{1,0:T(8,128)(2,1)}, bf16[16,4096]{1,0:T(8,128)(2,1)S(1)}, u32[]{:S(2)}, u32[]{:S(2)}) collective-permute-start(bf16[16,4096]{1,0:T(8,128)(2,1)} %get-tuple-element.65), channel_id=1, source_target_pairs={{0,1},{1,0},{2,3},{3,2},{4,5},{5,4},{6,7},{7,6},{8,9},{9,8},{10,11... | collective-permute-start | bytes 393224 | tf_op jit(solution)/shard_map/ppermute | solution.py:541
  64.2 13.7 %collective-permute-start.11 = (bf16[16,4096]{1,0:T(8,128)(2,1)S(1)}, bf16[16,4096]{1,0:T(8,128)(2,1)S(1)}, u32[]{:S(2)}, u32[]{:S(2)}) collective-permute-start(bf16[16,4096]{1,0:T(8,128)(2,1)S(1)} %get-tuple-element.67), channel_id=1, source_target_pairs={{2,1},{1,2},{4,3},{3,4},{6,5},{5,6},{8,7},{7,8},{10,9},{9,10},{12,... | collective-permute-start | bytes 393224 | tf_op jit(solution)/shard_map/ppermute | solution.py:541
